TPU v7x, 32 devices: a whole 2x2x4 slice. The times are simulated.
32 devices in a mesh: rep: 2 (over y), ch: 4 (over z), row: 2 (over x), sub: 2 (over core).
Axes of the slice: x: 2, y: 2, z: 4, core: 2. Of those that a mesh axis runs over, the one named last changes fastest.
Arguments:
- pair: bfloat16 [1024, 512, 128], P(('rep', 'row', 'sub'), 'ch'), parts along dimension 0, may hold values from -6 to 6
- grad_out: bfloat16 [1024, 512, 128], P(('rep', 'row', 'sub'), 'ch'), parts along dimension 0, may hold values from -6 to 6
- token_mask: int32 [1024], P('rep'), parts along dimension 0, may hold values 0 or 1
- ln_gain: float32 [128], replicated, may hold values from 0.1 to 1.9
- proj_weights: bfloat16 [4, 128, 128], replicated, may hold values from -0.5 to 0.5
- gate_weight: bfloat16 [128, 128], replicated, may hold values from -0.5 to 0.5
- out_weight: bfloat16 [128, 128], replicated, may hold values from -0.5 to 0.5
- out_gain: float32 [128], replicated, may hold values from 0.1 to 1.9
Outputs:
- grad_pair: bfloat16 [1024, 512, 128], P(('rep', 'row', 'sub'), 'ch'), parts along dimension 0
There are 2 independent parts, one for each index of `rep`. A program takes and returns all parts, laid end to end along the dimension named above; an argument that names none is the same for every part. Nothing has to cross between parts.
All inputs are finite; a program needn't handle non-finite values.
Results may differ from a plain program's by a relative error of at most 0.0095.
Values may be sent and summed in bfloat16 or wider, within the bound.
No kernel may reach another device: no remote copies, remote signals or barrier semaphores. Data moves between devices by JAX's collectives and lax.ppermute only.
A program may use at most 256 MiB of HBM per device.

v0:
```python
import jax
import jax.numpy as jnp
from jax import lax
from jax.sharding import PartitionSpec as P

epsilon = 1e-05


def norm_parts(values, axis):
    center = values - jnp.mean(values, axis=axis, keepdims=True)
    scaled = lax.rsqrt(jnp.mean(center * center, axis=axis, keepdims=True) + epsilon)
    return (center * scaled, scaled)


def norm_back(grad_hat, normal, scaled, axis):
    return scaled * (
        grad_hat
        - jnp.mean(grad_hat, axis=axis, keepdims=True)
        - normal * jnp.mean(grad_hat * normal, axis=axis, keepdims=True)
    )


def local(pair, grad_out, token_mask, ln_gain, proj_weights, gate_weight, out_weight, out_gain):
    row_count = pair.shape[0]
    col_count = pair.shape[1]
    mask_float = token_mask.astype(jnp.float32)
    row_mask = lax.dynamic_slice_in_dim(
        mask_float, lax.axis_index(("row", "sub")) * row_count, row_count
    )
    col_mask = lax.dynamic_slice_in_dim(mask_float, lax.axis_index("ch") * col_count, col_count)
    pair_mask = (row_mask[:, None] * col_mask[None, :])[:, None, :]
    pair_hat, pair_scale = norm_parts(pair.astype(jnp.float32), 2)
    normed = (pair_hat * ln_gain).astype(jnp.bfloat16)
    left_value = jnp.einsum(
        "ijd,dc->icj", normed, proj_weights[0], preferred_element_type=jnp.float32
    )
    left_gate = jax.nn.sigmoid(
        jnp.einsum("ijd,dc->icj", normed, proj_weights[1], preferred_element_type=jnp.float32)
    )
    right_value = jnp.einsum(
        "ijd,dc->icj", normed, proj_weights[2], preferred_element_type=jnp.float32
    )
    right_gate = jax.nn.sigmoid(
        jnp.einsum("ijd,dc->icj", normed, proj_weights[3], preferred_element_type=jnp.float32)
    )
    left_rows = (pair_mask * left_gate * left_value).astype(jnp.bfloat16)
    right_rows = (pair_mask * right_gate * right_value).astype(jnp.bfloat16)
    left_chan, right_chan = (
        lax.all_to_all(left_rows, "ch", split_axis=1, concat_axis=2, tiled=True),
        lax.all_to_all(right_rows, "ch", split_axis=1, concat_axis=2, tiled=True),
    )
    combined = jnp.einsum(
        "ick,jck->icj",
        left_chan,
        lax.all_gather(right_chan, ("row", "sub"), axis=0, tiled=True),
        preferred_element_type=jnp.float32,
    )
    comb_rows = lax.all_to_all(
        combined.astype(jnp.bfloat16), "ch", split_axis=2, concat_axis=1, tiled=True
    )
    comb_hat, comb_scale = norm_parts(comb_rows.astype(jnp.float32), 1)
    comb_normed = (comb_hat * out_gain[None, :, None]).astype(jnp.bfloat16)
    out_linear = jnp.einsum(
        "idj,dc->ijc", comb_normed, out_weight, preferred_element_type=jnp.float32
    )
    gate_value = jax.nn.sigmoid(
        jnp.einsum("ijd,dc->ijc", normed, gate_weight, preferred_element_type=jnp.float32)
    )
    grad_gate = grad_out * out_linear
    grad_linear = (grad_out * gate_value).astype(jnp.bfloat16)
    grad_normal = jnp.einsum(
        "ijc,dc->idj", grad_linear, out_weight, preferred_element_type=jnp.float32
    )
    grad_comb = norm_back(grad_normal * out_gain[None, :, None], comb_hat, comb_scale, 1).astype(
        jnp.bfloat16
    )
    grad_chan = lax.all_to_all(grad_comb, "ch", split_axis=1, concat_axis=2, tiled=True)
    columns = grad_chan
    grad_left = jnp.einsum(
        "icj,jck->ick",
        columns,
        lax.all_gather(right_chan, ("row", "sub"), axis=0, tiled=True),
        preferred_element_type=jnp.float32,
    )
    columns = grad_chan
    grad_right = lax.psum_scatter(
        jnp.einsum("icj,ick->jck", columns, left_chan, preferred_element_type=jnp.float32).astype(
            jnp.bfloat16
        ),
        ("row", "sub"),
        scatter_dimension=0,
        tiled=True,
    )
    left_back, right_back = (
        lax.all_to_all(
            grad_left.astype(jnp.bfloat16), "ch", split_axis=2, concat_axis=1, tiled=True
        ),
        lax.all_to_all(grad_right, "ch", split_axis=2, concat_axis=1, tiled=True),
    )
    left_masked = left_back * pair_mask
    right_masked = right_back * pair_mask
    grad_terms = jnp.stack(
        [
            left_masked * left_gate,
            left_masked * left_value * left_gate * (1.0 - left_gate),
            right_masked * right_gate,
            right_masked * right_value * right_gate * (1.0 - right_gate),
        ]
    ).astype(jnp.bfloat16)
    grad_sigm = (grad_gate * gate_value * (1.0 - gate_value)).astype(jnp.bfloat16)
    grad_normed = jnp.einsum(
        "picj,pdc->ijd", grad_terms, proj_weights, preferred_element_type=jnp.float32
    )
    grad_normed = grad_normed + jnp.einsum(
        "ijc,dc->ijd", grad_sigm, gate_weight, preferred_element_type=jnp.float32
    )
    return norm_back(grad_normed * ln_gain, pair_hat, pair_scale, 2).astype(jnp.bfloat16)


def solution(mesh):
    return jax.shard_map(
        local,
        mesh=mesh,
        in_specs=(
            P(("rep", "row", "sub"), "ch", None),
            P(("rep", "row", "sub"), "ch", None),
            P("rep"),
            P(),
            P(),
            P(),
            P(),
            P(),
        ),
        out_specs=P(("rep", "row", "sub"), "ch", None),
        check_vma=False,
    )
```

profile of v0, /device:TPU:15, one launch (start us, length us, event | category | flops | bytes accessed | tf_op | source)
XLA Modules:
  0.0 895.9 jit_solution(4804043278870345207)
XLA Ops:
  38.2 17.5 %fusion.31 = (bf16[128,128,128]{1,2,0:T(8,128)(2,1)}, bf16[128,128,128]{1,2,0:T(8,128)(2,1)}, f32[128,128,128]{2,1,0:T(8,128)}) fusion(f32[128,128,128]{2,1,0:T(8,128)} %add_divide_fusion.1, f32[128,128]{1,0:T(8,128)S(1)} %get-tuple-element.27, f32[128,128,128]{2,1,0:T(8,128)} %fusion.70, f32[128,128,128]{2,1,0:T(8,128)} %add_divide_fusion.2, ...), kind=kOutput, calls=%fused_computation.47 | convolution fusion | flops 559939584 | bytes 46367232 | tf_op jit(solution)/shard_map/ijd,dc->icj/dot_general | solution.py:34
  62.5 95.2 %all_to_all.81 = bf16[128,128,128]{2,0,1:T(8,128)(2,1)S(1)} all-to-all(bf16[128,128,128]{2,0,1:T(8,128)(2,1)} %copy.130), channel_id=1, replica_groups=mesh['rep'=2,'ch'=4,'row'=2,'sub'=2] {'ch'}, dimensions={1} | all-to-all | bytes 8388608 | tf_op jit(solution)/shard_map/all_to_all | solution.py:50
  167.2 98.4 %all_to_all.82 = bf16[128,128,128]{2,0,1:T(8,128)(2,1)} all-to-all(bf16[128,128,128]{2,0,1:T(8,128)(2,1)} %copy.135), channel_id=1, replica_groups=mesh['rep'=2,'ch'=4,'row'=2,'sub'=2] {'ch'}, dimensions={1} | all-to-all | bytes 8388608 | tf_op jit(solution)/shard_map/all_to_all | solution.py:49
  268.1 13.5 %convert_bitcast_fusion.3 = bf16[128,32,512]{0,2,1:T(8,128)(2,1)} fusion(bf16[512,32,512]{2,0,1:T(8,128)(2,1)} %all-gather.2.cloned.1.call-done, bf16[4,32,16,8,128]{4,3,2,1,0:T(8,128)(2,1)} %bitcast.192), kind=kOutput, calls=%fused_computation.81 | convolution fusion | flops 2149580800 | bytes 25165824 | tf_op jit(solution)/shard_map/ick,jck->icj/dot_general | solution.py:52
  293.5 8.3 add_divide_fusion
  301.9 81.1 %all-to-all-done.2 = bf16[128,32,512]{0,1,2:T(8,128)(2,1)} async-done(((bf16[128,32,512]{0,1,2:T(8,128)(2,1)}), bf16[128,32,512]{0,1,2:T(8,128)(2,1)}, u32[]{:S(2)}, u32[]{:S(2)}) %all-to-all-start.2) | async-done | bytes 4194336 | tf_op jit(solution)/shard_map/all_to_all | solution.py:58
  382.9 10.2 %bitcast_convert_fusion = (f32[128,32,4,128]{0,1,3,2:T(8,128)}, f32[128,4,32,128]{0,2,3,1:T(8,128)}) fusion(bf16[128,32,512]{0,1,2:T(8,128)(2,1)} %all-to-all-done.2), kind=kLoop, calls=%fused_computation.87 | loop fusion | flops 2097152 | bytes 20971520 | tf_op jit(solution)/shard_map/convert_element_type | solution.py:61
  393.1 11.4 %copy.144 = f32[128,4,32,128]{3,2,1,0:T(8,128)} copy(f32[128,4,32,128]{0,2,3,1:T(8,128)} %get-tuple-element.16) | data formatting | bytes 16777216 | tf_op jit(solution)/shard_map/convert_element_type | solution.py:61
  412.4 7.8 fusion.30
  420.3 10.3 %bitcast_reduce_fusion = (f32[128,128]{1,0:T(8,128)S(1)}, f32[128,128]{1,0:T(8,128)S(1)}, f32[128,128,128]{1,2,0:T(8,128)S(1)}) fusion(f32[128]{0:T(128)S(1)} %copy-done.8, f32[128,128]{1,0:T(8,128)S(1)} %add_rsqrt_fusion, f32[128,128]{1,0:T(8,128)S(1)} %broadcast_multiply_fusion.5, f32[128,4,32,128]{3,2,1,0:T(8,128)} %copy.144, ...), kind=kOutput, calls=%fused_computation.36 | convolution fusion | flops 555712512 | bytes 29655552 | tf_op jit(solution)/shard_map/ijc,dc->idj/dot_general | solution.py:71
  440.5 96.2 %all_to_all.83 = bf16[128,128,128]{2,0,1:T(8,128)(2,1)S(1)} all-to-all(bf16[128,128,128]{2,0,1:T(8,128)(2,1)S(1)} %copy.145), channel_id=1, replica_groups=mesh['rep'=2,'ch'=4,'row'=2,'sub'=2] {'ch'}, dimensions={1} | all-to-all | bytes 8388608 | tf_op jit(solution)/shard_map/all_to_all | solution.py:77
  549.9 10.9 %convolution_convert_fusion = bf16[32,512,512]{2,1,0:T(8,128)(2,1)} fusion(bf16[128,32,512]{2,0,1:T(8,128)(2,1)} %all_to_all.72, bf16[4,32,16,8,128]{4,3,2,1,0:T(8,128)(2,1)} %bitcast.193), kind=kOutput, calls=%fused_computation.12 | convolution fusion | flops 2155872256 | bytes 25165824 | tf_op jit(solution)/shard_map/icj,ick->jck/dot_general | solution.py:87
  560.7 21.2 %copy.177 = bf16[512,16384]{1,0:T(8,128)(2,1)} copy(bf16[512,16384]{0,1:T(8,128)(2,1)} %bitcast.189) | data formatting | bytes 33554432
  582.0 10.8 %convert_bitcast_fusion.2 = bf16[128,32,512]{0,2,1:T(8,128)(2,1)} fusion(bf16[512,32,512]{2,0,1:T(8,128)(2,1)} %all-gather.2.cloned.1.call-done, bf16[128,32,512]{2,0,1:T(8,128)(2,1)} %all_to_all.72), kind=kOutput, calls=%fused_computation.80 | convolution fusion | flops 2149580800 | bytes 25165824 | tf_op jit(solution)/shard_map/icj,jck->ick/dot_general | solution.py:79
  592.8 8.6 copy.148
  608.2 101.4 %reduce-scatter.4.cloned.1.call-done = bf16[128,16384]{1,0:T(8,128)(2,1)} async-done(((bf16[512,16384]{1,0:T(8,128)(2,1)}), bf16[128,16384]{1,0:T(8,128)(2,1)}) %reduce-scatter.4.cloned.1.call-update) | async-done | bytes 4194320
  728.1 11.5 %fusion.45 = f32[128,128,128]{1,2,0:T(8,128)} fusion(f32[128,128,128]{2,1,0:T(8,128)} %add_divide_fusion, bf16[128,128,128]{2,1,0:T(8,128)(2,1)} %param.9, bf16[128,128,128]{2,1,0:T(8,128)(2,1)} %get-tuple-element.14, bf16[128,128]{1,0:T(8,128)(2,1)S(1)} %copy-done, bf16[128,128]{1,0:T(8,128)(2,1)S(1)} %copy-done.5), kind=kOutput, calls=%fused_computation.73 | convolution fusion | flops 1086324736 | bytes 25231360 | tf_op jit(solution)/shard_map/ijc,dc->ijd/dot_general | solution.py:114
  747.7 10.4 %copy.150 = f32[128,4,32,128]{3,2,1,0:T(8,128)} copy(f32[128,4,32,128]{0,3,1,2:T(8,128)} %convert_bitcast_fusion.1) | data formatting | bytes 16777216 | tf_op jit(solution)/shard_map/convert_element_type | solution.py:100
  758.1 9.0 %copy.151 = f32[128,128,128]{1,2,0:T(8,128)} copy(f32[128,128,128]{2,1,0:T(8,128)} %bitcast.190) | data formatting | bytes 16777216 | tf_op jit(solution)/shard_map/convert_element_type | solution.py:100
  767.1 50.6 %all-to-all-done.5 = bf16[128,32,512]{0,1,2:T(8,128)(2,1)} async-done(((bf16[128,32,512]{0,1,2:T(8,128)(2,1)}), bf16[128,32,512]{0,1,2:T(8,128)(2,1)}, u32[]{:S(2)}, u32[]{:S(2)}) %all-to-all-start.5) | async-done | bytes 4194336 | tf_op jit(solution)/shard_map/all_to_all | solution.py:98
  825.7 10.3 %copy.156 = f32[128,4,32,128]{3,2,1,0:T(8,128)} copy(f32[128,4,32,128]{0,3,1,2:T(8,128)} %convert_bitcast_fusion) | data formatting | bytes 16777216 | tf_op jit(solution)/shard_map/convert_element_type | solution.py:101
  836.1 9.0 %copy.157 = f32[128,128,128]{1,2,0:T(8,128)} copy(f32[128,128,128]{2,1,0:T(8,128)} %bitcast.191) | data formatting | bytes 16777216 | tf_op jit(solution)/shard_map/convert_element_type | solution.py:101
  845.1 22.8 %fusion.43 = (bf16[1,128,128,128]{2,3,1,0:T(8,128)(2,1)S(1)}, bf16[1,128,128,128]{2,3,1,0:T(8,128)(2,1)}, bf16[1,128,128,128]{2,3,1,0:T(8,128)(2,1)}, bf16[1,128,128,128]{2,3,1,0:T(8,128)(2,1)}) fusion(f32[128,128,128]{2,1,0:T(8,128)} %add_divide_fusion.1, f32[128,128,128]{1,2,0:T(8,128)} %copy.151, f32[128,128]{1,0:T(8,128)S(1)} %copy-done.4, ...), kind=kLoop, calls=%fused_computation.71 | loop fusion | flops 33554432 | bytes 67174400 | tf_op jit(solution)/shard_map/stack | solution.py:102
  868.0 10.5 %fusion.84 = (f32[128,128]{1,0:T(8,128)S(1)}, f32[128,128]{1,0:T(8,128)S(1)}, f32[128,128,128]{1,2,0:T(8,128)S(1)}) fusion(f32[128,128]{1,0:T(8,128)S(1)} %get-tuple-element.26, f32[128,128]{1,0:T(8,128)S(1)} %broadcast_multiply_fusion.6, bf16[128,128,128]{1,2,0:T(8,128)(2,1)S(1)} %copy-done.2, f32[128]{0:T(128)S(1)} %copy-done.9, ...), kind=kOutput, calls=%fused_computation.114 | convolution fusion | flops 2189393920 | bytes 38142464 | tf_op jit(solution)/shard_map/picj,pdc->ijd/dot_general | solution.py:111
  (65 shorter events, 145.1 us)
Async XLA Ops:
  6.5 413.8 %copy-start = (bf16[128,128]{1,0:T(8,128)(2,1)S(1)}, bf16[128,128]{1,0:T(8,128)(2,1)}, u32[]{:S(2)}) copy-start(bf16[128,128]{1,0:T(8,128)(2,1)} %param.14) | copy-start | bytes 98308
  6.5 261.6 %all-gather.2.cloned.1.call-start = ((), (), s32[]{:S(2)}) async-start(), calls=%async_computation.7 | async-start | bytes 20971520 | tf_op jit(solution)/shard_map/all_gather | solution.py:82
  7.2 14.1 %copy-start.6 = (bf16[4,128,128]{2,1,0:T(8,128)(2,1)S(1)}, bf16[4,128,128]{2,1,0:T(8,128)(2,1)}, u32[]{:S(2)}) copy-start(bf16[4,128,128]{2,1,0:T(8,128)(2,1)} %param.12) | copy-start | bytes 393220
  7.2 14.1 %copy-start.9 = (f32[128]{0:T(128)S(1)}, f32[128]{0:T(128)}, u32[]{:S(2)}) copy-start(f32[128]{0:T(128)} %param.11) | copy-start | bytes 1540
  21.2 7.2 copy-start.1
  21.3 16.9 %copy-start.3 = (f32[128,128]{1,0:T(8,128)}, f32[128,128]{1,0:T(8,128)S(1)}, u32[]{:S(2)}) copy-start(f32[128,128]{1,0:T(8,128)S(1)} %get-tuple-element.27) | copy-start | bytes 196612
  281.6 12.0 %copy-start.5 = (bf16[128,128]{1,0:T(8,128)(2,1)S(1)}, bf16[128,128]{1,0:T(8,128)(2,1)}, u32[]{:S(2)}) copy-start(bf16[128,128]{1,0:T(8,128)(2,1)} %param.13) | copy-start | bytes 98308
  288.4 94.5 %all-to-all-start.2 = ((bf16[128,32,512]{0,1,2:T(8,128)(2,1)}), bf16[128,32,512]{0,1,2:T(8,128)(2,1)}, u32[]{:S(2)}, u32[]{:S(2)}) async-start(bf16[128,32,512]{0,1,2:T(8,128)(2,1)} %copy.138), calls=%async_computation.2 | async-start | bytes 8388608 | tf_op jit(solution)/shard_map/all_to_all | solution.py:58
  293.5 416.1 %reduce-scatter.4.cloned.1.call-start = ((), (), s32[]{:S(2)}) async-start(), calls=%async_computation.8 | async-start | bytes 20971520
  404.5 15.8 %copy-start.8 = (f32[128]{0:T(128)S(1)}, f32[128]{0:T(128)}, u32[]{:S(2)}) copy-start(f32[128]{0:T(128)} %param.15) | copy-start | bytes 1540
  601.3 121.5 %all-to-all-start.4 = ((bf16[128,32,512]{0,1,2:T(8,128)(2,1)}), bf16[128,32,512]{0,1,2:T(8,128)(2,1)}, u32[]{:S(2)}, u32[]{:S(2)}) async-start(bf16[128,32,512]{0,1,2:T(8,128)(2,1)} %copy.148), calls=%async_computation.4 | async-start | bytes 8388608 | tf_op jit(solution)/shard_map/all_to_all | solution.py:95
  722.8 94.9 %all-to-all-start.5 = ((bf16[128,32,512]{0,1,2:T(8,128)(2,1)}), bf16[128,32,512]{0,1,2:T(8,128)(2,1)}, u32[]{:S(2)}, u32[]{:S(2)}) async-start(bf16[128,32,512]{0,1,2:T(8,128)(2,1)} %copy.154), calls=%async_computation.5 | async-start | bytes 8388608 | tf_op jit(solution)/shard_map/all_to_all | solution.py:98
  836.1 9.0 %copy-start.4 = (f32[128,128]{1,0:T(8,128)S(1)}, f32[128,128]{1,0:T(8,128)}, u32[]{:S(2)}) copy-start(f32[128,128]{1,0:T(8,128)} %copy-done.3) | copy-start | bytes 196612
  845.1 22.8 %copy-start.2 = (bf16[128,128,128]{1,2,0:T(8,128)(2,1)S(1)}, bf16[128,128,128]{1,2,0:T(8,128)(2,1)}, u32[]{:S(2)}) copy-start(bf16[128,128,128]{1,2,0:T(8,128)(2,1)} %copy.127) | copy-start | bytes 12582916
  845.1 22.8 %copy-start.7 = (bf16[4,128,128]{2,1,0:T(8,128)(2,1)S(1)}, bf16[4,128,128]{2,1,0:T(8,128)(2,1)}, u32[]{:S(2)}) copy-start(bf16[4,128,128]{2,1,0:T(8,128)(2,1)} %param.12) | copy-start | bytes 393220
Sparse Core Ops, SparseCore 0:
  160.6 107.5 all-gather.1
  582.1 127.4 reduce-scatter.3
where the time goes:
time: 914 us; the launch traced here: 896 us
  blocking collectives  290 us (32%)
  waiting for transfers between devices  236 us (26%)
  local copies, waits for them, and re-layouts  153 us (17%)
  matrix products  110 us (12%)
  other arithmetic  76.4 us (8%)
  starting transfers between devices  17.3 us (2%)
  between operations  14 us (2%)
    unnamed x3, waiting for transfers between devices  101 us
    all_to_all x1, blocking collectives, local(): lax.all_to_all(left_rows, 'ch', split_axis=1, concat_axis=2, tiled=True)  98.4 us
    all_to_all x1, blocking collectives, local(): lax.all_to_all(grad_comb, 'ch', split_axis=1, concat_axis=2, tiled=True)  96.2 us
    all_to_all x1, blocking collectives, local(): lax.all_to_all(right_rows, 'ch', split_axis=1, concat_axis=2, tiled=True)  95.2 us
    all_to_all x1, waiting for transfers between devices, local(): lax.all_to_all(combined.astype(jnp.bfloat16), 'ch', split_axis=2, concat_...  81.1 us
    all_to_all x1, waiting for transfers between devices, local(): lax.all_to_all(grad_right, 'ch', split_axis=2, concat_axis=1, tiled=True)  50.6 us
    unnamed x23, local copies, waits for them, and re-layouts  34 us
    another operation x1, other arithmetic, local(): jnp.stack([left_masked * left_gate, left_masked * left_value * left_gate...  22.8 us
  transfers between devices with their start and end apart: 5, of which 4 were waited for; matrix products, arithmetic and copies ran while one was open for 10% of the time, Pallas kernels for 0%

commit v1 on v0

v1 whole, which is shorter than its diff:
```python
import functools

import jax
import jax.numpy as jnp
from jax import lax
from jax.experimental import pallas as pl
from jax.experimental.pallas import tpu as pltpu
from jax.sharding import PartitionSpec as P

epsilon = 1e-05
F32 = jnp.float32
BF16 = jnp.bfloat16
VMEM_LIMIT = 48 * 1024 * 1024


def dot(a, b, ca, cb):
    return lax.dot_general(a, b, (((ca,), (cb,)), ((), ())), preferred_element_type=F32)


def norm_rows(pair_block, gain):
    x = pair_block.astype(F32)
    center = x - jnp.mean(x, axis=1, keepdims=True)
    scaled = lax.rsqrt(jnp.mean(center * center, axis=1, keepdims=True) + epsilon)
    hat = center * scaled
    return hat, scaled, (hat * gain).astype(BF16)


def rows_of(ref, first, count):
    block = ref[first:first + count]
    return block.reshape(count * block.shape[1], block.shape[2])


def load_chan(ref, first, count):
    parts = [ref[:, first + t] for t in range(count)]
    parts = [p.astype(F32).reshape(p.shape[0] * p.shape[1], p.shape[2]) for p in parts]
    return parts[0] if count == 1 else jnp.concatenate(parts, axis=1)


def store_chan(ref, first, count, value):
    groups, _, chans, cols = ref.shape
    for t in range(count):
        part = value[:, t * cols:(t + 1) * cols] if count > 1 else value
        ref[:, first + t] = part.reshape(groups, chans, cols).astype(BF16)


def project_kernel(step, pair_ref, mask_ref, gain_ref, weight_ref, out_ref):
    rows, cols, chans = pair_ref.shape
    for first in range(0, rows, step):
        _, _, normed = norm_rows(rows_of(pair_ref, first, step), gain_ref[...])
        both = dot(weight_ref[...], normed, 1, 1)
        mask = mask_ref[0, :, first * cols:(first + step) * cols]
        store_chan(out_ref, first, step, mask * jax.nn.sigmoid(both[chans:]) * both[:chans])


def middle_kernel(
    step, pair_ref, gout_ref, comb_ref, gain_ref, gate_t_ref, out_w_ref, out_t_ref, out_gain_ref, eye_ref,
    gcomb_ref, sigm_ref,
):
    rows, cols, chans = pair_ref.shape
    out_gain = out_gain_ref[...]
    for first in range(0, rows, step):
        _, _, normed = norm_rows(rows_of(pair_ref, first, step), gain_ref[...])
        gate = jax.nn.sigmoid(dot(gate_t_ref[...], normed, 1, 1))
        gout = dot(eye_ref[...], rows_of(gout_ref, first, step), 1, 1)
        comb = load_chan(comb_ref, first, step)
        center = comb - jnp.mean(comb, axis=0, keepdims=True)
        scaled = lax.rsqrt(jnp.mean(center * center, axis=0, keepdims=True) + epsilon)
        hat = center * scaled
        lin = dot(out_t_ref[...], (hat * out_gain).astype(BF16), 1, 0)
        grad_lin = (gout * gate).astype(BF16)
        h = dot(out_w_ref[...], grad_lin, 1, 0) * out_gain
        grad = scaled * (
            h - jnp.mean(h, axis=0, keepdims=True) - hat * jnp.mean(h * hat, axis=0, keepdims=True)
        )
        store_chan(gcomb_ref, first, step, grad)
        sigm = (gout * lin * gate * (1.0 - gate)).astype(BF16)
        for t in range(step):
            sigm_ref[first + t] = sigm[:, t * cols:(t + 1) * cols] if step > 1 else sigm


def last_kernel(
    step, pair_ref, left_ref, right_ref, sigm_ref, mask_ref, gain_ref, weight_ref, held_ref, out_ref
):
    del held_ref
    rows, cols, chans = pair_ref.shape
    gain = gain_ref[...]
    weight = weight_ref[...]
    for first in range(0, rows, step):
        hat, scaled, normed = norm_rows(rows_of(pair_ref, first, step), gain)
        mask = mask_ref[0, :, first * cols:(first + step) * cols]
        proj = dot(weight[:4 * chans], normed, 1, 1)
        terms = []
        for which, ref in enumerate((left_ref, right_ref)):
            grad = load_chan(ref, first, step) * mask
            value = proj[2 * which * chans:(2 * which + 1) * chans]
            gate = jax.nn.sigmoid(proj[(2 * which + 1) * chans:(2 * which + 2) * chans])
            through = grad * gate
            terms += [through.astype(BF16), (through * value * (1.0 - gate)).astype(BF16)]
        parts = [sigm_ref[first + t] for t in range(step)]
        terms.append(parts[0] if step == 1 else jnp.concatenate(parts, axis=1))
        g = dot(jnp.concatenate(terms, axis=0), weight, 0, 0) * gain
        grad_in = scaled * (
            g - jnp.mean(g, axis=1, keepdims=True) - hat * jnp.mean(g * hat, axis=1, keepdims=True)
        )
        out_ref[first:first + step] = grad_in.reshape(step, cols, chans).astype(BF16)


def local(group, chunks, pair, grad_out, token_mask, ln_gain, proj_weights, gate_weight, out_weight, out_gain):
    rows, cols, chans = pair.shape
    peers = lax.axis_size(group)
    row_blocks = lax.axis_size(group[1:])
    col_blocks = peers // row_blocks
    own = chans // peers
    tokens = rows * row_blocks
    part_rows = rows // chunks
    block = min(8, part_rows)
    blocks = part_rows // block
    step = 4 if cols % 128 == 0 and block % 4 == 0 else 1

    mask_float = token_mask.astype(F32)
    row_mask = lax.dynamic_slice_in_dim(mask_float, lax.axis_index(group[1:]) * rows, rows)
    col_mask = lax.dynamic_slice_in_dim(mask_float, lax.axis_index(group[0]) * cols, cols)
    mask = (row_mask[:, None] * col_mask[None, :]).reshape(rows // block, 1, block * cols)
    gain = ln_gain.reshape(1, chans)
    proj_t = jnp.swapaxes(proj_weights, 1, 2)
    left_w = proj_t[:2].reshape(2 * chans, chans)
    right_w = proj_t[2:].reshape(2 * chans, chans)
    gate_t = gate_weight.T
    all_w = jnp.concatenate([left_w, right_w, gate_t], axis=0)
    eye = jnp.eye(chans, dtype=BF16)

    params = pltpu.CompilerParams(vmem_limit_bytes=VMEM_LIMIT)

    def cost(flops_per_pair, arrays, pairs):
        return pl.CostEstimate(
            flops=flops_per_pair * pairs, bytes_accessed=arrays * pairs * chans * 2, transcendentals=chans * pairs
        )

    def row_spec(first):
        return pl.BlockSpec((block, cols, chans), lambda s: (first + s, 0, 0))

    def mask_spec(first):
        return pl.BlockSpec((1, 1, block * cols), lambda s: (first + s, 0, 0))

    def whole(array):
        return pl.BlockSpec(array.shape, lambda s: (0,) * array.ndim)

    chan_spec = pl.BlockSpec((peers, block, own, cols), lambda s: (0, s, 0, 0))
    sigm_spec = pl.BlockSpec((block, chans, cols), lambda s: (s, 0, 0))

    def project(weight, first, count):
        return pl.pallas_call(
            functools.partial(project_kernel, step),
            grid=(count,),
            in_specs=[row_spec(first), mask_spec(first), whole(gain), whole(weight)],
            out_specs=chan_spec,
            out_shape=jax.ShapeDtypeStruct((peers, count * block, own, cols), BF16),
            compiler_params=params,
            cost_estimate=cost(4 * chans * chans, 2, count * block * cols),
        )(pair, mask, gain, weight)

    def exchange(array):
        return lax.all_to_all(array, group, split_axis=0, concat_axis=0, tiled=True)

    def by_channel(array):
        count = array.shape[1]
        array = array.reshape(col_blocks, row_blocks, count, own, cols)
        return jnp.transpose(array, (3, 1, 2, 0, 4)).reshape(own, row_blocks * count, tokens)

    def by_owner(array):
        count = array.shape[1] // row_blocks
        array = array.astype(BF16).reshape(own, row_blocks, count, col_blocks, cols)
        return jnp.transpose(array, (3, 1, 2, 0, 4)).reshape(peers, count, own, cols)

    def batch_dot(a, b, ca, cb):
        return lax.dot_general(a, b, (((ca,), (cb,)), ((0,), (0,))), preferred_element_type=F32)

    def middle(comb, first):
        out_t = out_weight.T
        gain_col = out_gain.reshape(chans, 1)
        return pl.pallas_call(
            functools.partial(middle_kernel, step),
            grid=(blocks,),
            in_specs=[row_spec(first), row_spec(first), chan_spec, whole(gain), whole(gate_t), whole(out_weight),
                      whole(out_t), whole(gain_col), whole(eye)],
            out_specs=[chan_spec, sigm_spec],
            out_shape=[
                jax.ShapeDtypeStruct((peers, part_rows, own, cols), BF16),
                jax.ShapeDtypeStruct((part_rows, chans, cols), BF16),
            ],
            compiler_params=params,
            cost_estimate=cost(8 * chans * chans, 5, part_rows * cols),
        )(pair, grad_out, comb, gain, gate_t, out_weight, out_t, gain_col, eye)

    def last(left_grad, right_grad, sigm, first, held):
        return pl.pallas_call(
            functools.partial(last_kernel, step),
            grid=(blocks,),
            in_specs=[row_spec(first), chan_spec, chan_spec, sigm_spec, mask_spec(first), whole(gain), whole(all_w),
                      pl.BlockSpec(memory_space=pl.ANY)],
            out_specs=row_spec(first),
            out_shape=jax.ShapeDtypeStruct((rows, cols, chans), BF16),
            input_output_aliases={7: 0},
            compiler_params=params,
            cost_estimate=cost(18 * chans * chans, 5, part_rows * cols),
        )(pair, left_grad, right_grad, sigm, mask, gain, all_w, held)

    right = by_channel(exchange(project(right_w, 0, rows // block)))
    firsts = [part * blocks for part in range(chunks)]
    lefts = [by_channel(exchange(project(left_w, first, blocks))) for first in firsts]
    sigms, left_grads, grad_parts = [], [], []
    for first, left in zip(firsts, lefts):
        comb = exchange(by_owner(batch_dot(left, right, 2, 2)))
        grad_comb, sigm = middle(comb, first)
        sigms.append(sigm)
        grad_comb = by_channel(exchange(grad_comb))
        left_grads.append(exchange(by_owner(batch_dot(grad_comb, right, 2, 1))))
        grad_parts.append(batch_dot(grad_comb, left, 1, 1))
    grad_right = by_owner(functools.reduce(jnp.add, grad_parts))
    right_grads = [exchange(grad_right[:, p * part_rows:(p + 1) * part_rows]) for p in range(chunks)]
    out = jnp.zeros((rows, cols, chans), BF16)
    for first, left_grad, right_grad, sigm in zip(firsts, left_grads, right_grads, sigms):
        out = last(left_grad, right_grad, sigm, first, out)
    return out


def solution(mesh):
    spread = P(("rep", "row", "sub"), "ch", None)
    return jax.shard_map(
        functools.partial(local, ("ch", "row", "sub"), 2),
        mesh=mesh,
        in_specs=(spread, spread, P("rep"), P(), P(), P(), P(), P()),
        out_specs=spread,
        check_vma=False,
    )
```

time: 914 us -> 662 us (0.72)
  blocking collectives: 290 us -> 52.3 us
  waiting for transfers between devices: 236 us -> 338 us
  matrix products: 110 us -> 28.3 us
  Pallas kernels: 0 us -> 81.1 us
  other arithmetic: 76.4 us -> 0.77 us
  local copies, waits for them, and re-layouts: 153 us -> 98.3 us
  starting transfers between devices: 17.3 us -> 51.8 us
  between operations: 14 us -> 0.69 us
    all_to_all x3 -> x1, blocking collectives: 290 us -> 52.3 us  [exchange(): return lax.all_to_all(array, group, split_axis=0, concat_axis=0, tiled=True)]
    all_to_all x3 -> x10, waiting for transfers between devices: 132 us -> 338 us  [exchange(): return lax.all_to_all(array, group, split_axis=0, concat_axis=0, tiled=True)]
    unnamed x3 -> x0, waiting for transfers between devices: 101 us -> none
    convert_element_type x11 -> x0, local copies, waits for them, and re-layouts: 88 us -> none  [the longest x2 19.4 us: local(): right_masked = right_back * pair_mask]
    dot_general x11 -> x6, matrix products: 110 us -> 28.3 us  [batch_dot(): lax.dot_general(a, b, (((ca,), (cb,)), ((0,), (0,))), preferred_element_t...]
    pallas_call x0 -> x7, Pallas kernels: none -> 81.1 us  [the longest x3 30.1 us: project(): pl.pallas_call(functools.partial(project_kernel, step), grid=(count,), in...]
    reshape x0 -> x17, local copies, waits for them, and re-layouts: none -> 64.3 us  [the longest x10 41.7 us: by_owner(): array = array.astype(BF16).reshape(own, row_blocks, count, col_blocks, cols)]
    all_to_all x3 -> x10, starting transfers between devices: 17.3 us -> 51.8 us  [exchange(): return lax.all_to_all(array, group, split_axis=0, concat_axis=0, tiled=True)]
  transfers between devices with their start and end apart: 5 -> 10, of which waited for: 4 -> 10; matrix products, arithmetic and copies ran while one was open for 10% -> 18% of each run, Pallas kernels for 0% -> 9%
where the time goes in v1:
time: 662 us; the launch traced here: 651 us
  waiting for transfers between devices  338 us (51%)
  local copies, waits for them, and re-layouts  98.3 us (15%)
  Pallas kernels  81.1 us (12%)
  blocking collectives  52.3 us (8%)
  starting transfers between devices  51.8 us (8%)
  matrix products  28.3 us (4%)
    all_to_all x10, waiting for transfers between devices, exchange(): return lax.all_to_all(array, group, split_axis=0, concat_axis=0, tiled=True)  338 us
    all_to_all x1, blocking collectives, exchange(): return lax.all_to_all(array, group, split_axis=0, concat_axis=0, tiled=True)  52.3 us
    all_to_all x10, starting transfers between devices, exchange(): return lax.all_to_all(array, group, split_axis=0, concat_axis=0, tiled=True)  51.8 us
    reshape x10, local copies, waits for them, and re-layouts, by_owner(): array = array.astype(BF16).reshape(own, row_blocks, count, col_blocks, cols)  41.7 us
    pallas_call x3, Pallas kernels, project(): pl.pallas_call(functools.partial(project_kernel, step), grid=(count,), in...  30.1 us
    pallas_call x2, Pallas kernels, last(): pl.pallas_call(functools.partial(last_kernel, step), grid=(blocks,), in_s...  28.9 us
    dot_general x6, matrix products, batch_dot(): lax.dot_general(a, b, (((ca,), (cb,)), ((0,), (0,))), preferred_element_t...  28.3 us
    pallas_call x2, Pallas kernels, middle(): pl.pallas_call(functools.partial(middle_kernel, step), grid=(blocks,), in...  22 us
  transfers between devices with their start and end apart: 10, of which 10 were waited for; matrix products, arithmetic and copies ran while one was open for 18% of the time, Pallas kernels for 9%

profile of v1, /device:TPU:15, one launch (start us, length us, event | category | flops | bytes accessed | tf_op | source)
XLA Modules:
  0.0 650.7 jit_solution(6004889019019299314)
XLA Ops:
  2.7 8.2 %shard_map.85 = bf16[16,64,8,128]{3,2,1,0:T(8,128)(2,1)} custom-call(bf16[128,128,128]{2,1,0:T(8,128)(2,1)} %pair_ref.13, f32[16,1,1024]{2,1,0:T(1,128)S(1)} %broadcast_multiply_fusion.mask_ref, f32[1,128]{1,0:T(1,128)S(1)} %bitcast.63, bf16[256,128]{1,0:T(8,128)(2,1)S(1)} %bitcast.53), custom_call_target="tpu_custom_call" | custom-call | flops 536870912 | bytes 4194304 | tf_op jit(solution)/shard_map/pallas_call | solution.py:152
  10.9 6.6 %all-to-all-start.5 = ((bf16[16,64,8,128]{3,2,1,0:T(8,128)(2,1)}), bf16[16,64,8,128]{3,2,1,0:T(8,128)(2,1)S(1)}, u32[]{:S(2)}, u32[]{:S(2)}) async-start(bf16[16,64,8,128]{3,2,1,0:T(8,128)(2,1)} %shard_map.85), calls=%async_computation.5 | async-start | bytes 4194304 | tf_op jit(solution)/shard_map/all_to_all | solution.py:163
  17.5 13.7 %shard_map.83 = bf16[16,128,8,128]{3,2,1,0:T(8,128)(2,1)S(1)} custom-call(bf16[128,128,128]{2,1,0:T(8,128)(2,1)} %pair_ref.13, f32[16,1,1024]{2,1,0:T(1,128)S(1)} %broadcast_multiply_fusion.mask_ref, f32[1,128]{1,0:T(1,128)S(1)} %bitcast.64, bf16[256,128]{1,0:T(8,128)(2,1)S(1)} %bitcast.56), custom_call_target="tpu_custom_call" | custom-call | flops 1073741824 | bytes 8388608 | tf_op jit(solution)/shard_map/pallas_call | solution.py:152
  33.3 31.5 %all-to-all-done.5 = bf16[16,64,8,128]{3,2,1,0:T(8,128)(2,1)S(1)} async-done(((bf16[16,64,8,128]{3,2,1,0:T(8,128)(2,1)}), bf16[16,64,8,128]{3,2,1,0:T(8,128)(2,1)S(1)}, u32[]{:S(2)}, u32[]{:S(2)}) %all-to-all-start.5) | async-done | bytes 2097184 | tf_op jit(solution)/shard_map/all_to_all | solution.py:163
  69.7 8.2 %shard_map.82 = bf16[16,64,8,128]{3,2,1,0:T(8,128)(2,1)} custom-call(bf16[128,128,128]{2,1,0:T(8,128)(2,1)} %pair_ref.13, f32[16,1,1024]{2,1,0:T(1,128)S(1)} %broadcast_multiply_fusion.mask_ref, f32[1,128]{1,0:T(1,128)S(1)} %bitcast.65, bf16[256,128]{1,0:T(8,128)(2,1)S(1)} %bitcast.54), custom_call_target="tpu_custom_call" | custom-call | flops 536870912 | bytes 4194304 | tf_op jit(solution)/shard_map/pallas_call | solution.py:152
  77.9 84.3 %all-to-all-done.1 = bf16[16,128,8,128]{3,2,1,0:T(8,128)(2,1)} async-done(((bf16[16,128,8,128]{3,2,1,0:T(8,128)(2,1)}), bf16[16,128,8,128]{3,2,1,0:T(8,128)(2,1)}, u32[]{:S(2)}, u32[]{:S(2)}) %all-to-all-start.1) | async-done | bytes 4194336 | tf_op jit(solution)/shard_map/all_to_all | solution.py:163
  172.8 8.2 %copy.32 = bf16[8,4,128,4,128]{4,3,2,1,0:T(4,128)(2,1)} copy(bf16[8,4,128,4,128]{4,0,2,1,3:T(8,128)(2,1)} %bitcast.9) | data formatting | bytes 8388608 | tf_op jit(solution)/shard_map/transpose | solution.py:168
  181.0 7.2 %reshape.121 = bf16[8,512,512]{2,1,0:T(8,128)(2,1)} reshape(bf16[8,4,128,4,128]{4,3,2,1,0:T(4,128)(2,1)} %copy.32) | data formatting | bytes 8388608 | tf_op jit(solution)/shard_map/reshape | solution.py:168
  198.2 16.4 %all-to-all-done = bf16[16,64,8,128]{3,2,1,0:T(8,128)(2,1)} async-done(((bf16[16,64,8,128]{3,2,1,0:T(8,128)(2,1)}), bf16[16,64,8,128]{3,2,1,0:T(8,128)(2,1)}, u32[]{:S(2)}, u32[]{:S(2)}) %all-to-all-start) | async-done | bytes 2097184 | tf_op jit(solution)/shard_map/all_to_all | solution.py:163
  227.2 5.6 convolution_convert_fusion.3
  241.0 26.2 %all-to-all-done.6.comb_ref = bf16[16,64,8,128]{3,2,1,0:T(8,128)(2,1)} async-done(((bf16[16,64,8,128]{3,2,1,0:T(8,128)(2,1)}), bf16[16,64,8,128]{3,2,1,0:T(8,128)(2,1)}, u32[]{:S(2)}, u32[]{:S(2)}) %all-to-all-start.6) | async-done | bytes 2097184 | tf_op jit(solution)/shard_map/all_to_all | solution.py:163
  272.7 11.0 %shard_map.86 = (bf16[16,64,8,128]{3,2,1,0:T(8,128)(2,1)}, bf16[64,128,128]{2,1,0:T(8,128)(2,1)S(1)}) custom-call(bf16[128,128,128]{2,1,0:T(8,128)(2,1)} %pair_ref.13, bf16[128,128,128]{2,1,0:T(8,128)(2,1)} %gout_ref.3, bf16[16,64,8,128]{3,2,1,0:T(8,128)(2,1)} %all-to-all-done.6.comb_ref, f32[1,128]{1,0:T(1,128)S(1)} %bitcast.66, ...), custom_call_target="tpu_custom_call" | custom-call | flops 1073741824 | bytes 10485760 | tf_op jit(solution)/shard_map/pallas_call | solution.py:181
  285.1 34.6 %all-to-all-done.2.comb_ref = bf16[16,64,8,128]{3,2,1,0:T(8,128)(2,1)S(1)} async-done(((bf16[16,64,8,128]{3,2,1,0:T(8,128)(2,1)}), bf16[16,64,8,128]{3,2,1,0:T(8,128)(2,1)S(1)}, u32[]{:S(2)}, u32[]{:S(2)}) %all-to-all-start.2) | async-done | bytes 2097184 | tf_op jit(solution)/shard_map/all_to_all | solution.py:163
  325.9 11.0 %shard_map.84 = (bf16[16,64,8,128]{3,2,1,0:T(8,128)(2,1)}, bf16[64,128,128]{2,1,0:T(8,128)(2,1)S(1)}) custom-call(bf16[128,128,128]{2,1,0:T(8,128)(2,1)} %pair_ref.13, bf16[128,128,128]{2,1,0:T(8,128)(2,1)} %gout_ref.3, bf16[16,64,8,128]{3,2,1,0:T(8,128)(2,1)} %copy-done.12, f32[1,128]{1,0:T(1,128)S(1)} %bitcast.67, bf16[128,128]{1,0:T(8,128)(2,1)S(1)} %bitcast.59, ...), custom_call_target="tpu_custom_call" | custom-call | flops 1073741824 | bytes 10485760 | tf_op jit(solution)/shard_map/pallas_call | solution.py:181
  338.3 35.0 %all-to-all-done.7 = bf16[16,64,8,128]{3,2,1,0:T(8,128)(2,1)S(1)} async-done(((bf16[16,64,8,128]{3,2,1,0:T(8,128)(2,1)}), bf16[16,64,8,128]{3,2,1,0:T(8,128)(2,1)S(1)}, u32[]{:S(2)}, u32[]{:S(2)}) %all-to-all-start.7) | async-done | bytes 2097184 | tf_op jit(solution)/shard_map/all_to_all | solution.py:163
  384.0 5.5 convolution_convert_fusion
  397.7 28.0 %all-to-all-done.3 = bf16[16,64,8,128]{3,2,1,0:T(8,128)(2,1)} async-done(((bf16[16,64,8,128]{3,2,1,0:T(8,128)(2,1)}), bf16[16,64,8,128]{3,2,1,0:T(8,128)(2,1)}, u32[]{:S(2)}, u32[]{:S(2)}) %all-to-all-start.3) | async-done | bytes 2097184 | tf_op jit(solution)/shard_map/all_to_all | solution.py:163
  453.0 25.1 %all-to-all-done.9.left_ref = bf16[16,64,8,128]{3,2,1,0:T(8,128)(2,1)S(1)} async-done(((bf16[16,64,8,128]{3,2,1,0:T(8,128)(2,1)}), bf16[16,64,8,128]{3,2,1,0:T(8,128)(2,1)S(1)}, u32[]{:S(2)}, u32[]{:S(2)}) %all-to-all-start.9) | async-done | bytes 2097184 | tf_op jit(solution)/shard_map/all_to_all | solution.py:163
  490.1 6.9 %reshape.135 = bf16[8,4,128,4,128]{4,3,2,1,0:T(4,128)(2,1)} reshape(bf16[8,512,512]{2,1,0:T(8,128)(2,1)} %add_convert_fusion) | data formatting | bytes 8388608 | tf_op jit(solution)/shard_map/reshape | solution.py:172
  504.1 26.4 %all-to-all-done.4.left_ref = bf16[16,64,8,128]{3,2,1,0:T(8,128)(2,1)} async-done(((bf16[16,64,8,128]{3,2,1,0:T(8,128)(2,1)}), bf16[16,64,8,128]{3,2,1,0:T(8,128)(2,1)}, u32[]{:S(2)}, u32[]{:S(2)}) %all-to-all-start.4) | async-done | bytes 2097184 | tf_op jit(solution)/shard_map/all_to_all | solution.py:163
  530.5 52.3 %all_to_all.55.right_ref = bf16[16,64,8,128]{3,2,1,0:T(8,128)(2,1)} all-to-all(bf16[16,64,8,128]{3,2,1,0:T(8,128)(2,1)} %get-tuple-element.13), channel_id=1, replica_groups=mesh['rep'=2,'ch'=4,'row'=2,'sub'=2] {'ch','row','sub'}, dimensions={0} | all-to-all | bytes 4194304 | tf_op jit(solution)/shard_map/all_to_all | solution.py:163
  591.5 14.4 %shard_map.87.held_ref = bf16[128,128,128]{2,1,0:T(8,128)(2,1)} custom-call(bf16[128,128,128]{2,1,0:T(8,128)(2,1)} %pair_ref.13, bf16[16,64,8,128]{3,2,1,0:T(8,128)(2,1)S(1)} %all-to-all-done.9.left_ref, bf16[16,64,8,128]{3,2,1,0:T(8,128)(2,1)S(1)} %copy-done.1, bf16[64,128,128]{2,1,0:T(8,128)(2,1)} %copy-done.2, ...), custom_call_target="tpu_custom_call", output_to_operand_aliasing={{}: (7, {})} | custom-call | flops 2415919104 | bytes 10485760 | tf_op jit(solution)/shard_map/pallas_call | solution.py:196
  605.9 29.9 %all-to-all-done.8.right_ref = bf16[16,64,8,128]{3,2,1,0:T(8,128)(2,1)} async-done(((bf16[16,64,8,128]{3,2,1,0:T(8,128)(2,1)}), bf16[16,64,8,128]{3,2,1,0:T(8,128)(2,1)}, u32[]{:S(2)}, u32[]{:S(2)}) %all-to-all-start.8) | async-done | bytes 2097184 | tf_op jit(solution)/shard_map/all_to_all | solution.py:163
  635.8 14.5 %shard_map.88 = bf16[128,128,128]{2,1,0:T(8,128)(2,1)} custom-call(bf16[128,128,128]{2,1,0:T(8,128)(2,1)} %pair_ref.13, bf16[16,64,8,128]{3,2,1,0:T(8,128)(2,1)} %all-to-all-done.4.left_ref, bf16[16,64,8,128]{3,2,1,0:T(8,128)(2,1)} %all-to-all-done.8.right_ref, bf16[64,128,128]{2,1,0:T(8,128)(2,1)} %copy-done.3, ...), custom_call_target="tpu_custom_call", output_to_operand_aliasing={{}: (7, {})} | custom-call | flops 2415919104 | bytes 10485760 | tf_op jit(solution)/shard_map/pallas_call | solution.py:196
  (76 shorter events, 139.2 us)
Async XLA Ops:
  10.9 54.0 %all-to-all-start.5 = ((bf16[16,64,8,128]{3,2,1,0:T(8,128)(2,1)}), bf16[16,64,8,128]{3,2,1,0:T(8,128)(2,1)S(1)}, u32[]{:S(2)}, u32[]{:S(2)}) async-start(bf16[16,64,8,128]{3,2,1,0:T(8,128)(2,1)} %shard_map.85), calls=%async_computation.5 | async-start | bytes 4194304 | tf_op jit(solution)/shard_map/all_to_all | solution.py:163
  31.3 2.0 copy-start
  64.8 97.4 %all-to-all-start.1 = ((bf16[16,128,8,128]{3,2,1,0:T(8,128)(2,1)}), bf16[16,128,8,128]{3,2,1,0:T(8,128)(2,1)}, u32[]{:S(2)}, u32[]{:S(2)}) async-start(bf16[16,128,8,128]{3,2,1,0:T(8,128)(2,1)} %copy-done), calls=%async_computation.1 | async-start | bytes 8388608 | tf_op jit(solution)/shard_map/all_to_all | solution.py:163
  162.2 52.4 %all-to-all-start = ((bf16[16,64,8,128]{3,2,1,0:T(8,128)(2,1)}), bf16[16,64,8,128]{3,2,1,0:T(8,128)(2,1)}, u32[]{:S(2)}, u32[]{:S(2)}) async-start(bf16[16,64,8,128]{3,2,1,0:T(8,128)(2,1)} %shard_map.82), calls=%async_computation | async-start | bytes 4194304 | tf_op jit(solution)/shard_map/all_to_all | solution.py:163
  172.8 15.4 %copy-start.7 = (bf16[8,256,512]{2,1,0:T(8,128)(2,1)}, bf16[8,256,512]{2,1,0:T(8,128)(2,1)S(1)}, u32[]{:S(2)}) copy-start(bf16[8,256,512]{2,1,0:T(8,128)(2,1)S(1)} %reshape.130) | copy-start | bytes 6291460
  214.6 52.6 %all-to-all-start.6 = ((bf16[16,64,8,128]{3,2,1,0:T(8,128)(2,1)}), bf16[16,64,8,128]{3,2,1,0:T(8,128)(2,1)}, u32[]{:S(2)}, u32[]{:S(2)}) async-start(bf16[16,64,8,128]{3,2,1,0:T(8,128)(2,1)} %bitcast.22), calls=%async_computation.6 | async-start | bytes 4194304 | tf_op jit(solution)/shard_map/all_to_all | solution.py:163
  227.2 5.6 copy-start.9
  267.2 5.1 copy-start.13
  267.2 5.2 copy-start.4
  267.2 5.3 copy-start.14
  267.2 5.4 copy-start.6
  267.2 52.5 %all-to-all-start.2 = ((bf16[16,64,8,128]{3,2,1,0:T(8,128)(2,1)}), bf16[16,64,8,128]{3,2,1,0:T(8,128)(2,1)S(1)}, u32[]{:S(2)}, u32[]{:S(2)}) async-start(bf16[16,64,8,128]{3,2,1,0:T(8,128)(2,1)} %bitcast.11), calls=%async_computation.2 | async-start | bytes 4194304 | tf_op jit(solution)/shard_map/all_to_all | solution.py:163
  283.7 1.4 copy-start.2
  319.7 1.3 copy-start.12
  321.0 52.3 %all-to-all-start.7 = ((bf16[16,64,8,128]{3,2,1,0:T(8,128)(2,1)}), bf16[16,64,8,128]{3,2,1,0:T(8,128)(2,1)S(1)}, u32[]{:S(2)}, u32[]{:S(2)}) async-start(bf16[16,64,8,128]{3,2,1,0:T(8,128)(2,1)} %get-tuple-element.10), calls=%async_computation.7 | async-start | bytes 4194304 | tf_op jit(solution)/shard_map/all_to_all | solution.py:163
  336.9 1.4 copy-start.3
  373.4 52.4 %all-to-all-start.3 = ((bf16[16,64,8,128]{3,2,1,0:T(8,128)(2,1)}), bf16[16,64,8,128]{3,2,1,0:T(8,128)(2,1)}, u32[]{:S(2)}, u32[]{:S(2)}) async-start(bf16[16,64,8,128]{3,2,1,0:T(8,128)(2,1)} %get-tuple-element.9), calls=%async_computation.3 | async-start | bytes 4194304 | tf_op jit(solution)/shard_map/all_to_all | solution.py:163
  384.0 5.6 copy-start.8
  425.8 52.3 %all-to-all-start.9 = ((bf16[16,64,8,128]{3,2,1,0:T(8,128)(2,1)}), bf16[16,64,8,128]{3,2,1,0:T(8,128)(2,1)S(1)}, u32[]{:S(2)}, u32[]{:S(2)}) async-start(bf16[16,64,8,128]{3,2,1,0:T(8,128)(2,1)} %bitcast.74), calls=%async_computation.9 | async-start | bytes 4194304 | tf_op jit(solution)/shard_map/all_to_all | solution.py:163
  478.1 52.4 %all-to-all-start.4 = ((bf16[16,64,8,128]{3,2,1,0:T(8,128)(2,1)}), bf16[16,64,8,128]{3,2,1,0:T(8,128)(2,1)}, u32[]{:S(2)}, u32[]{:S(2)}) async-start(bf16[16,64,8,128]{3,2,1,0:T(8,128)(2,1)} %bitcast.72), calls=%async_computation.4 | async-start | bytes 4194304 | tf_op jit(solution)/shard_map/all_to_all | solution.py:163
  483.0 3.7 copy-start.10
  483.0 3.7 copy-start.11
  582.9 52.9 %all-to-all-start.8 = ((bf16[16,64,8,128]{3,2,1,0:T(8,128)(2,1)}), bf16[16,64,8,128]{3,2,1,0:T(8,128)(2,1)}, u32[]{:S(2)}, u32[]{:S(2)}) async-start(bf16[16,64,8,128]{3,2,1,0:T(8,128)(2,1)} %get-tuple-element.14), calls=%async_computation.8 | async-start | bytes 4194304 | tf_op jit(solution)/shard_map/all_to_all | solution.py:163
  588.4 3.1 copy-start.1
  (1 other events, 0.7 us)

commit v2 on v1

v2 whole, which is shorter than its diff:
```python
import functools

import jax
import jax.numpy as jnp
from jax import lax
from jax.experimental import pallas as pl
from jax.experimental.pallas import tpu as pltpu
from jax.sharding import Mesh
from jax.sharding import PartitionSpec as P

epsilon = 1e-05
F32 = jnp.float32
BF16 = jnp.bfloat16
VMEM_LIMIT = 48 * 1024 * 1024
GROUP = ("rep", "low", "row", "sub")
SWAP = ("rep", "high")


def dot(a, b, ca, cb):
    return lax.dot_general(a, b, (((ca,), (cb,)), ((), ())), preferred_element_type=F32)


def norm_rows(pair_block, gain):
    x = pair_block.astype(F32)
    center = x - jnp.mean(x, axis=1, keepdims=True)
    scaled = lax.rsqrt(jnp.mean(center * center, axis=1, keepdims=True) + epsilon)
    hat = center * scaled
    return hat, scaled, (hat * gain).astype(BF16)


def rows_of(ref, first, count):
    block = ref[first:first + count]
    return block.reshape(count * block.shape[1], block.shape[2])


def load_chan(ref, slot, first, count):
    parts = [ref[:, slot, first + t] for t in range(count)]
    parts = [p.astype(F32).reshape(p.shape[0] * p.shape[1], p.shape[2]) for p in parts]
    return parts[0] if count == 1 else jnp.concatenate(parts, axis=1)


def store_chan(ref, slot, first, count, value):
    groups, _, _, chans, cols = ref.shape
    for t in range(count):
        part = value[:, t * cols:(t + 1) * cols] if count > 1 else value
        ref[:, slot, first + t] = part.reshape(groups, chans, cols).astype(BF16)


def project_kernel(step, flip_ref, pair_a, pair_b, mask_a, mask_b, gain_ref, weight_ref, left_ref, right_ref):
    rows, cols, chans = pair_a.shape
    for which, (pair_ref, mask_ref) in enumerate(((pair_a, mask_a), (pair_b, mask_b))):
        slot = flip_ref[which]
        for first in range(0, rows, step):
            _, _, normed = norm_rows(rows_of(pair_ref, first, step), gain_ref[...])
            proj = dot(weight_ref[...], normed, 1, 1)
            mask = mask_ref[0, :, first * cols:(first + step) * cols]
            left = mask * jax.nn.sigmoid(proj[chans:2 * chans]) * proj[:chans]
            right = mask * jax.nn.sigmoid(proj[3 * chans:]) * proj[2 * chans:3 * chans]
            store_chan(left_ref, slot, first, step, left)
            store_chan(right_ref, slot, first, step, right)


def middle_kernel(
    step, flip_ref, pair_a, pair_b, gout_a, gout_b, comb_ref, gain_ref, gate_t_ref, out_w_ref, out_t_ref,
    out_gain_ref, eye_ref, gcomb_ref, sigm_ref,
):
    rows, cols, chans = pair_a.shape
    out_gain = out_gain_ref[...]
    for which, (pair_ref, gout_ref) in enumerate(((pair_a, gout_a), (pair_b, gout_b))):
        slot = flip_ref[which]
        for first in range(0, rows, step):
            _, _, normed = norm_rows(rows_of(pair_ref, first, step), gain_ref[...])
            gate = jax.nn.sigmoid(dot(gate_t_ref[...], normed, 1, 1))
            gout = dot(eye_ref[...], rows_of(gout_ref, first, step), 1, 1)
            comb = load_chan(comb_ref, slot, first, step)
            center = comb - jnp.mean(comb, axis=0, keepdims=True)
            scaled = lax.rsqrt(jnp.mean(center * center, axis=0, keepdims=True) + epsilon)
            hat = center * scaled
            lin = dot(out_t_ref[...], (hat * out_gain).astype(BF16), 1, 0)
            grad_lin = (gout * gate).astype(BF16)
            h = dot(out_w_ref[...], grad_lin, 1, 0) * out_gain
            grad = scaled * (
                h - jnp.mean(h, axis=0, keepdims=True) - hat * jnp.mean(h * hat, axis=0, keepdims=True)
            )
            store_chan(gcomb_ref, slot, first, step, grad)
            sigm = (gout * lin * gate * (1.0 - gate)).astype(BF16)
            for t in range(step):
                sigm_ref[which, first + t] = sigm[:, t * cols:(t + 1) * cols] if step > 1 else sigm


def last_kernel(
    step, flip_ref, pair_a, pair_b, left_ref, right_ref, sigm_ref, mask_a, mask_b, gain_ref, weight_ref, out_a, out_b
):
    rows, cols, chans = pair_a.shape
    gain = gain_ref[...]
    weight = weight_ref[...]
    for which, (pair_ref, mask_ref, out_ref) in enumerate(((pair_a, mask_a, out_a), (pair_b, mask_b, out_b))):
        slot = flip_ref[which]
        for first in range(0, rows, step):
            hat, scaled, normed = norm_rows(rows_of(pair_ref, first, step), gain)
            mask = mask_ref[0, :, first * cols:(first + step) * cols]
            proj = dot(weight[:4 * chans], normed, 1, 1)
            terms = []
            for side, ref in enumerate((left_ref, right_ref)):
                grad = load_chan(ref, slot, first, step) * mask
                value = proj[2 * side * chans:(2 * side + 1) * chans]
                gate = jax.nn.sigmoid(proj[(2 * side + 1) * chans:(2 * side + 2) * chans])
                through = grad * gate
                terms += [through.astype(BF16), (through * value * (1.0 - gate)).astype(BF16)]
            parts = [sigm_ref[which, first + t] for t in range(step)]
            terms.append(parts[0] if step == 1 else jnp.concatenate(parts, axis=1))
            g = dot(jnp.concatenate(terms, axis=0), weight, 0, 0) * gain
            grad_in = scaled * (
                g - jnp.mean(g, axis=1, keepdims=True) - hat * jnp.mean(g * hat, axis=1, keepdims=True)
            )
            out_ref[first:first + step] = grad_in.reshape(step, cols, chans).astype(BF16)


def local(chunks, pair, grad_out, token_mask, ln_gain, proj_weights, gate_weight, out_weight, out_gain):
    full_rows, cols, chans = pair.shape
    halves = lax.axis_size("rep")
    low = lax.axis_size("low")
    row_blocks = lax.axis_size(("row", "sub"))
    peers = halves * low * row_blocks
    own = chans // peers
    tokens = full_rows * row_blocks
    half_rows = full_rows // halves
    rows = half_rows // chunks
    block = min(4, rows)
    blocks = rows // block
    step = 4 if cols % 128 == 0 and block % 4 == 0 else 1
    rep, high = lax.axis_index("rep"), lax.axis_index("high")

    places = [(y, b) for y in range(halves) for b in range(halves)]
    at = {place: n for n, place in enumerate(places)}
    goes = [
        [(at[y, b], at[b, y]) for y, b in places],
        [(at[y, b], at[1 - b, y]) for y, b in places],
    ]
    back = [[(d, s) for s, d in perm] for perm in goes]
    half_of = [high, 1 - high]

    def move_in(array, part):
        return [
            lax.ppermute(
                lax.dynamic_slice_in_dim(array, half_of[w] * half_rows + part * rows, rows), SWAP, goes[w]
            )
            for w in range(2)
        ]

    pairs = [move_in(pair, part) for part in range(chunks)]
    mask_float = lax.ppermute(token_mask.astype(F32), SWAP, goes[0])
    gouts = [move_in(grad_out, part) for part in range(chunks)]

    flip = jnp.stack([rep, 1 - rep]).astype(jnp.int32)
    row_mask = lax.dynamic_slice_in_dim(
        mask_float, lax.axis_index(("row", "sub")) * full_rows + rep * half_rows, half_rows
    )

    def pair_mask(slot):
        col_mask = lax.dynamic_slice_in_dim(mask_float, (slot * low + lax.axis_index("low")) * cols, cols)
        return (row_mask[:, None] * col_mask[None, :]).reshape(half_rows // block, 1, block * cols)

    masks = [pair_mask(rep), pair_mask(1 - rep)]
    gain = ln_gain.reshape(1, chans)
    gain_col = out_gain.reshape(chans, 1)
    proj_t = jnp.swapaxes(proj_weights, 1, 2).reshape(4 * chans, chans)
    gate_t = gate_weight.T
    out_t = out_weight.T
    all_w = jnp.concatenate([proj_t, gate_t], axis=0)
    eye = jnp.eye(chans, dtype=BF16)

    row_spec = pl.BlockSpec((block, cols, chans), lambda s, f: (s, 0, 0))
    chan_spec = pl.BlockSpec((peers, halves, block, own, cols), lambda s, f: (0, 0, s, 0, 0))
    sigm_spec = pl.BlockSpec((halves, block, chans, cols), lambda s, f: (0, s, 0, 0))
    row_shape = jax.ShapeDtypeStruct((rows, cols, chans), BF16)
    chan_shape = jax.ShapeDtypeStruct((peers, halves, rows, own, cols), BF16)
    sigm_shape = jax.ShapeDtypeStruct((halves, rows, chans, cols), BF16)

    def mask_spec(part):
        return pl.BlockSpec((1, 1, block * cols), lambda s, f: (part * blocks + s, 0, 0))

    def whole(array):
        return pl.BlockSpec(array.shape, lambda s, f: (0,) * array.ndim)

    def call(kernel, in_specs, out_specs, out_shape, flops, arrays, operands):
        count = halves * rows * cols
        return pl.pallas_call(
            functools.partial(kernel, step),
            grid_spec=pltpu.PrefetchScalarGridSpec(
                num_scalar_prefetch=1, grid=(blocks,), in_specs=in_specs, out_specs=out_specs
            ),
            out_shape=out_shape,
            compiler_params=pltpu.CompilerParams(vmem_limit_bytes=VMEM_LIMIT),
            cost_estimate=pl.CostEstimate(
                flops=flops * chans * chans * count, bytes_accessed=arrays * chans * 2 * count,
                transcendentals=chans * count,
            ),
        )(flip, *operands)

    def project(part):
        return call(
            project_kernel,
            [row_spec] * 2 + [mask_spec(part)] * 2 + [whole(gain), whole(proj_t)],
            [chan_spec] * 2, [chan_shape] * 2, 8, 3,
            (*pairs[part], *masks, gain, proj_t),
        )

    def middle(comb, part):
        return call(
            middle_kernel,
            [row_spec] * 4 + [chan_spec, whole(gain), whole(gate_t), whole(out_weight), whole(out_t),
                              whole(gain_col), whole(eye)],
            [chan_spec, sigm_spec], [chan_shape, sigm_shape], 8, 5,
            (*pairs[part], *gouts[part], comb, gain, gate_t, out_weight, out_t, gain_col, eye),
        )

    def last(left_grad, right_grad, sigm, part):
        return call(
            last_kernel,
            [row_spec] * 2 + [chan_spec] * 2 + [sigm_spec] + [mask_spec(part)] * 2 + [whole(gain), whole(all_w)],
            [row_spec] * 2, [row_shape] * 2, 18, 5,
            (*pairs[part], left_grad, right_grad, sigm, *masks, gain, all_w),
        )

    def exchange(array):
        return lax.all_to_all(array, GROUP, split_axis=0, concat_axis=0, tiled=True)

    def by_channel(array):
        array = array.reshape(halves, low, row_blocks, halves, rows, own, cols)
        return jnp.transpose(array, (5, 2, 0, 4, 3, 1, 6)).reshape(own, row_blocks, halves, rows, tokens)

    def flat(array):
        return array.reshape(own, -1, tokens)

    def by_owner(array):
        array = array.astype(BF16).reshape(own, row_blocks, halves, rows, halves, low, cols)
        return jnp.transpose(array, (2, 5, 1, 4, 3, 0, 6)).reshape(peers, halves, rows, own, cols)

    def batch_dot(a, b, ca, cb):
        return lax.dot_general(a, b, (((ca,), (cb,)), ((0,), (0,))), preferred_element_type=F32)

    lefts, rights = [], []
    for part in range(chunks):
        left, right = project(part)
        rights.append(by_channel(exchange(right)))
        lefts.append(flat(by_channel(exchange(left))))
    right = flat(jnp.concatenate(rights, axis=3))

    sigms, left_grads, grad_parts = [], [], []
    for part in range(chunks):
        comb = exchange(by_owner(batch_dot(lefts[part], right, 2, 2)))
        grad_comb, sigm = middle(comb, part)
        sigms.append(sigm)
        grad_comb = flat(by_channel(exchange(grad_comb)))
        left_grads.append(exchange(by_owner(batch_dot(grad_comb, right, 2, 1))))
        grad_parts.append(batch_dot(grad_comb, lefts[part], 1, 1))
    grad_right = functools.reduce(jnp.add, grad_parts).astype(BF16)
    grad_right = grad_right.reshape(own, row_blocks, halves, chunks, rows, tokens)

    out = jnp.zeros((full_rows, cols, chans), BF16)
    for part in range(chunks):
        right_grad = exchange(by_owner(grad_right[:, :, :, part]))
        results = last(left_grads[part], right_grad, sigms[part], part)
        for w in range(2):
            home = lax.ppermute(results[w], SWAP, back[w])
            out = lax.dynamic_update_slice_in_dim(out, home, half_of[w] * half_rows + part * rows, 0)
    return out


def solution(mesh):
    size = mesh.shape
    halves = size["rep"]
    split = (size["rep"], halves, size["ch"] // halves, size["row"], size["sub"])
    fine = Mesh(mesh.devices.reshape(split), ("rep", "high", "low", "row", "sub"))
    spread = P(("rep", "row", "sub"), ("high", "low"), None)
    return jax.shard_map(
        functools.partial(local, 2),
        mesh=fine,
        in_specs=(spread, spread, P("rep"), P(), P(), P(), P(), P()),
        out_specs=spread,
        check_vma=False,
    )
```

time: 662 us -> 854 us (1.29)
  waiting for transfers between devices: 338 us -> 438 us
  starting transfers between devices: 51.8 us -> 120 us
  local copies, waits for them, and re-layouts: 98.3 us -> 128 us
  Pallas kernels: 81.1 us -> 67 us
    ppermute x0 -> x13, waiting for transfers between devices: none -> 405 us  [the longest x8 264 us: move_in(): lax.ppermute(lax.dynamic_slice_in_dim(array, half_of[w] * half_rows + par...]
    all_to_all x10, waiting for transfers between devices: 338 us -> 33.3 us  [exchange(): return lax.all_to_all(array, GROUP, split_axis=0, concat_axis=0, tiled=True)]
    ppermute x0 -> x13, starting transfers between devices: none -> 44.2 us  [the longest x4 19.9 us: local(): home = lax.ppermute(results[w], SWAP, back[w])]
    another operation x0 -> x6, local copies, waits for them, and re-layouts: none -> 24.5 us  [the longest x4 16.5 us: flat(): return array.reshape(own, -1, tokens)]
    all_to_all x10, starting transfers between devices: 51.8 us -> 75.9 us  [exchange(): return lax.all_to_all(array, GROUP, split_axis=0, concat_axis=0, tiled=True)]
    pallas_call x7 -> x6, Pallas kernels: 81.1 us -> 67 us  [call(): pl.pallas_call(functools.partial(kernel, step), grid_spec=pltpu.PrefetchS...]
    reshape x17 -> x14, local copies, waits for them, and re-layouts: 64.3 us -> 57.1 us  [the longest x8 33.4 us: by_owner(): array.astype(BF16).reshape(own, row_blocks, halves, rows, halves, low, cols)]
    all_to_all x1 -> x2, blocking collectives: 52.3 us -> 59.3 us  [exchange(): return lax.all_to_all(array, GROUP, split_axis=0, concat_axis=0, tiled=True)]
  transfers between devices with their start and end apart: 10 -> 23, of which waited for: 10 -> 14; matrix products, arithmetic and copies ran while one was open for 18% -> 17% of each run, Pallas kernels for 9% -> 7%
where the time goes in v2:
time: 854 us; the launch traced here: 840 us
  waiting for transfers between devices  438 us (51%)
  local copies, waits for them, and re-layouts  128 us (15%)
  starting transfers between devices  120 us (14%)
  Pallas kernels  67 us (8%)
  blocking collectives  59.3 us (7%)
  matrix products  24 us (3%)
    ppermute x8, waiting for transfers between devices, move_in(): lax.ppermute(lax.dynamic_slice_in_dim(array, half_of[w] * half_rows + par...  264 us
    ppermute x1, waiting for transfers between devices, local(): mask_float = lax.ppermute(token_mask.astype(F32), SWAP, goes[0])  83.2 us
    all_to_all x10, starting transfers between devices, exchange(): return lax.all_to_all(array, GROUP, split_axis=0, concat_axis=0, tiled=True)  75.9 us
    pallas_call x6, Pallas kernels, call(): pl.pallas_call(functools.partial(kernel, step), grid_spec=pltpu.PrefetchS...  67 us
    all_to_all x2, blocking collectives, exchange(): return lax.all_to_all(array, GROUP, split_axis=0, concat_axis=0, tiled=True)  59.3 us
    ppermute x4, waiting for transfers between devices, local(): home = lax.ppermute(results[w], SWAP, back[w])  57.8 us
    reshape x8, local copies, waits for them, and re-layouts, by_owner(): array.astype(BF16).reshape(own, row_blocks, halves, rows, halves, low, cols)  33.4 us
    all_to_all x10, waiting for transfers between devices, exchange(): return lax.all_to_all(array, GROUP, split_axis=0, concat_axis=0, tiled=True)  33.3 us
  transfers between devices with their start and end apart: 23, of which 14 were waited for; matrix products, arithmetic and copies ran while one was open for 17% of the time, Pallas kernels for 7%

profile of v2, /device:TPU:15, one launch (start us, length us, event | category | flops | bytes accessed | tf_op | source)
XLA Modules:
  0.0 840.4 jit_solution(15911871140159292788)
XLA Ops:
  13.7 83.2 %collective-permute-done.4 = f32[512]{0:T(512)S(1)} collective-permute-done((f32[512]{0:T(512)S(1)}, f32[512]{0:T(512)S(1)}, u32[]{:S(2)}, u32[]{:S(2)}) %collective-permute-start.4) | collective-permute-done | bytes 2080 | tf_op jit(solution)/shard_map/ppermute | solution.py:152
  104.5 29.3 %all_to_all.60 = bf16[16,2,32,8,128]{4,3,2,1,0:T(8,128)(2,1)} all-to-all(bf16[16,2,32,8,128]{4,3,2,1,0:T(8,128)(2,1)} %get-tuple-element.19), channel_id=1, replica_groups=mesh['rep'=2,'high'=2,'low'=2,'row'=2,'sub'=2] {'rep','low','row','sub'}, dimensions={0} | all-to-all | bytes 4194304 | tf_op jit(solution)/shard_map/all_to_all | solution.py:227
  146.7 65.6 %collective-permute-done.1.pair_b = bf16[32,128,128]{2,1,0:T(8,128)(2,1)S(1)} collective-permute-done((bf16[32,128,128]{2,1,0:T(8,128)(2,1)}, bf16[32,128,128]{2,1,0:T(8,128)(2,1)S(1)}, u32[]{:S(2)}, u32[]{:S(2)}) %collective-permute-start.1) | collective-permute-done | bytes 1048608 | tf_op jit(solution)/shard_map/ppermute | solution.py:145
  212.2 22.5 %collective-permute-done.pair_a = bf16[32,128,128]{2,1,0:T(8,128)(2,1)S(1)} collective-permute-done((bf16[32,128,128]{2,1,0:T(8,128)(2,1)}, bf16[32,128,128]{2,1,0:T(8,128)(2,1)S(1)}, u32[]{:S(2)}, u32[]{:S(2)}) %collective-permute-start) | collective-permute-done | bytes 1048608 | tf_op jit(solution)/shard_map/ppermute | solution.py:145
  243.0 30.0 %all_to_all.61 = bf16[16,2,32,8,128]{4,3,2,1,0:T(8,128)(2,1)} all-to-all(bf16[16,2,32,8,128]{4,3,2,1,0:T(8,128)(2,1)} %get-tuple-element.18), channel_id=1, replica_groups=mesh['rep'=2,'high'=2,'low'=2,'row'=2,'sub'=2] {'rep','low','row','sub'}, dimensions={0} | all-to-all | bytes 4194304 | tf_op jit(solution)/shard_map/all_to_all | solution.py:227
  273.0 8.1 all-to-all-start
  355.6 8.2 all-to-all-start.3
  373.4 65.2 %collective-permute-done.8.gout_b = bf16[32,128,128]{2,1,0:T(8,128)(2,1)} collective-permute-done((bf16[32,128,128]{2,1,0:T(8,128)(2,1)}, bf16[32,128,128]{2,1,0:T(8,128)(2,1)}, u32[]{:S(2)}, u32[]{:S(2)}) %collective-permute-start.8) | collective-permute-done | bytes 1048608 | tf_op jit(solution)/shard_map/ppermute | solution.py:145
  438.6 22.5 %collective-permute-done.7.gout_a = bf16[32,128,128]{2,1,0:T(8,128)(2,1)} collective-permute-done((bf16[32,128,128]{2,1,0:T(8,128)(2,1)}, bf16[32,128,128]{2,1,0:T(8,128)(2,1)}, u32[]{:S(2)}, u32[]{:S(2)}) %collective-permute-start.7) | collective-permute-done | bytes 1048608 | tf_op jit(solution)/shard_map/ppermute | solution.py:145
  461.1 11.8 %shard_map.85 = (bf16[16,2,32,8,128]{4,3,2,1,0:T(8,128)(2,1)}, bf16[2,32,128,128]{3,2,1,0:T(8,128)(2,1)}) custom-call(s32[2]{0:T(128)S(1)} %pad_add_fusion.flip_ref, bf16[32,128,128]{2,1,0:T(8,128)(2,1)S(1)} %collective-permute-done.5.pair_a, bf16[32,128,128]{2,1,0:T(8,128)(2,1)S(1)} %collective-permute-done.6.pair_b, ...), custom_call_target="tpu_custom_call" | custom-call | flops 1073741824 | bytes 10485760 | tf_op jit(solution)/shard_map/pallas_call | solution.py:188
  483.8 65.6 %collective-permute-done.3.gout_b = bf16[32,128,128]{2,1,0:T(8,128)(2,1)S(1)} collective-permute-done((bf16[32,128,128]{2,1,0:T(8,128)(2,1)}, bf16[32,128,128]{2,1,0:T(8,128)(2,1)S(1)}, u32[]{:S(2)}, u32[]{:S(2)}) %collective-permute-start.3) | collective-permute-done | bytes 1048608 | tf_op jit(solution)/shard_map/ppermute | solution.py:145
  549.4 22.5 %collective-permute-done.2.gout_a = bf16[32,128,128]{2,1,0:T(8,128)(2,1)S(1)} collective-permute-done((bf16[32,128,128]{2,1,0:T(8,128)(2,1)}, bf16[32,128,128]{2,1,0:T(8,128)(2,1)S(1)}, u32[]{:S(2)}, u32[]{:S(2)}) %collective-permute-start.2) | collective-permute-done | bytes 1048608 | tf_op jit(solution)/shard_map/ppermute | solution.py:145
  573.1 11.3 %shard_map.84 = (bf16[16,2,32,8,128]{4,3,2,1,0:T(8,128)(2,1)}, bf16[2,32,128,128]{3,2,1,0:T(8,128)(2,1)}) custom-call(s32[2]{0:T(128)S(1)} %pad_add_fusion.flip_ref, bf16[32,128,128]{2,1,0:T(8,128)(2,1)S(1)} %copy-done.1, bf16[32,128,128]{2,1,0:T(8,128)(2,1)S(1)} %collective-permute-done.1.pair_b, bf16[32,128,128]{2,1,0:T(8,128)(2,1)S(1)} %collective-permute-done.2.gout_a, ...), custom_call_target="tpu_custom_call" | custom-call | flops 1073741824 | bytes 10485760 | tf_op jit(solution)/shard_map/pallas_call | solution.py:188
  616.2 8.2 all-to-all-start.10
  649.8 8.7 %all-to-all-start.5 = ((bf16[16,2,32,8,128]{4,3,2,1,0:T(8,128)(2,1)}), bf16[16,2,32,8,128]{4,3,2,1,0:T(8,128)(2,1)}, u32[]{:S(2)}, u32[]{:S(2)}) async-start(bf16[16,2,32,8,128]{4,3,2,1,0:T(8,128)(2,1)} %bitcast.98), calls=%async_computation.5 | async-start | bytes 4194304 | tf_op jit(solution)/shard_map/all_to_all | solution.py:227
  674.2 9.5 %all-to-all-done.5.left_ref = bf16[16,2,32,8,128]{4,3,2,1,0:T(8,128)(2,1)} async-done(((bf16[16,2,32,8,128]{4,3,2,1,0:T(8,128)(2,1)}), bf16[16,2,32,8,128]{4,3,2,1,0:T(8,128)(2,1)}, u32[]{:S(2)}, u32[]{:S(2)}) %all-to-all-start.5) | async-done | bytes 2097184 | tf_op jit(solution)/shard_map/all_to_all | solution.py:227
  683.7 8.4 %all-to-all-start.9 = ((bf16[16,2,32,8,128]{4,3,2,1,0:T(8,128)(2,1)}), bf16[16,2,32,8,128]{4,3,2,1,0:T(8,128)(2,1)}, u32[]{:S(2)}, u32[]{:S(2)}) async-start(bf16[16,2,32,8,128]{4,3,2,1,0:T(8,128)(2,1)} %bitcast.102), calls=%async_computation.9 | async-start | bytes 4194304 | tf_op jit(solution)/shard_map/all_to_all | solution.py:227
  700.4 17.1 %all-to-all-done.9.right_ref = bf16[16,2,32,8,128]{4,3,2,1,0:T(8,128)(2,1)} async-done(((bf16[16,2,32,8,128]{4,3,2,1,0:T(8,128)(2,1)}), bf16[16,2,32,8,128]{4,3,2,1,0:T(8,128)(2,1)}, u32[]{:S(2)}, u32[]{:S(2)}) %all-to-all-start.9) | async-done | bytes 2097184 | tf_op jit(solution)/shard_map/all_to_all | solution.py:227
  717.5 8.5 %all-to-all-start.11 = ((bf16[16,2,32,8,128]{4,3,2,1,0:T(8,128)(2,1)}), bf16[16,2,32,8,128]{4,3,2,1,0:T(8,128)(2,1)}, u32[]{:S(2)}, u32[]{:S(2)}) async-start(bf16[16,2,32,8,128]{4,3,2,1,0:T(8,128)(2,1)} %bitcast.97), calls=%async_computation.11 | async-start | bytes 4194304 | tf_op jit(solution)/shard_map/all_to_all | solution.py:227
  727.3 15.0 %shard_map.86 = (bf16[32,128,128]{2,1,0:T(8,128)(2,1)}, bf16[32,128,128]{2,1,0:T(8,128)(2,1)}) custom-call(s32[2]{0:T(128)S(1)} %pad_add_fusion.flip_ref, bf16[32,128,128]{2,1,0:T(8,128)(2,1)S(1)} %copy-done.2, bf16[32,128,128]{2,1,0:T(8,128)(2,1)S(1)} %collective-permute-done.1.pair_b, bf16[16,2,32,8,128]{4,3,2,1,0:T(8,128)(2,1)} %all-to-all-done.5.left_ref, ...), custom_call_target="tpu_custom_call" | custom-call | flops 2415919104 | bytes 10485760 | tf_op jit(solution)/shard_map/pallas_call | solution.py:188
  752.1 14.3 %shard_map.87 = (bf16[32,128,128]{2,1,0:T(8,128)(2,1)S(1)}, bf16[32,128,128]{2,1,0:T(8,128)(2,1)S(1)}) custom-call(s32[2]{0:T(128)S(1)} %pad_add_fusion.flip_ref, bf16[32,128,128]{2,1,0:T(8,128)(2,1)S(1)} %collective-permute-done.5.pair_a, bf16[32,128,128]{2,1,0:T(8,128)(2,1)S(1)} %collective-permute-done.6.pair_b, ...), custom_call_target="tpu_custom_call" | custom-call | flops 2415919104 | bytes 10485760 | tf_op jit(solution)/shard_map/pallas_call | solution.py:188
  766.4 10.1 %collective-permute-start.11 = (bf16[32,128,128]{2,1,0:T(8,128)(2,1)S(1)}, bf16[32,128,128]{2,1,0:T(8,128)(2,1)S(1)}, u32[]{:S(2)}, u32[]{:S(2)}) collective-permute-start(bf16[32,128,128]{2,1,0:T(8,128)(2,1)S(1)} %get-tuple-element.27), channel_id=1, source_target_pairs={{0,0},{16,8},{8,16},{24,24},{1,1},{17,9},{9,17},{25,25},{2,2},{18,... | collective-permute-start | bytes 3145736 | tf_op jit(solution)/shard_map/ppermute | solution.py:266
  776.6 15.6 %collective-permute-done.9 = bf16[32,128,128]{2,1,0:T(8,128)(2,1)} collective-permute-done((bf16[32,128,128]{2,1,0:T(8,128)(2,1)}, bf16[32,128,128]{2,1,0:T(8,128)(2,1)}, u32[]{:S(2)}, u32[]{:S(2)}) %collective-permute-start.9) | collective-permute-done | bytes 1048608 | tf_op jit(solution)/shard_map/ppermute | solution.py:266
  794.8 42.2 %collective-permute-done.11 = bf16[32,128,128]{2,1,0:T(8,128)(2,1)S(1)} collective-permute-done((bf16[32,128,128]{2,1,0:T(8,128)(2,1)S(1)}, bf16[32,128,128]{2,1,0:T(8,128)(2,1)S(1)}, u32[]{:S(2)}, u32[]{:S(2)}) %collective-permute-start.11) | collective-permute-done | bytes 1048608 | tf_op jit(solution)/shard_map/ppermute | solution.py:266
  (119 shorter events, 236.6 us)
Async XLA Ops:
  4.0 93.2 %collective-permute-start.6 = (bf16[32,128,128]{2,1,0:T(8,128)(2,1)}, bf16[32,128,128]{2,1,0:T(8,128)(2,1)S(1)}, u32[]{:S(2)}, u32[]{:S(2)}) collective-permute-start(bf16[32,128,128]{2,1,0:T(8,128)(2,1)} %get-tuple-element.35), channel_id=1, source_target_pairs={{0,16},{8,0},{16,24},{24,8},{1,17},{9,1},{17,25},{25,9},{2,18},{10... | collective-permute-start | bytes 3145736 | tf_op jit(solution)/shard_map/ppermute | solution.py:145
  6.3 90.9 %collective-permute-start.5 = (bf16[32,128,128]{2,1,0:T(8,128)(2,1)S(1)}, bf16[32,128,128]{2,1,0:T(8,128)(2,1)S(1)}, u32[]{:S(2)}, u32[]{:S(2)}) collective-permute-start(bf16[32,128,128]{2,1,0:T(8,128)(2,1)S(1)} %get-tuple-element.38), channel_id=1, source_target_pairs={{0,0},{8,16},{16,8},{24,24},{1,1},{9,17},{17,9},{25,25},{2,2},{10,... | collective-permute-start | bytes 3145736 | tf_op jit(solution)/shard_map/ppermute | solution.py:145
  8.3 88.5 %collective-permute-start.4 = (f32[512]{0:T(512)S(1)}, f32[512]{0:T(512)S(1)}, u32[]{:S(2)}, u32[]{:S(2)}) collective-permute-start(f32[512]{0:T(512)S(1)} %convert_element_type.23), channel_id=1, source_target_pairs={{0,0},{8,16},{16,8},{24,24},{1,1},{9,17},{17,9},{25,25},{2,2},{10,... | collective-permute-start | bytes 6152 | tf_op jit(solution)/shard_map/ppermute | solution.py:152
  97.2 137.5 %copy-start.4 = (f32[16,1,512]{2,1,0:T(1,128)}, f32[16,1,512]{2,1,0:T(1,128)S(1)}, u32[]{:S(2)}) copy-start(f32[16,1,512]{2,1,0:T(1,128)S(1)} %get-tuple-element.39.mask_b) | copy-start | bytes 98308
  133.8 109.2 %all-to-all-start.6 = ((bf16[16,2,32,8,128]{4,3,2,1,0:T(8,128)(2,1)}), bf16[16,2,32,8,128]{4,3,2,1,0:T(8,128)(2,1)}, u32[]{:S(2)}, u32[]{:S(2)}) async-start(bf16[16,2,32,8,128]{4,3,2,1,0:T(8,128)(2,1)} %get-tuple-element.21), calls=%async_computation.6 | async-start | bytes 4194304 | tf_op jit(solution)/shard_map/all_to_all | solution.py:227
  141.6 70.6 %collective-permute-start.1 = (bf16[32,128,128]{2,1,0:T(8,128)(2,1)}, bf16[32,128,128]{2,1,0:T(8,128)(2,1)S(1)}, u32[]{:S(2)}, u32[]{:S(2)}) collective-permute-start(bf16[32,128,128]{2,1,0:T(8,128)(2,1)} %get-tuple-element.36), channel_id=1, source_target_pairs={{0,16},{8,0},{16,24},{24,8},{1,17},{9,1},{17,25},{25,9},{2,18},{10... | collective-permute-start | bytes 3145736 | tf_op jit(solution)/shard_map/ppermute | solution.py:145
  144.7 90.0 %collective-permute-start = (bf16[32,128,128]{2,1,0:T(8,128)(2,1)}, bf16[32,128,128]{2,1,0:T(8,128)(2,1)S(1)}, u32[]{:S(2)}, u32[]{:S(2)}) collective-permute-start(bf16[32,128,128]{2,1,0:T(8,128)(2,1)} %get-tuple-element.37), channel_id=1, source_target_pairs={{0,0},{8,16},{16,8},{24,24},{1,1},{9,17},{17,9},{25,25},{2,2},{10,... | collective-permute-start | bytes 3145736 | tf_op jit(solution)/shard_map/ppermute | solution.py:145
  273.0 51.7 %all-to-all-start = ((bf16[16,2,32,8,128]{4,3,2,1,0:T(8,128)(2,1)}), bf16[16,2,32,8,128]{4,3,2,1,0:T(8,128)(2,1)}, u32[]{:S(2)}, u32[]{:S(2)}) async-start(bf16[16,2,32,8,128]{4,3,2,1,0:T(8,128)(2,1)} %get-tuple-element.17), calls=%async_computation | async-start | bytes 4194304 | tf_op jit(solution)/shard_map/all_to_all | solution.py:227
  324.7 30.9 %all-to-all-start.7 = ((bf16[16,2,32,8,128]{4,3,2,1,0:T(8,128)(2,1)}), bf16[16,2,32,8,128]{4,3,2,1,0:T(8,128)(2,1)}, u32[]{:S(2)}, u32[]{:S(2)}) async-start(bf16[16,2,32,8,128]{4,3,2,1,0:T(8,128)(2,1)} %bitcast.100), calls=%async_computation.7 | async-start | bytes 4194304 | tf_op jit(solution)/shard_map/all_to_all | solution.py:227
  355.6 117.3 %all-to-all-start.3 = ((bf16[16,2,32,8,128]{4,3,2,1,0:T(8,128)(2,1)}), bf16[16,2,32,8,128]{4,3,2,1,0:T(8,128)(2,1)}, u32[]{:S(2)}, u32[]{:S(2)}) async-start(bf16[16,2,32,8,128]{4,3,2,1,0:T(8,128)(2,1)} %bitcast.95), calls=%async_computation.3 | async-start | bytes 4194304 | tf_op jit(solution)/shard_map/all_to_all | solution.py:227
  368.1 70.5 %collective-permute-start.8 = (bf16[32,128,128]{2,1,0:T(8,128)(2,1)}, bf16[32,128,128]{2,1,0:T(8,128)(2,1)}, u32[]{:S(2)}, u32[]{:S(2)}) collective-permute-start(bf16[32,128,128]{2,1,0:T(8,128)(2,1)} %get-tuple-element.31), channel_id=1, source_target_pairs={{0,16},{8,0},{16,24},{24,8},{1,17},{9,1},{17,25},{25,9},{2,18},{10... | collective-permute-start | bytes 3145736 | tf_op jit(solution)/shard_map/ppermute | solution.py:145
  371.1 90.0 %collective-permute-start.7 = (bf16[32,128,128]{2,1,0:T(8,128)(2,1)}, bf16[32,128,128]{2,1,0:T(8,128)(2,1)}, u32[]{:S(2)}, u32[]{:S(2)}) collective-permute-start(bf16[32,128,128]{2,1,0:T(8,128)(2,1)} %get-tuple-element.34), channel_id=1, source_target_pairs={{0,0},{8,16},{16,8},{24,24},{1,1},{9,17},{17,9},{25,25},{2,2},{10,... | collective-permute-start | bytes 3145736 | tf_op jit(solution)/shard_map/ppermute | solution.py:145
  472.9 111.5 %all-to-all-start.8 = ((bf16[16,2,32,8,128]{4,3,2,1,0:T(8,128)(2,1)}), bf16[16,2,32,8,128]{4,3,2,1,0:T(8,128)(2,1)}, u32[]{:S(2)}, u32[]{:S(2)}) async-start(bf16[16,2,32,8,128]{4,3,2,1,0:T(8,128)(2,1)} %get-tuple-element.22), calls=%async_computation.8 | async-start | bytes 4194304 | tf_op jit(solution)/shard_map/all_to_all | solution.py:227
  478.8 70.6 %collective-permute-start.3 = (bf16[32,128,128]{2,1,0:T(8,128)(2,1)}, bf16[32,128,128]{2,1,0:T(8,128)(2,1)S(1)}, u32[]{:S(2)}, u32[]{:S(2)}) collective-permute-start(bf16[32,128,128]{2,1,0:T(8,128)(2,1)} %get-tuple-element.32), channel_id=1, source_target_pairs={{0,16},{8,0},{16,24},{24,8},{1,17},{9,1},{17,25},{25,9},{2,18},{10... | collective-permute-start | bytes 3145736 | tf_op jit(solution)/shard_map/ppermute | solution.py:145
  481.9 90.0 %collective-permute-start.2 = (bf16[32,128,128]{2,1,0:T(8,128)(2,1)}, bf16[32,128,128]{2,1,0:T(8,128)(2,1)S(1)}, u32[]{:S(2)}, u32[]{:S(2)}) collective-permute-start(bf16[32,128,128]{2,1,0:T(8,128)(2,1)} %get-tuple-element.33), channel_id=1, source_target_pairs={{0,0},{8,16},{16,8},{24,24},{1,1},{9,17},{17,9},{25,25},{2,2},{10,... | collective-permute-start | bytes 3145736 | tf_op jit(solution)/shard_map/ppermute | solution.py:145
  584.4 31.9 %all-to-all-start.4 = ((bf16[16,2,32,8,128]{4,3,2,1,0:T(8,128)(2,1)}), bf16[16,2,32,8,128]{4,3,2,1,0:T(8,128)(2,1)}, u32[]{:S(2)}, u32[]{:S(2)}) async-start(bf16[16,2,32,8,128]{4,3,2,1,0:T(8,128)(2,1)} %get-tuple-element.20), calls=%async_computation.4 | async-start | bytes 4194304 | tf_op jit(solution)/shard_map/all_to_all | solution.py:227
  616.2 33.5 %all-to-all-start.10 = ((bf16[16,2,32,8,128]{4,3,2,1,0:T(8,128)(2,1)}), bf16[16,2,32,8,128]{4,3,2,1,0:T(8,128)(2,1)}, u32[]{:S(2)}, u32[]{:S(2)}) async-start(bf16[16,2,32,8,128]{4,3,2,1,0:T(8,128)(2,1)} %bitcast.99), calls=%async_computation.10 | async-start | bytes 4194304 | tf_op jit(solution)/shard_map/all_to_all | solution.py:227
  649.8 33.9 %all-to-all-start.5 = ((bf16[16,2,32,8,128]{4,3,2,1,0:T(8,128)(2,1)}), bf16[16,2,32,8,128]{4,3,2,1,0:T(8,128)(2,1)}, u32[]{:S(2)}, u32[]{:S(2)}) async-start(bf16[16,2,32,8,128]{4,3,2,1,0:T(8,128)(2,1)} %bitcast.98), calls=%async_computation.5 | async-start | bytes 4194304 | tf_op jit(solution)/shard_map/all_to_all | solution.py:227
  683.7 33.8 %all-to-all-start.9 = ((bf16[16,2,32,8,128]{4,3,2,1,0:T(8,128)(2,1)}), bf16[16,2,32,8,128]{4,3,2,1,0:T(8,128)(2,1)}, u32[]{:S(2)}, u32[]{:S(2)}) async-start(bf16[16,2,32,8,128]{4,3,2,1,0:T(8,128)(2,1)} %bitcast.102), calls=%async_computation.9 | async-start | bytes 4194304 | tf_op jit(solution)/shard_map/all_to_all | solution.py:227
  717.5 34.6 %all-to-all-start.11 = ((bf16[16,2,32,8,128]{4,3,2,1,0:T(8,128)(2,1)}), bf16[16,2,32,8,128]{4,3,2,1,0:T(8,128)(2,1)}, u32[]{:S(2)}, u32[]{:S(2)}) async-start(bf16[16,2,32,8,128]{4,3,2,1,0:T(8,128)(2,1)} %bitcast.97), calls=%async_computation.11 | async-start | bytes 4194304 | tf_op jit(solution)/shard_map/all_to_all | solution.py:227
  742.3 49.9 %collective-permute-start.9 = (bf16[32,128,128]{2,1,0:T(8,128)(2,1)}, bf16[32,128,128]{2,1,0:T(8,128)(2,1)}, u32[]{:S(2)}, u32[]{:S(2)}) collective-permute-start(bf16[32,128,128]{2,1,0:T(8,128)(2,1)} %get-tuple-element.24), channel_id=1, source_target_pairs={{0,0},{16,8},{8,16},{24,24},{1,1},{17,9},{9,17},{25,25},{2,2},{18,... | collective-permute-start | bytes 3145736 | tf_op jit(solution)/shard_map/ppermute | solution.py:266
  747.2 47.5 %collective-permute-start.10 = (bf16[32,128,128]{2,1,0:T(8,128)(2,1)}, bf16[32,128,128]{2,1,0:T(8,128)(2,1)S(1)}, u32[]{:S(2)}, u32[]{:S(2)}) collective-permute-start(bf16[32,128,128]{2,1,0:T(8,128)(2,1)} %get-tuple-element.25), channel_id=1, source_target_pairs={{16,0},{0,8},{24,16},{8,24},{17,1},{1,9},{25,17},{9,25},{18,2},{2,... | collective-permute-start | bytes 3145736 | tf_op jit(solution)/shard_map/ppermute | solution.py:266
  766.4 70.6 %collective-permute-start.11 = (bf16[32,128,128]{2,1,0:T(8,128)(2,1)S(1)}, bf16[32,128,128]{2,1,0:T(8,128)(2,1)S(1)}, u32[]{:S(2)}, u32[]{:S(2)}) collective-permute-start(bf16[32,128,128]{2,1,0:T(8,128)(2,1)S(1)} %get-tuple-element.27), channel_id=1, source_target_pairs={{0,0},{16,8},{8,16},{24,24},{1,1},{17,9},{9,17},{25,25},{2,2},{18,... | collective-permute-start | bytes 3145736 | tf_op jit(solution)/shard_map/ppermute | solution.py:266
  776.5 60.7 %collective-permute-start.12 = (bf16[32,128,128]{2,1,0:T(8,128)(2,1)S(1)}, bf16[32,128,128]{2,1,0:T(8,128)(2,1)S(1)}, u32[]{:S(2)}, u32[]{:S(2)}) collective-permute-start(bf16[32,128,128]{2,1,0:T(8,128)(2,1)S(1)} %get-tuple-element.28), channel_id=1, source_target_pairs={{16,0},{0,8},{24,16},{8,24},{17,1},{1,9},{25,17},{9,25},{18,2},{2,... | collective-permute-start | bytes 3145736 | tf_op jit(solution)/shard_map/ppermute | solution.py:266
  (17 other events, 321.6 us)

commit v3 on v2

--- a/solution.py
+++ b/solution.py
@@ -133,26 +133,33 @@
 
     places = [(y, b) for y in range(halves) for b in range(halves)]
     at = {place: n for n, place in enumerate(places)}
-    goes = [
-        [(at[y, b], at[b, y]) for y, b in places],
-        [(at[y, b], at[1 - b, y]) for y, b in places],
-    ]
-    back = [[(d, s) for s, d in perm] for perm in goes]
-    half_of = [high, 1 - high]
-
-    def move_in(array, part):
-        return [
-            lax.ppermute(
-                lax.dynamic_slice_in_dim(array, half_of[w] * half_rows + part * rows, rows), SWAP, goes[w]
-            )
-            for w in range(2)
-        ]
-
-    pairs = [move_in(pair, part) for part in range(chunks)]
-    mask_float = lax.ppermute(token_mask.astype(F32), SWAP, goes[0])
-    gouts = [move_in(grad_out, part) for part in range(chunks)]
-
-    flip = jnp.stack([rep, 1 - rep]).astype(jnp.int32)
+    over_rep = [(at[y, b], at[1 - y, b]) for y, b in places]
+    over_high = [(at[y, b], at[y, 1 - b]) for y, b in places]
+    home = rep == high
+
+    def half_part(array, half, part):
+        return lax.dynamic_slice_in_dim(array, half * half_rows + part * rows, rows)
+
+    def swap_rep(array):
+        return lax.ppermute(array, SWAP, over_rep)
+
+    def swap_high(array):
+        return lax.ppermute(array, SWAP, over_high)
+
+    def first_hop(array, part):
+        return swap_rep(half_part(array, 1 - rep, part))
+
+    def second_hop(array, came, part):
+        mine = half_part(array, rep, part)
+        return jnp.where(home, mine, came), swap_high(jnp.where(home, came, mine))
+
+    def tie(*values):
+        return lax.optimization_barrier(values)
+
+    mask_float = token_mask.astype(F32)
+    mask_float = jnp.where(home, mask_float, swap_rep(mask_float))
+
+    flip = jnp.stack([high, 1 - high]).astype(jnp.int32)
     row_mask = lax.dynamic_slice_in_dim(
         mask_float, lax.axis_index(("row", "sub")) * full_rows + rep * half_rows, half_rows
     )
@@ -161,7 +168,7 @@
         col_mask = lax.dynamic_slice_in_dim(mask_float, (slot * low + lax.axis_index("low")) * cols, cols)
         return (row_mask[:, None] * col_mask[None, :]).reshape(half_rows // block, 1, block * cols)
 
-    masks = [pair_mask(rep), pair_mask(1 - rep)]
+    masks = [pair_mask(high), pair_mask(1 - high)]
     gain = ln_gain.reshape(1, chans)
     gain_col = out_gain.reshape(chans, 1)
     proj_t = jnp.swapaxes(proj_weights, 1, 2).reshape(4 * chans, chans)
@@ -240,17 +247,40 @@
     def batch_dot(a, b, ca, cb):
         return lax.dot_general(a, b, (((ca,), (cb,)), ((0,), (0,))), preferred_element_type=F32)
 
-    lefts, rights = [], []
-    for part in range(chunks):
-        left, right = project(part)
-        rights.append(by_channel(exchange(right)))
-        lefts.append(flat(by_channel(exchange(left))))
-    right = flat(jnp.concatenate(rights, axis=3))
+    pairs, gouts = [None] * chunks, [None] * chunks
+    came = first_hop(pair, 0)
+    later, came = tie(pair, came)
+    pairs[0] = second_hop(pair, came, 0)
+    came = first_hop(later, 1)
+    (*pairs[0], came) = tie(*pairs[0], came)
+    left_a, right_a = project(0)
+    right_a = exchange(right_a)
+    pairs[1] = second_hop(pair, came, 1)
+    (left_a, *pairs[1]) = tie(left_a, *pairs[1])
+    left_a = exchange(left_a)
+    later, right_a = tie(grad_out, right_a)
+    came = first_hop(later, 0)
+    left_b, right_b = project(1)
+    right_b, came = tie(right_b, came)
+    right_b = exchange(right_b)
+    gouts[0] = second_hop(grad_out, came, 0)
+    (left_b, *gouts[0]) = tie(left_b, *gouts[0])
+    left_b = exchange(left_b)
+    later, right_b = tie(later, right_b)
+    came = first_hop(later, 1)
+    right = flat(jnp.concatenate([by_channel(right_a), by_channel(right_b)], axis=3))
+    lefts = [flat(by_channel(left_a)), flat(by_channel(left_b))]
+    comb_a = by_owner(batch_dot(lefts[0], right, 2, 2))
+    comb_a, came = tie(comb_a, came)
+    comb_a = exchange(comb_a)
+    gouts[1] = second_hop(grad_out, came, 1)
+    comb_b = by_owner(batch_dot(lefts[1], right, 2, 2))
+    (comb_b, *gouts[1]) = tie(comb_b, *gouts[1])
+    combs = [comb_a, exchange(comb_b)]
 
     sigms, left_grads, grad_parts = [], [], []
     for part in range(chunks):
-        comb = exchange(by_owner(batch_dot(lefts[part], right, 2, 2)))
-        grad_comb, sigm = middle(comb, part)
+        grad_comb, sigm = middle(combs[part], part)
         sigms.append(sigm)
         grad_comb = flat(by_channel(exchange(grad_comb)))
         left_grads.append(exchange(by_owner(batch_dot(grad_comb, right, 2, 1))))
@@ -261,10 +291,12 @@
     out = jnp.zeros((full_rows, cols, chans), BF16)
     for part in range(chunks):
         right_grad = exchange(by_owner(grad_right[:, :, :, part]))
-        results = last(left_grads[part], right_grad, sigms[part], part)
-        for w in range(2):
-            home = lax.ppermute(results[w], SWAP, back[w])
-            out = lax.dynamic_update_slice_in_dim(out, home, half_of[w] * half_rows + part * rows, 0)
+        kept, goes = last(left_grads[part], right_grad, sigms[part], part)
+        came = swap_high(goes)
+        stays, goes = jnp.where(home, kept, came), jnp.where(home, came, kept)
+        came = swap_rep(goes)
+        out = lax.dynamic_update_slice_in_dim(out, stays, rep * half_rows + part * rows, 0)
+        out = lax.dynamic_update_slice_in_dim(out, came, (1 - rep) * half_rows + part * rows, 0)
     return out
 
 

time: 854 us -> 783 us (0.917)
  waiting for transfers between devices: 438 us -> 369 us
  starting transfers between devices: 120 us -> 89.3 us
  other arithmetic: 3.01 us -> 14.7 us
    ppermute x13, waiting for transfers between devices: 405 us -> 260 us  [the longest x6 173 us: swap_high(): return lax.ppermute(array, SWAP, over_high)]
    all_to_all x10, waiting for transfers between devices: 33.3 us -> 109 us  [exchange(): return lax.all_to_all(array, GROUP, split_axis=0, concat_axis=0, tiled=True)]
    ppermute x13, starting transfers between devices: 44.2 us -> 12.6 us  [the longest x6 8.85 us: swap_high(): return lax.ppermute(array, SWAP, over_high)]
    select_n x0 -> x6, other arithmetic: none -> 11.7 us  [the longest x3 8.36 us: second_hop(): return (jnp.where(home, mine, came), swap_high(jnp.where(home, came, mine)))]
  transfers between devices with their start and end apart: 23 -> 23, of which waited for: 14 -> 18; matrix products, arithmetic and copies ran while one was open for 17% -> 20% of each run, Pallas kernels for 7% -> 8%
where the time goes in v3:
time: 783 us; the launch traced here: 771 us
  waiting for transfers between devices  369 us (47%)
  local copies, waits for them, and re-layouts  134 us (17%)
  starting transfers between devices  89.3 us (11%)
  blocking collectives  66.4 us (8%)
  Pallas kernels  65.9 us (8%)
  matrix products  31.7 us (4%)
  other arithmetic  14.7 us (2%)
    ppermute x6, waiting for transfers between devices, swap_high(): return lax.ppermute(array, SWAP, over_high)  173 us
    all_to_all x10, waiting for transfers between devices, exchange(): return lax.all_to_all(array, GROUP, split_axis=0, concat_axis=0, tiled=True)  109 us
    ppermute x7, waiting for transfers between devices, swap_rep(): return lax.ppermute(array, SWAP, over_rep)  87.2 us
    all_to_all x10, starting transfers between devices, exchange(): return lax.all_to_all(array, GROUP, split_axis=0, concat_axis=0, tiled=True)  76.7 us
    all_to_all x2, blocking collectives, exchange(): return lax.all_to_all(array, GROUP, split_axis=0, concat_axis=0, tiled=True)  66.4 us
    pallas_call x6, Pallas kernels, call(): pl.pallas_call(functools.partial(kernel, step), grid_spec=pltpu.PrefetchS...  65.9 us
    reshape x8, local copies, waits for them, and re-layouts, by_owner(): array.astype(BF16).reshape(own, row_blocks, halves, rows, halves, low, cols)  33.5 us
    dot_general x6, matrix products, batch_dot(): lax.dot_general(a, b, (((ca,), (cb,)), ((0,), (0,))), preferred_element_t...  31.7 us
  transfers between devices with their start and end apart: 23, of which 18 were waited for; matrix products, arithmetic and copies ran while one was open for 20% of the time, Pallas kernels for 8%

profile of v3, /device:TPU:15, one launch (start us, length us, event | category | flops | bytes accessed | tf_op | source)
XLA Modules:
  0.0 771.3 jit_solution(4627305111335985615)
XLA Ops:
  1.6 23.8 %collective-permute-done = bf16[32,128,128]{2,1,0:T(8,128)(2,1)S(1)} collective-permute-done((bf16[32,128,128]{2,1,0:T(8,128)(2,1)S(1)}, bf16[32,128,128]{2,1,0:T(8,128)(2,1)S(1)}, u32[]{:S(2)}, u32[]{:S(2)}) %collective-permute-start) | collective-permute-done | bytes 1048608 | tf_op jit(solution)/shard_map/ppermute | solution.py:144
  34.1 21.4 %collective-permute-done.3 = f32[512]{0:T(512)S(1)} collective-permute-done((f32[512]{0:T(512)S(1)}, f32[512]{0:T(512)S(1)}, u32[]{:S(2)}, u32[]{:S(2)}) %collective-permute-start.3) | collective-permute-done | bytes 2080 | tf_op jit(solution)/shard_map/ppermute | solution.py:144
  55.9 19.8 %collective-permute-done.1.pair_b = bf16[32,128,128]{2,1,0:T(8,128)(2,1)S(1)} collective-permute-done((bf16[32,128,128]{2,1,0:T(8,128)(2,1)}, bf16[32,128,128]{2,1,0:T(8,128)(2,1)S(1)}, u32[]{:S(2)}, u32[]{:S(2)}) %collective-permute-start.1) | collective-permute-done | bytes 1048608 | tf_op jit(solution)/shard_map/ppermute | solution.py:147
  94.8 41.7 %all-to-all-done = bf16[16,2,32,8,128]{4,3,2,1,0:T(8,128)(2,1)} async-done(((bf16[16,2,32,8,128]{4,3,2,1,0:T(8,128)(2,1)}), bf16[16,2,32,8,128]{4,3,2,1,0:T(8,128)(2,1)}, u32[]{:S(2)}, u32[]{:S(2)}) %all-to-all-start) | async-done | bytes 2097184 | tf_op jit(solution)/shard_map/all_to_all | solution.py:234
  148.8 13.0 %collective-permute-done.5 = bf16[32,128,128]{2,1,0:T(8,128)(2,1)} collective-permute-done((bf16[32,128,128]{2,1,0:T(8,128)(2,1)S(1)}, bf16[32,128,128]{2,1,0:T(8,128)(2,1)}, u32[]{:S(2)}, u32[]{:S(2)}) %collective-permute-start.5) | collective-permute-done | bytes 1048608 | tf_op jit(solution)/shard_map/ppermute | solution.py:144
  161.9 33.9 %all_to_all.60 = bf16[16,2,32,8,128]{4,3,2,1,0:T(8,128)(2,1)} all-to-all(bf16[16,2,32,8,128]{4,3,2,1,0:T(8,128)(2,1)} %get-tuple-element.56), channel_id=1, replica_groups=mesh['rep'=2,'high'=2,'low'=2,'row'=2,'sub'=2] {'rep','low','row','sub'}, dimensions={0} | all-to-all | bytes 4194304 | tf_op jit(solution)/shard_map/all_to_all | solution.py:234
  215.8 13.5 %all-to-all-done.1 = bf16[16,2,32,8,128]{4,3,2,1,0:T(8,128)(2,1)} async-done(((bf16[16,2,32,8,128]{4,3,2,1,0:T(8,128)(2,1)}), bf16[16,2,32,8,128]{4,3,2,1,0:T(8,128)(2,1)}, u32[]{:S(2)}, u32[]{:S(2)}) %all-to-all-start.1) | async-done | bytes 2097184 | tf_op jit(solution)/shard_map/all_to_all | solution.py:234
  268.3 45.0 %collective-permute-done.6.gout_b = bf16[32,128,128]{2,1,0:T(8,128)(2,1)S(1)} collective-permute-done((bf16[32,128,128]{2,1,0:T(8,128)(2,1)S(1)}, bf16[32,128,128]{2,1,0:T(8,128)(2,1)S(1)}, u32[]{:S(2)}, u32[]{:S(2)}) %collective-permute-start.6) | collective-permute-done | bytes 1048608 | tf_op jit(solution)/shard_map/ppermute | solution.py:147
  314.3 32.5 %all_to_all.61 = bf16[16,2,32,8,128]{4,3,2,1,0:T(8,128)(2,1)} all-to-all(bf16[16,2,32,8,128]{4,3,2,1,0:T(8,128)(2,1)S(1)} %copy-done.3), channel_id=1, replica_groups=mesh['rep'=2,'high'=2,'low'=2,'row'=2,'sub'=2] {'rep','low','row','sub'}, dimensions={0} | all-to-all | bytes 4194304 | tf_op jit(solution)/shard_map/all_to_all | solution.py:234
  346.9 8.4 %all-to-all-start.3 = ((bf16[16,2,32,8,128]{4,3,2,1,0:T(8,128)(2,1)}), bf16[16,2,32,8,128]{4,3,2,1,0:T(8,128)(2,1)}, u32[]{:S(2)}, u32[]{:S(2)}) async-start(bf16[16,2,32,8,128]{4,3,2,1,0:T(8,128)(2,1)} %bitcast.95), calls=%async_computation.3 | async-start | bytes 4194304 | tf_op jit(solution)/shard_map/all_to_all | solution.py:234
  378.2 24.8 %collective-permute-done.8.gout_b = bf16[32,128,128]{2,1,0:T(8,128)(2,1)} collective-permute-done((bf16[32,128,128]{2,1,0:T(8,128)(2,1)}, bf16[32,128,128]{2,1,0:T(8,128)(2,1)}, u32[]{:S(2)}, u32[]{:S(2)}) %collective-permute-start.8) | collective-permute-done | bytes 1048608 | tf_op jit(solution)/shard_map/ppermute | solution.py:147
  413.8 11.2 %shard_map.84 = (bf16[16,2,32,8,128]{4,3,2,1,0:T(8,128)(2,1)}, bf16[2,32,128,128]{3,2,1,0:T(8,128)(2,1)}) custom-call(s32[2]{0:T(128)S(1)} %pad_add_fusion.flip_ref, bf16[32,128,128]{2,1,0:T(8,128)(2,1)S(1)} %get-tuple-element.41.pair_a, bf16[32,128,128]{2,1,0:T(8,128)(2,1)S(1)} %copy-done.5, bf16[32,128,128]{2,1,0:T(8,128)(2,1)S(1)} %copy-done, ...), custom_call_target="tpu_custom_call" | custom-call | flops 1073741824 | bytes 10485760 | tf_op jit(solution)/shard_map/pallas_call | solution.py:195
  425.0 10.0 %all-to-all-done.7.comb_ref = bf16[16,2,32,8,128]{4,3,2,1,0:T(8,128)(2,1)} async-done(((bf16[16,2,32,8,128]{4,3,2,1,0:T(8,128)(2,1)}), bf16[16,2,32,8,128]{4,3,2,1,0:T(8,128)(2,1)}, u32[]{:S(2)}, u32[]{:S(2)}) %all-to-all-start.7) | async-done | bytes 2097184 | tf_op jit(solution)/shard_map/all_to_all | solution.py:234
  444.7 11.5 %shard_map.85 = (bf16[16,2,32,8,128]{4,3,2,1,0:T(8,128)(2,1)}, bf16[2,32,128,128]{3,2,1,0:T(8,128)(2,1)}) custom-call(s32[2]{0:T(128)S(1)} %pad_add_fusion.flip_ref, bf16[32,128,128]{2,1,0:T(8,128)(2,1)S(1)} %get-tuple-element.45.pair_a, bf16[32,128,128]{2,1,0:T(8,128)(2,1)S(1)} %copy-done.8, bf16[32,128,128]{2,1,0:T(8,128)(2,1)S(1)} %get-tuple-element.63.gout_a, ...), custom_call_target="tpu_custom_call" | custom-call | flops 1073741824 | bytes 10485760 | tf_op jit(solution)/shard_map/pallas_call | solution.py:195
  456.2 12.6 %all-to-all-done.4 = bf16[16,2,32,8,128]{4,3,2,1,0:T(8,128)(2,1)} async-done(((bf16[16,2,32,8,128]{4,3,2,1,0:T(8,128)(2,1)}), bf16[16,2,32,8,128]{4,3,2,1,0:T(8,128)(2,1)}, u32[]{:S(2)}, u32[]{:S(2)}) %all-to-all-start.4) | async-done | bytes 2097184 | tf_op jit(solution)/shard_map/all_to_all | solution.py:234
  502.5 8.7 %all-to-all-start.5 = ((bf16[16,2,32,8,128]{4,3,2,1,0:T(8,128)(2,1)}), bf16[16,2,32,8,128]{4,3,2,1,0:T(8,128)(2,1)}, u32[]{:S(2)}, u32[]{:S(2)}) async-start(bf16[16,2,32,8,128]{4,3,2,1,0:T(8,128)(2,1)} %bitcast.97), calls=%async_computation.5 | async-start | bytes 4194304 | tf_op jit(solution)/shard_map/all_to_all | solution.py:234
  557.4 17.2 %all-to-all-done.9.right_ref = bf16[16,2,32,8,128]{4,3,2,1,0:T(8,128)(2,1)} async-done(((bf16[16,2,32,8,128]{4,3,2,1,0:T(8,128)(2,1)}), bf16[16,2,32,8,128]{4,3,2,1,0:T(8,128)(2,1)}, u32[]{:S(2)}, u32[]{:S(2)}) %all-to-all-start.9) | async-done | bytes 2097184 | tf_op jit(solution)/shard_map/all_to_all | solution.py:234
  596.6 11.6 %all-to-all-done.11.right_ref = bf16[16,2,32,8,128]{4,3,2,1,0:T(8,128)(2,1)} async-done(((bf16[16,2,32,8,128]{4,3,2,1,0:T(8,128)(2,1)}), bf16[16,2,32,8,128]{4,3,2,1,0:T(8,128)(2,1)}, u32[]{:S(2)}, u32[]{:S(2)}) %all-to-all-start.11) | async-done | bytes 2097184 | tf_op jit(solution)/shard_map/all_to_all | solution.py:234
  608.2 8.9 %all-to-all-start.10 = ((bf16[16,2,32,8,128]{4,3,2,1,0:T(8,128)(2,1)}), bf16[16,2,32,8,128]{4,3,2,1,0:T(8,128)(2,1)}, u32[]{:S(2)}, u32[]{:S(2)}) async-start(bf16[16,2,32,8,128]{4,3,2,1,0:T(8,128)(2,1)} %bitcast.96), calls=%async_computation.10 | async-start | bytes 4194304 | tf_op jit(solution)/shard_map/all_to_all | solution.py:234
  617.2 14.4 %shard_map.86 = (bf16[32,128,128]{2,1,0:T(8,128)(2,1)S(1)}, bf16[32,128,128]{2,1,0:T(8,128)(2,1)S(1)}) custom-call(s32[2]{0:T(128)S(1)} %pad_add_fusion.flip_ref, bf16[32,128,128]{2,1,0:T(8,128)(2,1)S(1)} %get-tuple-element.41.pair_a, bf16[32,128,128]{2,1,0:T(8,128)(2,1)S(1)} %copy-done.6, bf16[16,2,32,8,128]{4,3,2,1,0:T(8,128)(2,1)} %all-to-all-done.5.left_ref, ...), custom_call_target="tpu_custom_call" | custom-call | flops 2415919104 | bytes 10485760 | tf_op jit(solution)/shard_map/pallas_call | solution.py:195
  632.2 44.7 %collective-permute-done.9 = bf16[32,128,128]{2,1,0:T(8,128)(2,1)S(1)} collective-permute-done((bf16[32,128,128]{2,1,0:T(8,128)(2,1)S(1)}, bf16[32,128,128]{2,1,0:T(8,128)(2,1)S(1)}, u32[]{:S(2)}, u32[]{:S(2)}) %collective-permute-start.9) | collective-permute-done | bytes 1048608 | tf_op jit(solution)/shard_map/ppermute | solution.py:147
  682.1 14.4 %shard_map.87 = (bf16[32,128,128]{2,1,0:T(8,128)(2,1)S(1)}, bf16[32,128,128]{2,1,0:T(8,128)(2,1)S(1)}) custom-call(s32[2]{0:T(128)S(1)} %pad_add_fusion.flip_ref, bf16[32,128,128]{2,1,0:T(8,128)(2,1)S(1)} %get-tuple-element.45.pair_a, bf16[32,128,128]{2,1,0:T(8,128)(2,1)S(1)} %copy-done.9, bf16[16,2,32,8,128]{4,3,2,1,0:T(8,128)(2,1)} %all-to-all-done.10.left_ref, ...), custom_call_target="tpu_custom_call" | custom-call | flops 2415919104 | bytes 10485760 | tf_op jit(solution)/shard_map/pallas_call | solution.py:195
  707.9 36.4 %collective-permute-done.11 = bf16[32,128,128]{2,1,0:T(8,128)(2,1)S(1)} collective-permute-done((bf16[32,128,128]{2,1,0:T(8,128)(2,1)S(1)}, bf16[32,128,128]{2,1,0:T(8,128)(2,1)S(1)}, u32[]{:S(2)}, u32[]{:S(2)}) %collective-permute-start.11) | collective-permute-done | bytes 1048608 | tf_op jit(solution)/shard_map/ppermute | solution.py:147
  747.0 23.0 %collective-permute-done.12 = bf16[32,128,128]{2,1,0:T(8,128)(2,1)S(1)} collective-permute-done((bf16[32,128,128]{2,1,0:T(8,128)(2,1)S(1)}, bf16[32,128,128]{2,1,0:T(8,128)(2,1)S(1)}, u32[]{:S(2)}, u32[]{:S(2)}) %collective-permute-start.12) | collective-permute-done | bytes 1048608 | tf_op jit(solution)/shard_map/ppermute | solution.py:144
  (143 shorter events, 268.3 us)
Async XLA Ops:
  1.3 24.1 %collective-permute-start = (bf16[32,128,128]{2,1,0:T(8,128)(2,1)S(1)}, bf16[32,128,128]{2,1,0:T(8,128)(2,1)S(1)}, u32[]{:S(2)}, u32[]{:S(2)}) collective-permute-start(bf16[32,128,128]{2,1,0:T(8,128)(2,1)S(1)} %constant_dynamic-slice_fusion.3), channel_id=1, source_target_pairs={{0,16},{8,24},{16,0},{24,8},{1,17},{9,25},{17,1},{25,9},{2,18},{10... | collective-permute-start | bytes 3145736 | tf_op jit(solution)/shard_map/ppermute | solution.py:144
  27.8 47.9 %collective-permute-start.1 = (bf16[32,128,128]{2,1,0:T(8,128)(2,1)}, bf16[32,128,128]{2,1,0:T(8,128)(2,1)S(1)}, u32[]{:S(2)}, u32[]{:S(2)}) collective-permute-start(bf16[32,128,128]{2,1,0:T(8,128)(2,1)} %get-tuple-element.79), channel_id=1, source_target_pairs={{0,8},{8,0},{16,24},{24,16},{1,9},{9,1},{17,25},{25,17},{2,10},{10... | collective-permute-start | bytes 3145736 | tf_op jit(solution)/shard_map/ppermute | solution.py:147
  32.4 43.3 %collective-permute-start.2 = (bf16[32,128,128]{2,1,0:T(8,128)(2,1)}, bf16[32,128,128]{2,1,0:T(8,128)(2,1)S(1)}, u32[]{:S(2)}, u32[]{:S(2)}) collective-permute-start(bf16[32,128,128]{2,1,0:T(8,128)(2,1)} %constant_dynamic-slice_fusion.2), channel_id=1, source_target_pairs={{0,16},{8,24},{16,0},{24,8},{1,17},{9,25},{17,1},{25,9},{2,18},{10... | collective-permute-start | bytes 3145736 | tf_op jit(solution)/shard_map/ppermute | solution.py:144
  32.6 22.8 %collective-permute-start.3 = (f32[512]{0:T(512)S(1)}, f32[512]{0:T(512)S(1)}, u32[]{:S(2)}, u32[]{:S(2)}) collective-permute-start(f32[512]{0:T(512)S(1)} %convert_element_type.23), channel_id=1, source_target_pairs={{0,16},{8,24},{16,0},{24,8},{1,17},{9,25},{17,1},{25,9},{2,18},{10... | collective-permute-start | bytes 6152 | tf_op jit(solution)/shard_map/ppermute | solution.py:144
  55.9 84.4 %copy-start.13 = (f32[16,1,512]{2,1,0:T(1,128)}, f32[16,1,512]{2,1,0:T(1,128)S(1)}, u32[]{:S(2)}) copy-start(f32[16,1,512]{2,1,0:T(1,128)S(1)} %get-tuple-element.89.mask_b) | copy-start | bytes 98308
  84.2 52.4 %all-to-all-start = ((bf16[16,2,32,8,128]{4,3,2,1,0:T(8,128)(2,1)}), bf16[16,2,32,8,128]{4,3,2,1,0:T(8,128)(2,1)}, u32[]{:S(2)}, u32[]{:S(2)}) async-start(bf16[16,2,32,8,128]{4,3,2,1,0:T(8,128)(2,1)} %get-tuple-element.49), calls=%async_computation | async-start | bytes 4194304 | tf_op jit(solution)/shard_map/all_to_all | solution.py:234
  92.2 48.1 %collective-permute-start.4 = (bf16[32,128,128]{2,1,0:T(8,128)(2,1)}, bf16[32,128,128]{2,1,0:T(8,128)(2,1)S(1)}, u32[]{:S(2)}, u32[]{:S(2)}) collective-permute-start(bf16[32,128,128]{2,1,0:T(8,128)(2,1)} %get-tuple-element.77), channel_id=1, source_target_pairs={{0,8},{8,0},{16,24},{24,16},{1,9},{9,1},{17,25},{25,17},{2,10},{10... | collective-permute-start | bytes 3145736 | tf_op jit(solution)/shard_map/ppermute | solution.py:147
  137.9 24.0 %collective-permute-start.5 = (bf16[32,128,128]{2,1,0:T(8,128)(2,1)S(1)}, bf16[32,128,128]{2,1,0:T(8,128)(2,1)}, u32[]{:S(2)}, u32[]{:S(2)}) collective-permute-start(bf16[32,128,128]{2,1,0:T(8,128)(2,1)S(1)} %constant_dynamic-slice_fusion.1), channel_id=1, source_target_pairs={{0,16},{8,24},{16,0},{24,8},{1,17},{9,25},{17,1},{25,9},{2,18},{10... | collective-permute-start | bytes 3145736 | tf_op jit(solution)/shard_map/ppermute | solution.py:144
  195.7 33.5 %all-to-all-start.1 = ((bf16[16,2,32,8,128]{4,3,2,1,0:T(8,128)(2,1)}), bf16[16,2,32,8,128]{4,3,2,1,0:T(8,128)(2,1)}, u32[]{:S(2)}, u32[]{:S(2)}) async-start(bf16[16,2,32,8,128]{4,3,2,1,0:T(8,128)(2,1)} %copy-done.1), calls=%async_computation.1 | async-start | bytes 4194304 | tf_op jit(solution)/shard_map/all_to_all | solution.py:234
  206.3 57.5 %collective-permute-start.7 = (bf16[32,128,128]{2,1,0:T(8,128)(2,1)}, bf16[32,128,128]{2,1,0:T(8,128)(2,1)S(1)}, u32[]{:S(2)}, u32[]{:S(2)}) collective-permute-start(bf16[32,128,128]{2,1,0:T(8,128)(2,1)} %constant_dynamic-slice_fusion), channel_id=1, source_target_pairs={{0,16},{8,24},{16,0},{24,8},{1,17},{9,25},{17,1},{25,9},{2,18},{10... | collective-permute-start | bytes 3145736 | tf_op jit(solution)/shard_map/ppermute | solution.py:144
  268.3 45.0 %collective-permute-start.6 = (bf16[32,128,128]{2,1,0:T(8,128)(2,1)S(1)}, bf16[32,128,128]{2,1,0:T(8,128)(2,1)S(1)}, u32[]{:S(2)}, u32[]{:S(2)}) collective-permute-start(bf16[32,128,128]{2,1,0:T(8,128)(2,1)S(1)} %get-tuple-element.84), channel_id=1, source_target_pairs={{0,8},{8,0},{16,24},{24,16},{1,9},{9,1},{17,25},{25,17},{2,10},{10... | collective-permute-start | bytes 3145736 | tf_op jit(solution)/shard_map/ppermute | solution.py:147
  346.9 56.2 %all-to-all-start.3 = ((bf16[16,2,32,8,128]{4,3,2,1,0:T(8,128)(2,1)}), bf16[16,2,32,8,128]{4,3,2,1,0:T(8,128)(2,1)}, u32[]{:S(2)}, u32[]{:S(2)}) async-start(bf16[16,2,32,8,128]{4,3,2,1,0:T(8,128)(2,1)} %bitcast.95), calls=%async_computation.3 | async-start | bytes 4194304 | tf_op jit(solution)/shard_map/all_to_all | solution.py:234
  355.3 47.8 %collective-permute-start.8 = (bf16[32,128,128]{2,1,0:T(8,128)(2,1)}, bf16[32,128,128]{2,1,0:T(8,128)(2,1)}, u32[]{:S(2)}, u32[]{:S(2)}) collective-permute-start(bf16[32,128,128]{2,1,0:T(8,128)(2,1)} %get-tuple-element.73), channel_id=1, source_target_pairs={{0,8},{8,0},{16,24},{24,16},{1,9},{9,1},{17,25},{25,17},{2,10},{10... | collective-permute-start | bytes 3145736 | tf_op jit(solution)/shard_map/ppermute | solution.py:147
  403.1 32.0 %all-to-all-start.7 = ((bf16[16,2,32,8,128]{4,3,2,1,0:T(8,128)(2,1)}), bf16[16,2,32,8,128]{4,3,2,1,0:T(8,128)(2,1)}, u32[]{:S(2)}, u32[]{:S(2)}) async-start(bf16[16,2,32,8,128]{4,3,2,1,0:T(8,128)(2,1)} %bitcast.98), calls=%async_computation.7 | async-start | bytes 4194304 | tf_op jit(solution)/shard_map/all_to_all | solution.py:234
  435.0 33.8 %all-to-all-start.4 = ((bf16[16,2,32,8,128]{4,3,2,1,0:T(8,128)(2,1)}), bf16[16,2,32,8,128]{4,3,2,1,0:T(8,128)(2,1)}, u32[]{:S(2)}, u32[]{:S(2)}) async-start(bf16[16,2,32,8,128]{4,3,2,1,0:T(8,128)(2,1)} %get-tuple-element.60), calls=%async_computation.4 | async-start | bytes 4194304 | tf_op jit(solution)/shard_map/all_to_all | solution.py:234
  468.8 33.7 %all-to-all-start.8 = ((bf16[16,2,32,8,128]{4,3,2,1,0:T(8,128)(2,1)}), bf16[16,2,32,8,128]{4,3,2,1,0:T(8,128)(2,1)}, u32[]{:S(2)}, u32[]{:S(2)}) async-start(bf16[16,2,32,8,128]{4,3,2,1,0:T(8,128)(2,1)} %get-tuple-element.66), calls=%async_computation.8 | async-start | bytes 4194304 | tf_op jit(solution)/shard_map/all_to_all | solution.py:234
  502.5 41.4 %all-to-all-start.5 = ((bf16[16,2,32,8,128]{4,3,2,1,0:T(8,128)(2,1)}), bf16[16,2,32,8,128]{4,3,2,1,0:T(8,128)(2,1)}, u32[]{:S(2)}, u32[]{:S(2)}) async-start(bf16[16,2,32,8,128]{4,3,2,1,0:T(8,128)(2,1)} %bitcast.97), calls=%async_computation.5 | async-start | bytes 4194304 | tf_op jit(solution)/shard_map/all_to_all | solution.py:234
  544.0 30.6 %all-to-all-start.9 = ((bf16[16,2,32,8,128]{4,3,2,1,0:T(8,128)(2,1)}), bf16[16,2,32,8,128]{4,3,2,1,0:T(8,128)(2,1)}, u32[]{:S(2)}, u32[]{:S(2)}) async-start(bf16[16,2,32,8,128]{4,3,2,1,0:T(8,128)(2,1)} %bitcast.101), calls=%async_computation.9 | async-start | bytes 4194304 | tf_op jit(solution)/shard_map/all_to_all | solution.py:234
  574.6 33.6 %all-to-all-start.11 = ((bf16[16,2,32,8,128]{4,3,2,1,0:T(8,128)(2,1)}), bf16[16,2,32,8,128]{4,3,2,1,0:T(8,128)(2,1)}, u32[]{:S(2)}, u32[]{:S(2)}) async-start(bf16[16,2,32,8,128]{4,3,2,1,0:T(8,128)(2,1)} %bitcast.100), calls=%async_computation.11 | async-start | bytes 4194304 | tf_op jit(solution)/shard_map/all_to_all | solution.py:234
  608.2 73.9 %all-to-all-start.10 = ((bf16[16,2,32,8,128]{4,3,2,1,0:T(8,128)(2,1)}), bf16[16,2,32,8,128]{4,3,2,1,0:T(8,128)(2,1)}, u32[]{:S(2)}, u32[]{:S(2)}) async-start(bf16[16,2,32,8,128]{4,3,2,1,0:T(8,128)(2,1)} %bitcast.96), calls=%async_computation.10 | async-start | bytes 4194304 | tf_op jit(solution)/shard_map/all_to_all | solution.py:234
  631.5 45.4 %collective-permute-start.9 = (bf16[32,128,128]{2,1,0:T(8,128)(2,1)S(1)}, bf16[32,128,128]{2,1,0:T(8,128)(2,1)S(1)}, u32[]{:S(2)}, u32[]{:S(2)}) collective-permute-start(bf16[32,128,128]{2,1,0:T(8,128)(2,1)S(1)} %get-tuple-element.69), channel_id=1, source_target_pairs={{0,8},{8,0},{16,24},{24,16},{1,9},{9,1},{17,25},{25,17},{2,10},{10... | collective-permute-start | bytes 3145736 | tf_op jit(solution)/shard_map/ppermute | solution.py:147
  681.8 23.8 %collective-permute-start.10 = (bf16[32,128,128]{2,1,0:T(8,128)(2,1)}, bf16[32,128,128]{2,1,0:T(8,128)(2,1)}, u32[]{:S(2)}, u32[]{:S(2)}) collective-permute-start(bf16[32,128,128]{2,1,0:T(8,128)(2,1)} %get-tuple-element.87), channel_id=1, source_target_pairs={{0,16},{8,24},{16,0},{24,8},{1,17},{9,25},{17,1},{25,9},{2,18},{10... | collective-permute-start | bytes 3145736 | tf_op jit(solution)/shard_map/ppermute | solution.py:144
  696.4 47.9 %collective-permute-start.11 = (bf16[32,128,128]{2,1,0:T(8,128)(2,1)S(1)}, bf16[32,128,128]{2,1,0:T(8,128)(2,1)S(1)}, u32[]{:S(2)}, u32[]{:S(2)}) collective-permute-start(bf16[32,128,128]{2,1,0:T(8,128)(2,1)S(1)} %get-tuple-element.72), channel_id=1, source_target_pairs={{0,8},{8,0},{16,24},{24,16},{1,9},{9,1},{17,25},{25,17},{2,10},{10... | collective-permute-start | bytes 3145736 | tf_op jit(solution)/shard_map/ppermute | solution.py:147
  745.8 24.2 %collective-permute-start.12 = (bf16[32,128,128]{2,1,0:T(8,128)(2,1)S(1)}, bf16[32,128,128]{2,1,0:T(8,128)(2,1)S(1)}, u32[]{:S(2)}, u32[]{:S(2)}) collective-permute-start(bf16[32,128,128]{2,1,0:T(8,128)(2,1)S(1)} %get-tuple-element.85), channel_id=1, source_target_pairs={{0,16},{8,24},{16,0},{24,8},{1,17},{9,25},{17,1},{25,9},{2,18},{10... | collective-permute-start | bytes 3145736 | tf_op jit(solution)/shard_map/ppermute | solution.py:144
  (26 other events, 332.1 us)

commit v4 on v1

--- a/solution.py
+++ b/solution.py
@@ -47,7 +47,7 @@
     rows, cols, chans = pair_ref.shape
     for first in range(0, rows, step):
         _, _, normed = norm_rows(rows_of(pair_ref, first, step), gain_ref[...])
-        both = dot(weight_ref[...], normed, 1, 1)
+        both = dot(weight_ref[0], normed, 1, 1)
         mask = mask_ref[0, :, first * cols:(first + step) * cols]
         store_chan(out_ref, first, step, mask * jax.nn.sigmoid(both[chans:]) * both[:chans])
 
@@ -123,10 +123,9 @@
     mask = (row_mask[:, None] * col_mask[None, :]).reshape(rows // block, 1, block * cols)
     gain = ln_gain.reshape(1, chans)
     proj_t = jnp.swapaxes(proj_weights, 1, 2)
-    left_w = proj_t[:2].reshape(2 * chans, chans)
-    right_w = proj_t[2:].reshape(2 * chans, chans)
+    sides = proj_t.reshape(2, 2 * chans, chans)
     gate_t = gate_weight.T
-    all_w = jnp.concatenate([left_w, right_w, gate_t], axis=0)
+    all_w = jnp.concatenate([proj_t.reshape(4 * chans, chans), gate_t], axis=0)
     eye = jnp.eye(chans, dtype=BF16)
 
     params = pltpu.CompilerParams(vmem_limit_bytes=VMEM_LIMIT)
@@ -148,16 +147,24 @@
     chan_spec = pl.BlockSpec((peers, block, own, cols), lambda s: (0, s, 0, 0))
     sigm_spec = pl.BlockSpec((block, chans, cols), lambda s: (s, 0, 0))
 
-    def project(weight, first, count):
+    def project(rights, first, count):
+        def place(s):
+            return jnp.where(s < rights, s, s - rights + first)
+
         return pl.pallas_call(
             functools.partial(project_kernel, step),
-            grid=(count,),
-            in_specs=[row_spec(first), mask_spec(first), whole(gain), whole(weight)],
+            grid=(rights + count,),
+            in_specs=[
+                pl.BlockSpec((block, cols, chans), lambda s: (place(s), 0, 0)),
+                pl.BlockSpec((1, 1, block * cols), lambda s: (place(s), 0, 0)),
+                whole(gain),
+                pl.BlockSpec((1, 2 * chans, chans), lambda s: (jnp.where(s < rights, 1, 0), 0, 0)),
+            ],
             out_specs=chan_spec,
-            out_shape=jax.ShapeDtypeStruct((peers, count * block, own, cols), BF16),
+            out_shape=jax.ShapeDtypeStruct((peers, (rights + count) * block, own, cols), BF16),
             compiler_params=params,
-            cost_estimate=cost(4 * chans * chans, 2, count * block * cols),
-        )(pair, mask, gain, weight)
+            cost_estimate=cost(4 * chans * chans, 2, (rights + count) * block * cols),
+        )(pair, mask, gain, sides)
 
     def exchange(array):
         return lax.all_to_all(array, group, split_axis=0, concat_axis=0, tiled=True)
@@ -192,11 +199,15 @@
             cost_estimate=cost(8 * chans * chans, 5, part_rows * cols),
         )(pair, grad_out, comb, gain, gate_t, out_weight, out_t, gain_col, eye)
 
+    def chan_from(first):
+        return pl.BlockSpec((peers, block, own, cols), lambda s: (0, first + s, 0, 0))
+
     def last(left_grad, right_grad, sigm, first, held):
+        (left_grad, left_at), (right_grad, right_at) = left_grad, right_grad
         return pl.pallas_call(
             functools.partial(last_kernel, step),
             grid=(blocks,),
-            in_specs=[row_spec(first), chan_spec, chan_spec, sigm_spec, mask_spec(first), whole(gain), whole(all_w),
+            in_specs=[row_spec(first), chan_from(left_at), chan_from(right_at), sigm_spec, mask_spec(first), whole(gain), whole(all_w),
                       pl.BlockSpec(memory_space=pl.ANY)],
             out_specs=row_spec(first),
             out_shape=jax.ShapeDtypeStruct((rows, cols, chans), BF16),
@@ -205,21 +216,27 @@
             cost_estimate=cost(18 * chans * chans, 5, part_rows * cols),
         )(pair, left_grad, right_grad, sigm, mask, gain, all_w, held)
 
-    right = by_channel(exchange(project(right_w, 0, rows // block)))
     firsts = [part * blocks for part in range(chunks)]
-    lefts = [by_channel(exchange(project(left_w, first, blocks))) for first in firsts]
+    both = exchange(project(rows // block, 0, blocks))
+    right = by_channel(both[:, :rows])
+    lefts = [by_channel(both[:, rows:])]
+    lefts += [by_channel(exchange(project(0, first, blocks))) for first in firsts[1:]]
     sigms, left_grads, grad_parts = [], [], []
     for first, left in zip(firsts, lefts):
         comb = exchange(by_owner(batch_dot(left, right, 2, 2)))
         grad_comb, sigm = middle(comb, first)
         sigms.append(sigm)
         grad_comb = by_channel(exchange(grad_comb))
-        left_grads.append(exchange(by_owner(batch_dot(grad_comb, right, 2, 1))))
+        left_grads.append(by_owner(batch_dot(grad_comb, right, 2, 1)))
         grad_parts.append(batch_dot(grad_comb, left, 1, 1))
     grad_right = by_owner(functools.reduce(jnp.add, grad_parts))
-    right_grads = [exchange(grad_right[:, p * part_rows:(p + 1) * part_rows]) for p in range(chunks)]
+    right_grads = [grad_right[:, p * part_rows:(p + 1) * part_rows] for p in range(chunks)]
+    left_sent = [(exchange(array), 0) for array in left_grads[:-1]]
+    both = exchange(jnp.concatenate([left_grads[-1], right_grads[0]], axis=1))
+    left_sent.append((both, 0))
+    right_sent = [(both, blocks)] + [(exchange(array), 0) for array in right_grads[1:]]
     out = jnp.zeros((rows, cols, chans), BF16)
-    for first, left_grad, right_grad, sigm in zip(firsts, left_grads, right_grads, sigms):
+    for first, left_grad, right_grad, sigm in zip(firsts, left_sent, right_sent, sigms):
         out = last(left_grad, right_grad, sigm, first, out)
     return out
 

time: 662 us -> 659 us (level)
  blocking collectives: 52.3 us -> 97.3 us
  waiting for transfers between devices: 338 us -> 298 us
  starting transfers between devices: 51.8 us -> 42.6 us
  local copies, waits for them, and re-layouts: 98.3 us -> 105 us
    all_to_all x1, blocking collectives: 52.3 us -> 97.3 us  [exchange(): return lax.all_to_all(array, group, split_axis=0, concat_axis=0, tiled=True)]
    all_to_all x10 -> x8, waiting for transfers between devices: 338 us -> 298 us  [exchange(): return lax.all_to_all(array, group, split_axis=0, concat_axis=0, tiled=True)]
    all_to_all x10 -> x8, starting transfers between devices: 51.8 us -> 42.6 us  [exchange(): return lax.all_to_all(array, group, split_axis=0, concat_axis=0, tiled=True)]
    pallas_call x3 -> x2, Pallas kernels: 30.1 us -> 25.3 us  [project(): pl.pallas_call(functools.partial(project_kernel, step), grid=(rights + co...]
  transfers between devices with their start and end apart: 10 -> 8, of which waited for: 10 -> 8; matrix products, arithmetic and copies ran while one was open for 18% -> 19% of each run, Pallas kernels for 9% -> 7%
where the time goes in v4:
time: 659 us; the launch traced here: 649 us
  waiting for transfers between devices  298 us (45%)
  local copies, waits for them, and re-layouts  105 us (16%)
  blocking collectives  97.3 us (15%)
  Pallas kernels  76.3 us (12%)
  starting transfers between devices  42.6 us (6%)
  matrix products  26.3 us (4%)
    all_to_all x8, waiting for transfers between devices, exchange(): return lax.all_to_all(array, group, split_axis=0, concat_axis=0, tiled=True)  298 us
    all_to_all x1, blocking collectives, exchange(): return lax.all_to_all(array, group, split_axis=0, concat_axis=0, tiled=True)  97.3 us
    reshape x10, local copies, waits for them, and re-layouts, by_owner(): array = array.astype(BF16).reshape(own, row_blocks, count, col_blocks, cols)  45.8 us
    all_to_all x8, starting transfers between devices, exchange(): return lax.all_to_all(array, group, split_axis=0, concat_axis=0, tiled=True)  42.6 us
    pallas_call x2, Pallas kernels, last(): pl.pallas_call(functools.partial(last_kernel, step), grid=(blocks,), in_s...  29 us
    dot_general x6, matrix products, batch_dot(): lax.dot_general(a, b, (((ca,), (cb,)), ((0,), (0,))), preferred_element_t...  26.3 us
    pallas_call x2, Pallas kernels, project(): pl.pallas_call(functools.partial(project_kernel, step), grid=(rights + co...  25.3 us
    pallas_call x2, Pallas kernels, middle(): pl.pallas_call(functools.partial(middle_kernel, step), grid=(blocks,), in...  21.9 us
  transfers between devices with their start and end apart: 8, of which 8 were waited for; matrix products, arithmetic and copies ran while one was open for 19% of the time, Pallas kernels for 7%

profile of v4, /device:TPU:15, one launch (start us, length us, event | category | flops | bytes accessed | tf_op | source)
XLA Modules:
  0.0 649.1 jit_solution(10331471644963825812)
XLA Ops:
  4.9 17.1 %shard_map.83 = bf16[16,192,8,128]{3,2,1,0:T(8,128)(2,1)} custom-call(bf16[128,128,128]{2,1,0:T(8,128)(2,1)S(1)} %copy-done, f32[16,1,1024]{2,1,0:T(1,128)S(1)} %broadcast_multiply_fusion.mask_ref, f32[1,128]{1,0:T(1,128)S(1)} %bitcast.61, bf16[2,256,128]{2,1,0:T(8,128)(2,1)S(1)} %bitcast.53), custom_call_target="tpu_custom_call" | custom-call | flops 1610612736 | bytes 12582912 | tf_op jit(solution)/shard_map/pallas_call | solution.py:154
  22.0 6.7 %all-to-all-start.1 = ((bf16[16,192,8,128]{3,2,1,0:T(8,128)(2,1)}), bf16[16,192,8,128]{3,2,1,0:T(8,128)(2,1)}, u32[]{:S(2)}, u32[]{:S(2)}) async-start(bf16[16,192,8,128]{3,2,1,0:T(8,128)(2,1)} %shard_map.83), calls=%async_computation.1 | async-start | bytes 12582912 | tf_op jit(solution)/shard_map/all_to_all | solution.py:170
  28.7 8.2 %shard_map.82 = bf16[16,64,8,128]{3,2,1,0:T(8,128)(2,1)} custom-call(bf16[128,128,128]{2,1,0:T(8,128)(2,1)} %pair_ref.11, f32[16,1,1024]{2,1,0:T(1,128)S(1)} %broadcast_multiply_fusion.mask_ref, f32[1,128]{1,0:T(1,128)S(1)} %bitcast.62, bf16[2,256,128]{2,1,0:T(8,128)(2,1)S(1)} %bitcast.54), custom_call_target="tpu_custom_call" | custom-call | flops 536870912 | bytes 4194304 | tf_op jit(solution)/shard_map/pallas_call | solution.py:154
  36.8 129.2 %all-to-all-done.1 = bf16[16,192,8,128]{3,2,1,0:T(8,128)(2,1)} async-done(((bf16[16,192,8,128]{3,2,1,0:T(8,128)(2,1)}), bf16[16,192,8,128]{3,2,1,0:T(8,128)(2,1)}, u32[]{:S(2)}, u32[]{:S(2)}) %all-to-all-start.1) | async-done | bytes 6291488 | tf_op jit(solution)/shard_map/all_to_all | solution.py:170
  173.5 5.3 copy.31
  178.7 7.3 %reshape.120 = bf16[8,512,512]{2,1,0:T(8,128)(2,1)} reshape(bf16[8,4,128,4,128]{4,3,2,1,0:T(4,128)(2,1)} %copy.31) | data formatting | bytes 8388608 | tf_op jit(solution)/shard_map/reshape | solution.py:175
  193.4 5.6 convolution_convert_fusion.1
  207.2 11.3 %all-to-all-done = bf16[16,64,8,128]{3,2,1,0:T(8,128)(2,1)} async-done(((bf16[16,64,8,128]{3,2,1,0:T(8,128)(2,1)}), bf16[16,64,8,128]{3,2,1,0:T(8,128)(2,1)}, u32[]{:S(2)}, u32[]{:S(2)}) %all-to-all-start) | async-done | bytes 2097184 | tf_op jit(solution)/shard_map/all_to_all | solution.py:170
  218.5 5.2 all-to-all-start.4
  231.1 5.6 convolution_convert_fusion.3
  244.9 26.2 %all-to-all-done.4.comb_ref = bf16[16,64,8,128]{3,2,1,0:T(8,128)(2,1)} async-done(((bf16[16,64,8,128]{3,2,1,0:T(8,128)(2,1)}), bf16[16,64,8,128]{3,2,1,0:T(8,128)(2,1)}, u32[]{:S(2)}, u32[]{:S(2)}) %all-to-all-start.4) | async-done | bytes 2097184 | tf_op jit(solution)/shard_map/all_to_all | solution.py:170
  276.5 11.0 %shard_map.85 = (bf16[16,64,8,128]{3,2,1,0:T(8,128)(2,1)}, bf16[64,128,128]{2,1,0:T(8,128)(2,1)S(1)}) custom-call(bf16[128,128,128]{2,1,0:T(8,128)(2,1)} %pair_ref.11, bf16[128,128,128]{2,1,0:T(8,128)(2,1)} %gout_ref.3, bf16[16,64,8,128]{3,2,1,0:T(8,128)(2,1)} %all-to-all-done.4.comb_ref, f32[1,128]{1,0:T(1,128)S(1)} %bitcast.63, ...), custom_call_target="tpu_custom_call" | custom-call | flops 1073741824 | bytes 10485760 | tf_op jit(solution)/shard_map/pallas_call | solution.py:188
  288.9 34.7 %all-to-all-done.2.comb_ref = bf16[16,64,8,128]{3,2,1,0:T(8,128)(2,1)S(1)} async-done(((bf16[16,64,8,128]{3,2,1,0:T(8,128)(2,1)}), bf16[16,64,8,128]{3,2,1,0:T(8,128)(2,1)S(1)}, u32[]{:S(2)}, u32[]{:S(2)}) %all-to-all-start.2) | async-done | bytes 2097184 | tf_op jit(solution)/shard_map/all_to_all | solution.py:170
  329.8 11.0 %shard_map.84 = (bf16[16,64,8,128]{3,2,1,0:T(8,128)(2,1)}, bf16[64,128,128]{2,1,0:T(8,128)(2,1)S(1)}) custom-call(bf16[128,128,128]{2,1,0:T(8,128)(2,1)} %pair_ref.11, bf16[128,128,128]{2,1,0:T(8,128)(2,1)} %gout_ref.3, bf16[16,64,8,128]{3,2,1,0:T(8,128)(2,1)} %copy-done.16, f32[1,128]{1,0:T(1,128)S(1)} %bitcast.64, bf16[128,128]{1,0:T(8,128)(2,1)S(1)} %bitcast.57, ...), custom_call_target="tpu_custom_call" | custom-call | flops 1073741824 | bytes 10485760 | tf_op jit(solution)/shard_map/pallas_call | solution.py:188
  342.2 35.1 %all-to-all-done.5 = bf16[16,64,8,128]{3,2,1,0:T(8,128)(2,1)S(1)} async-done(((bf16[16,64,8,128]{3,2,1,0:T(8,128)(2,1)}), bf16[16,64,8,128]{3,2,1,0:T(8,128)(2,1)S(1)}, u32[]{:S(2)}, u32[]{:S(2)}) %all-to-all-start.5) | async-done | bytes 2097184 | tf_op jit(solution)/shard_map/all_to_all | solution.py:170
  387.9 5.5 convolution_convert_fusion
  401.6 28.1 %all-to-all-done.3 = bf16[16,64,8,128]{3,2,1,0:T(8,128)(2,1)} async-done(((bf16[16,64,8,128]{3,2,1,0:T(8,128)(2,1)}), bf16[16,64,8,128]{3,2,1,0:T(8,128)(2,1)}, u32[]{:S(2)}, u32[]{:S(2)}) %all-to-all-start.3) | async-done | bytes 2097184 | tf_op jit(solution)/shard_map/all_to_all | solution.py:170
  450.6 6.9 %reshape.134 = bf16[8,4,128,4,128]{4,3,2,1,0:T(4,128)(2,1)} reshape(bf16[8,512,512]{2,1,0:T(8,128)(2,1)} %add_convert_fusion) | data formatting | bytes 8388608 | tf_op jit(solution)/shard_map/reshape | solution.py:179
  457.5 7.0 %copy.44 = bf16[8,4,128,4,128]{4,0,2,1,3:T(8,128)(2,1)} copy(bf16[8,4,128,4,128]{4,3,2,1,0:T(4,128)(2,1)} %reshape.134) | data formatting | bytes 8388608 | tf_op jit(solution)/shard_map/reshape | solution.py:179
  482.2 97.3 %all_to_all.45.right_ref.left_ref = bf16[16,128,8,128]{3,2,1,0:T(8,128)(2,1)} all-to-all(bf16[16,128,8,128]{3,2,1,0:T(8,128)(2,1)} %pad_maximum_fusion), channel_id=1, replica_groups=mesh['rep'=2,'ch'=4,'row'=2,'sub'=2] {'ch','row','sub'}, dimensions={0} | all-to-all | bytes 8388608 | tf_op jit(solution)/shard_map/all_to_all | solution.py:170
  579.5 5.7 all-to-all-start.7
  588.3 14.5 %shard_map.86.held_ref = bf16[128,128,128]{2,1,0:T(8,128)(2,1)} custom-call(bf16[128,128,128]{2,1,0:T(8,128)(2,1)} %pair_ref.11, bf16[16,64,8,128]{3,2,1,0:T(8,128)(2,1)S(1)} %all-to-all-done.8.left_ref, bf16[16,128,8,128]{3,2,1,0:T(8,128)(2,1)} %all_to_all.45.right_ref.left_ref, ...), custom_call_target="tpu_custom_call", output_to_operand_aliasing={{}: (7, {})} | custom-call | flops 2415919104 | bytes 10485760 | tf_op jit(solution)/shard_map/pallas_call | solution.py:207
  602.8 29.7 %all-to-all-done.7.right_ref = bf16[16,64,8,128]{3,2,1,0:T(8,128)(2,1)} async-done(((bf16[16,64,8,128]{3,2,1,0:T(8,128)(2,1)}), bf16[16,64,8,128]{3,2,1,0:T(8,128)(2,1)}, u32[]{:S(2)}, u32[]{:S(2)}) %all-to-all-start.7) | async-done | bytes 2097184 | tf_op jit(solution)/shard_map/all_to_all | solution.py:170
  634.1 14.5 %shard_map.87 = bf16[128,128,128]{2,1,0:T(8,128)(2,1)} custom-call(bf16[128,128,128]{2,1,0:T(8,128)(2,1)} %pair_ref.11, bf16[16,128,8,128]{3,2,1,0:T(8,128)(2,1)} %all_to_all.45.right_ref.left_ref, bf16[16,64,8,128]{3,2,1,0:T(8,128)(2,1)} %all-to-all-done.7.right_ref, bf16[64,128,128]{2,1,0:T(8,128)(2,1)S(1)} %copy-done.4, ...), custom_call_target="tpu_custom_call", output_to_operand_aliasing={{}: (7, {})} | custom-call | flops 2415919104 | bytes 10485760 | tf_op jit(solution)/shard_map/pallas_call | solution.py:207
  (80 shorter events, 119.9 us)
Async XLA Ops:
  2.0 2.2 copy-start
  22.0 6.7 %copy-start.7 = (f32[128]{0:T(128)S(1)}, f32[128]{0:T(128)}, u32[]{:S(2)}) copy-start(f32[128]{0:T(128)} %param.11) | copy-start | bytes 1540
  22.0 144.1 %all-to-all-start.1 = ((bf16[16,192,8,128]{3,2,1,0:T(8,128)(2,1)}), bf16[16,192,8,128]{3,2,1,0:T(8,128)(2,1)}, u32[]{:S(2)}, u32[]{:S(2)}) async-start(bf16[16,192,8,128]{3,2,1,0:T(8,128)(2,1)} %shard_map.83), calls=%async_computation.1 | async-start | bytes 12582912 | tf_op jit(solution)/shard_map/all_to_all | solution.py:170
  166.1 52.4 %all-to-all-start = ((bf16[16,64,8,128]{3,2,1,0:T(8,128)(2,1)}), bf16[16,64,8,128]{3,2,1,0:T(8,128)(2,1)}, u32[]{:S(2)}, u32[]{:S(2)}) async-start(bf16[16,64,8,128]{3,2,1,0:T(8,128)(2,1)} %shard_map.82), calls=%async_computation | async-start | bytes 4194304 | tf_op jit(solution)/shard_map/all_to_all | solution.py:170
  193.4 5.6 copy-start.9
  218.5 52.6 %all-to-all-start.4 = ((bf16[16,64,8,128]{3,2,1,0:T(8,128)(2,1)}), bf16[16,64,8,128]{3,2,1,0:T(8,128)(2,1)}, u32[]{:S(2)}, u32[]{:S(2)}) async-start(bf16[16,64,8,128]{3,2,1,0:T(8,128)(2,1)} %bitcast.21), calls=%async_computation.4 | async-start | bytes 4194304 | tf_op jit(solution)/shard_map/all_to_all | solution.py:170
  231.0 5.6 copy-start.11
  271.1 5.0 copy-start.17
  271.1 5.2 copy-start.18
  271.1 5.3 copy-start.5
  271.1 52.5 %all-to-all-start.2 = ((bf16[16,64,8,128]{3,2,1,0:T(8,128)(2,1)}), bf16[16,64,8,128]{3,2,1,0:T(8,128)(2,1)S(1)}, u32[]{:S(2)}, u32[]{:S(2)}) async-start(bf16[16,64,8,128]{3,2,1,0:T(8,128)(2,1)} %bitcast.10), calls=%async_computation.2 | async-start | bytes 4194304 | tf_op jit(solution)/shard_map/all_to_all | solution.py:170
  287.5 1.4 copy-start.1
  324.9 52.3 %all-to-all-start.5 = ((bf16[16,64,8,128]{3,2,1,0:T(8,128)(2,1)}), bf16[16,64,8,128]{3,2,1,0:T(8,128)(2,1)S(1)}, u32[]{:S(2)}, u32[]{:S(2)}) async-start(bf16[16,64,8,128]{3,2,1,0:T(8,128)(2,1)} %get-tuple-element.10), calls=%async_computation.5 | async-start | bytes 4194304 | tf_op jit(solution)/shard_map/all_to_all | solution.py:170
  377.2 52.4 %all-to-all-start.3 = ((bf16[16,64,8,128]{3,2,1,0:T(8,128)(2,1)}), bf16[16,64,8,128]{3,2,1,0:T(8,128)(2,1)}, u32[]{:S(2)}, u32[]{:S(2)}) async-start(bf16[16,64,8,128]{3,2,1,0:T(8,128)(2,1)} %get-tuple-element.9), calls=%async_computation.3 | async-start | bytes 4194304 | tf_op jit(solution)/shard_map/all_to_all | solution.py:170
  387.8 5.5 copy-start.10
  429.7 52.5 %all-to-all-start.8 = ((bf16[16,64,8,128]{3,2,1,0:T(8,128)(2,1)}), bf16[16,64,8,128]{3,2,1,0:T(8,128)(2,1)S(1)}, u32[]{:S(2)}, u32[]{:S(2)}) async-start(bf16[16,64,8,128]{3,2,1,0:T(8,128)(2,1)} %bitcast.69), calls=%async_computation.8 | async-start | bytes 4194304 | tf_op jit(solution)/shard_map/all_to_all | solution.py:170
  443.6 3.7 copy-start.12
  443.6 3.7 copy-start.13
  457.5 7.1 %copy-start.8 = (bf16[8,512,512]{2,1,0:T(8,128)(2,1)S(1)}, bf16[8,512,512]{2,1,0:T(8,128)(2,1)}, u32[]{:S(2)}) copy-start(bf16[8,512,512]{2,1,0:T(8,128)(2,1)} %reshape.120) | copy-start | bytes 12582916
  457.5 7.1 %copy-start.14 = (bf16[8,256,512]{2,1,0:T(8,128)(2,1)S(1)}, bf16[8,256,512]{2,1,0:T(8,128)(2,1)}, u32[]{:S(2)}) copy-start(bf16[8,256,512]{2,1,0:T(8,128)(2,1)} %reshape.125) | copy-start | bytes 6291460
  471.2 3.1 copy-start.15
  579.5 53.1 %all-to-all-start.7 = ((bf16[16,64,8,128]{3,2,1,0:T(8,128)(2,1)}), bf16[16,64,8,128]{3,2,1,0:T(8,128)(2,1)}, u32[]{:S(2)}, u32[]{:S(2)}) async-start(bf16[16,64,8,128]{3,2,1,0:T(8,128)(2,1)} %get-tuple-element.13), calls=%async_computation.7 | async-start | bytes 4194304 | tf_op jit(solution)/shard_map/all_to_all | solution.py:170
  585.2 3.1 copy-start.2
  632.5 1.6 copy-start.4
  (3 other events, 3.4 us)

commit v5 on v1

v5 whole, which is shorter than its diff:
```python
import functools

import jax
import jax.numpy as jnp
from jax import lax
from jax.experimental import pallas as pl
from jax.experimental.pallas import tpu as pltpu
from jax.sharding import PartitionSpec as P

epsilon = 1e-05
F32 = jnp.float32
BF16 = jnp.bfloat16
VMEM_LIMIT = 56 * 1024 * 1024
ROWS = ("row", "sub")


def dot(a, b, ca, cb):
    return lax.dot_general(a, b, (((ca,), (cb,)), ((), ())), preferred_element_type=F32)


def turn(block):
    return jnp.swapaxes(block.astype(F32), 0, 1)


def norm_rows(pair_block, gain):
    x = pair_block.astype(F32)
    center = x - jnp.mean(x, axis=1, keepdims=True)
    scaled = lax.rsqrt(jnp.mean(center * center, axis=1, keepdims=True) + epsilon)
    hat = center * scaled
    return hat, scaled, (hat * gain).astype(BF16)


def rows_of(ref, first, count):
    block = ref[first:first + count]
    return block.reshape(count * block.shape[1], block.shape[2])


def load_chan(refs, first, count):
    parts = [jnp.concatenate([ref[first + t].astype(F32) for ref in refs], axis=0) for t in range(count)]
    return parts[0] if count == 1 else jnp.concatenate(parts, axis=1)


def store_chan(refs, first, count, value):
    _, own, cols = refs[0].shape
    for s, ref in enumerate(refs):
        group = value[s * own:(s + 1) * own].astype(BF16)
        for t in range(count):
            ref[first + t] = group[:, t * cols:(t + 1) * cols] if count > 1 else group


def project_kernel(step, pair_ref, mask_ref, gain_ref, weight_ref, *out_refs):
    rows, cols, chans = pair_ref.shape
    for first in range(0, rows, step):
        _, _, normed = norm_rows(rows_of(pair_ref, first, step), gain_ref[...])
        both = dot(weight_ref[...], normed, 1, 1)
        mask = mask_ref[0, :, first * cols:(first + step) * cols]
        store_chan(out_refs, first, step, mask * jax.nn.sigmoid(both[chans:]) * both[:chans])


def middle_kernel(
    step, groups, pair_ref, gout_ref, gain_ref, gate_t_ref, out_w_ref, out_t_ref, out_gain_ref, eye_ref, *refs
):
    comb_refs, gcomb_refs, sigm_ref = refs[:groups], refs[groups:2 * groups], refs[2 * groups]
    rows, cols, chans = pair_ref.shape
    out_gain = out_gain_ref[...]
    for first in range(0, rows, step):
        _, _, normed = norm_rows(rows_of(pair_ref, first, step), gain_ref[...])
        gate = jax.nn.sigmoid(dot(gate_t_ref[...], normed, 1, 1))
        gout = dot(eye_ref[...], rows_of(gout_ref, first, step), 1, 1)
        comb = load_chan(comb_refs, first, step)
        center = comb - jnp.mean(comb, axis=0, keepdims=True)
        scaled = lax.rsqrt(jnp.mean(center * center, axis=0, keepdims=True) + epsilon)
        hat = center * scaled
        lin = dot(out_t_ref[...], (hat * out_gain).astype(BF16), 1, 0)
        grad_lin = (gout * gate).astype(BF16)
        h = dot(out_w_ref[...], grad_lin, 1, 0) * out_gain
        grad = scaled * (
            h - jnp.mean(h, axis=0, keepdims=True) - hat * jnp.mean(h * hat, axis=0, keepdims=True)
        )
        store_chan(gcomb_refs, first, step, grad)
        sigm = (gout * lin * gate * (1.0 - gate)).astype(BF16)
        for t in range(step):
            sigm_ref[first + t] = sigm[:, t * cols:(t + 1) * cols] if step > 1 else sigm


def last_kernel(step, groups, pair_ref, sigm_ref, mask_ref, gain_ref, weight_ref, held_ref, *refs):
    del held_ref
    left_refs, right_refs, out_ref = refs[:groups], refs[groups:2 * groups], refs[2 * groups]
    rows, cols, chans = pair_ref.shape
    gain = gain_ref[...]
    weight = weight_ref[...]
    for first in range(0, rows, step):
        hat, scaled, normed = norm_rows(rows_of(pair_ref, first, step), gain)
        mask = mask_ref[0, :, first * cols:(first + step) * cols]
        proj = dot(weight[:4 * chans], normed, 1, 1)
        terms = []
        for which, piece_refs in enumerate((left_refs, right_refs)):
            grad = load_chan(piece_refs, first, step) * mask
            value = proj[2 * which * chans:(2 * which + 1) * chans]
            gate = jax.nn.sigmoid(proj[(2 * which + 1) * chans:(2 * which + 2) * chans])
            through = grad * gate
            terms += [through.astype(BF16), (through * value * (1.0 - gate)).astype(BF16)]
        parts = [sigm_ref[first + t] for t in range(step)]
        terms.append(parts[0] if step == 1 else jnp.concatenate(parts, axis=1))
        g = dot(jnp.concatenate(terms, axis=0), weight, 0, 0) * gain
        grad_in = scaled * (
            g - jnp.mean(g, axis=1, keepdims=True) - hat * jnp.mean(g * hat, axis=1, keepdims=True)
        )
        out_ref[first:first + step] = grad_in.reshape(step, cols, chans).astype(BF16)


def gather_kernel(*refs):
    out_ref = refs[-1]
    blocks, _, cols, _ = out_ref.shape
    for s, ref in enumerate(refs[:-1]):
        turned = turn(ref[...]).astype(BF16)
        for b in range(blocks):
            out_ref[b, :, :, s * cols:(s + 1) * cols] = turned[:, b * cols:(b + 1) * cols]


def split_kernel(in_ref, *out_refs):
    cols = out_refs[0].shape[2]
    for s, ref in enumerate(out_refs):
        ref[...] = turn(in_ref[0, :, :, s * cols:(s + 1) * cols]).astype(BF16)


def combine_kernel(groups, partner_ref, right_ref, *refs):
    left_refs, out_refs, left_buf, sums = refs[:groups], refs[groups:2 * groups], refs[2 * groups], refs[-1]
    rows, own, cols = left_refs[0].shape
    for s, ref in enumerate(left_refs):
        left_buf[:, :, s * cols:(s + 1) * cols] = turn(ref[...]).astype(BF16)
    for s, ref in enumerate(out_refs):
        other = partner_ref[s]
        for c in range(own):
            sums[c] = dot(left_buf[c], right_ref[other, c], 1, 1)
        ref[...] = turn(sums[...]).astype(BF16)


def left_kernel(groups, partner_ref, right_ref, *refs):
    grad_refs, out_refs, sums = refs[:groups], refs[groups:2 * groups], refs[-1]
    rows, own, cols = grad_refs[0].shape
    grads = [turn(ref[...]).astype(BF16) for ref in grad_refs]
    for c in range(own):
        total = dot(grads[0][c], right_ref[partner_ref[0], c], 1, 0)
        for s in range(1, groups):
            total += dot(grads[s][c], right_ref[partner_ref[s], c], 1, 0)
        sums[c] = total
    for s, ref in enumerate(out_refs):
        ref[...] = turn(sums[:, :, s * cols:(s + 1) * cols]).astype(BF16)


def right_kernel(groups, chunks, partner_ref, *refs):
    count = groups * chunks
    grad_refs, left_refs, out_refs, left_buf = refs[:count], refs[count:2 * count], refs[2 * count:-1], refs[-1]
    rows, own, cols = grad_refs[0].shape
    part = out_refs[0].shape[2]
    row_blocks = out_refs[0].shape[0]
    span = groups // row_blocks
    for n, ref in enumerate(left_refs):
        piece, s = divmod(n, groups)
        left_buf[:, piece * rows:(piece + 1) * rows, s * cols:(s + 1) * cols] = turn(ref[...]).astype(BF16)
    for s in range(groups):
        grads = [turn(grad_refs[piece * groups + s][...]).astype(BF16) for piece in range(chunks)]
        grad = grads[0] if chunks == 1 else jnp.concatenate(grads, axis=1)
        other = partner_ref[s]
        owner = other // span
        for c in range(own):
            total = dot(grad[c], left_buf[c], 0, 0).astype(BF16)
            for m in range(cols // part):
                block = total[m * part:(m + 1) * part]
                if span == 1:
                    out_refs[m][owner, c] = block
                else:
                    chunk = (other % span) * (cols // part) + m
                    for h, ref in enumerate(out_refs):

                        @pl.when(chunk == h)
                        def _(ref=ref, block=block, c=c):
                            ref[owner, c] = block


def local(chunks, pair, grad_out, token_mask, ln_gain, proj_weights, gate_weight, out_weight, out_gain):
    rows, cols, chans = pair.shape
    groups = lax.axis_size("ch")
    row_blocks = lax.axis_size(ROWS)
    own = chans // groups
    tokens = rows * row_blocks
    part_rows = rows // chunks
    block = min(8, part_rows)
    blocks = part_rows // block
    step = 4 if cols % 128 == 0 and block % 4 == 0 else 1
    some = 16 if own % 16 == 0 else own
    z = lax.axis_index("ch")
    partner = jnp.stack([z ^ s for s in range(groups)]).astype(jnp.int32)

    def mine(array, axis):
        parts = [lax.dynamic_slice_in_dim(array, (z ^ s) * own, own, axis) for s in range(groups)]
        return jnp.concatenate(parts, axis=axis)

    mask_float = token_mask.astype(F32)
    row_mask = lax.dynamic_slice_in_dim(mask_float, lax.axis_index(ROWS) * rows, rows)
    col_mask = lax.dynamic_slice_in_dim(mask_float, z * cols, cols)
    mask = (row_mask[:, None] * col_mask[None, :]).reshape(rows // block, 1, block * cols)
    gain = ln_gain.reshape(1, chans)
    proj_t = mine(jnp.swapaxes(proj_weights, 1, 2), 1)
    left_w = proj_t[:2].reshape(2 * chans, chans)
    right_w = proj_t[2:].reshape(2 * chans, chans)
    gate_t = gate_weight.T
    all_w = jnp.concatenate([left_w, right_w, gate_t], axis=0)
    out_w = mine(out_weight, 0)
    out_t = out_w.T
    gain_col = mine(out_gain, 0).reshape(chans, 1)
    eye = jnp.eye(chans, dtype=BF16)

    params = pltpu.CompilerParams(vmem_limit_bytes=VMEM_LIMIT)

    def cost(flops, arrays):
        return pl.CostEstimate(
            flops=flops, bytes_accessed=arrays * part_rows * cols * chans * 2, transcendentals=0
        )

    pairs = part_rows * cols

    def row_spec(first):
        return pl.BlockSpec((block, cols, chans), lambda s: (first + s, 0, 0))

    def mask_spec(first):
        return pl.BlockSpec((1, 1, block * cols), lambda s: (first + s, 0, 0))

    def whole(array):
        return pl.BlockSpec(array.shape, lambda s: (0,) * array.ndim)

    piece_spec = pl.BlockSpec((block, own, cols), lambda s: (s, 0, 0))
    sigm_spec = pl.BlockSpec((block, chans, cols), lambda s: (s, 0, 0))

    def pieces(count):
        return [jax.ShapeDtypeStruct((count, own, cols), BF16)] * groups

    def project(weight, first, count):
        return pl.pallas_call(
            functools.partial(project_kernel, step),
            grid=(count,),
            in_specs=[row_spec(first), mask_spec(first), whole(gain), whole(weight)],
            out_specs=[piece_spec] * groups,
            out_shape=pieces(count * block),
            compiler_params=params,
            cost_estimate=cost(4 * chans * chans * count * block * cols, 2 * count // blocks),
        )(pair, mask, gain, weight)

    def middle(comb, first):
        return pl.pallas_call(
            functools.partial(middle_kernel, step, groups),
            grid=(blocks,),
            in_specs=[row_spec(first), row_spec(first), whole(gain), whole(gate_t), whole(out_w),
                      whole(out_t), whole(gain_col), whole(eye)] + [piece_spec] * groups,
            out_specs=[piece_spec] * groups + [sigm_spec],
            out_shape=pieces(part_rows) + [jax.ShapeDtypeStruct((part_rows, chans, cols), BF16)],
            compiler_params=params,
            cost_estimate=cost(8 * chans * chans * pairs, 5),
        )(pair, grad_out, gain, gate_t, out_w, out_t, gain_col, eye, *comb)

    def last(left_grad, right_grad, sigm, first, held):
        return pl.pallas_call(
            functools.partial(last_kernel, step, groups),
            grid=(blocks,),
            in_specs=[row_spec(first), sigm_spec, mask_spec(first), whole(gain), whole(all_w),
                      pl.BlockSpec(memory_space=pl.ANY)] + [piece_spec] * (2 * groups),
            out_specs=row_spec(first),
            out_shape=jax.ShapeDtypeStruct((rows, cols, chans), BF16),
            input_output_aliases={5: 0},
            compiler_params=params,
            cost_estimate=cost(18 * chans * chans * pairs, 5),
        )(pair, sigm, mask, gain, all_w, held, *left_grad, *right_grad)

    def exchange(sent):
        return [sent[0]] + [
            lax.ppermute(sent[s], "ch", [(a, a ^ s) for a in range(groups)]) for s in range(1, groups)
        ]

    def chan_spec(count):
        return pl.BlockSpec((count, some, cols), lambda g, *_: (0, g, 0))

    def all_spec(*shape):
        lead, tail = shape[0], shape[1:]
        return pl.BlockSpec((lead, some) + tail, lambda g, *_: (0, g, 0, 0))

    def gather(got):
        return pl.pallas_call(
            gather_kernel,
            grid=(own // some,),
            in_specs=[chan_spec(rows)] * groups,
            out_specs=all_spec(rows // cols, cols, tokens),
            out_shape=jax.ShapeDtypeStruct((rows // cols, own, cols, tokens), BF16),
            compiler_params=params,
            cost_estimate=cost(0, 4),
        )(*got)

    def split(array):
        return pl.pallas_call(
            split_kernel,
            grid=(own // some,),
            in_specs=[all_spec(1, part_rows, tokens)],
            out_specs=[chan_spec(part_rows)] * groups,
            out_shape=pieces(part_rows),
            compiler_params=params,
            cost_estimate=cost(0, 2),
        )(array)

    product = 2 * part_rows * tokens * tokens * own

    def with_right(kernel, got, scratch):
        return pl.pallas_call(
            functools.partial(kernel, groups),
            grid_spec=pltpu.PrefetchScalarGridSpec(
                num_scalar_prefetch=1, grid=(own // some,),
                in_specs=[all_spec(groups, cols, tokens)] + [chan_spec(part_rows)] * groups,
                out_specs=[chan_spec(part_rows)] * groups,
                scratch_shapes=scratch,
            ),
            out_shape=pieces(part_rows),
            compiler_params=params,
            cost_estimate=cost(product, 2 + row_blocks * chunks),
        )(partner, right, *got)

    def combine(left):
        return with_right(combine_kernel, left, [
            pltpu.VMEM((some, part_rows, tokens), BF16), pltpu.VMEM((some, part_rows, cols), F32)
        ])

    def left_back(grad):
        return with_right(left_kernel, grad, [pltpu.VMEM((some, part_rows, tokens), F32)])

    def right_back(grads, lefts):
        return pl.pallas_call(
            functools.partial(right_kernel, groups, chunks),
            grid_spec=pltpu.PrefetchScalarGridSpec(
                num_scalar_prefetch=1, grid=(own // some,),
                in_specs=[chan_spec(part_rows)] * (2 * groups * chunks),
                out_specs=[all_spec(row_blocks, part_rows, tokens)] * chunks,
                scratch_shapes=[pltpu.VMEM((some, rows, tokens), BF16)],
            ),
            out_shape=[jax.ShapeDtypeStruct((row_blocks, own, part_rows, tokens), BF16)] * chunks,
            compiler_params=params,
            cost_estimate=cost(product * chunks, (2 + row_blocks) * chunks),
        )(partner, *sum(grads, []), *sum(lefts, []))

    firsts = [p * blocks for p in range(chunks)]
    right = gather(exchange(project(right_w, 0, rows // block)))
    right = lax.all_gather(right, ROWS, axis=0, tiled=True)
    lefts = [exchange(project(left_w, first, blocks)) for first in firsts]
    sigms, left_grads, grads = [], [], []
    for first, left in zip(firsts, lefts):
        *grad_comb, sigm = middle(exchange(combine(left)), first)
        sigms.append(sigm)
        grads.append(exchange(grad_comb))
        left_grads.append(exchange(left_back(grads[-1])))
    right_grads = [
        exchange(split(lax.psum_scatter(array, ROWS, scatter_dimension=0, tiled=True)))
        for array in right_back(grads, lefts)
    ]
    out = jnp.zeros((rows, cols, chans), BF16)
    for first, left_grad, right_grad, sigm in zip(firsts, left_grads, right_grads, sigms):
        out = last(left_grad, right_grad, sigm, first, out)
    return out


def solution(mesh):
    spread = P(("rep", "row", "sub"), "ch", None)
    return jax.shard_map(
        functools.partial(local, 2),
        mesh=mesh,
        in_specs=(spread, spread, P("rep"), P(), P(), P(), P(), P()),
        out_specs=spread,
        check_vma=False,
    )
```

time: 662 us -> 709 us (1.071); the launches traced: 651 us -> 706 us
  waiting for transfers between devices: 338 us -> 466 us
  local copies, waits for them, and re-layouts: 98.3 us -> 14 us
  Pallas kernels: 81.1 us -> 153 us
  blocking collectives: 52.3 us -> 0 us
  matrix products: 28.3 us -> 0 us
  between operations: 0.69 us -> 13.4 us
    all_to_all x10 -> x0, waiting for transfers between devices: 338 us -> none  [exchange(): return lax.all_to_all(array, group, split_axis=0, concat_axis=0, tiled=True)]
    ppermute x0 -> x33, waiting for transfers between devices: none -> 299 us  [exchange(): lax.ppermute(sent[s], 'ch', [(a, a ^ s) for a in range(groups)])]
    reduce_scatter x0 -> x2, waiting for transfers between devices: none -> 115 us  [local(): lax.psum_scatter(array, ROWS, scatter_dimension=0, tiled=True)]
    pallas_call x4 -> x12, Pallas kernels: 50.9 us -> 122 us  [the longest x4 44.4 us: with_right(): pl.pallas_call(functools.partial(kernel, groups), grid_spec=pltpu.Prefetc...]
    reshape x17 -> x1, local copies, waits for them, and re-layouts: 64.3 us -> 0.73 us  [local(): gain_col = mine(out_gain, 0).reshape(chans, 1)]
    ppermute x0 -> x33, starting transfers between devices: none -> 54.6 us  [exchange(): lax.ppermute(sent[s], 'ch', [(a, a ^ s) for a in range(groups)])]
    all_to_all x1 -> x0, blocking collectives: 52.3 us -> none  [exchange(): return lax.all_to_all(array, group, split_axis=0, concat_axis=0, tiled=True)]
    all_to_all x10 -> x0, starting transfers between devices: 51.8 us -> none  [exchange(): return lax.all_to_all(array, group, split_axis=0, concat_axis=0, tiled=True)]
  transfers between devices with their start and end apart: 10 -> 36, of which waited for: 10 -> 20; matrix products, arithmetic and copies ran while one was open for 18% -> 1% of each run, Pallas kernels for 9% -> 15%
where the time goes in v5:
time: 709 us; the launch traced here: 706 us
  waiting for transfers between devices  466 us (66%)
  Pallas kernels  153 us (22%)
  starting transfers between devices  54.8 us (8%)
  local copies, waits for them, and re-layouts  14 us (2%)
  between operations  13.4 us (2%)
    ppermute x33, waiting for transfers between devices, exchange(): lax.ppermute(sent[s], 'ch', [(a, a ^ s) for a in range(groups)])  299 us
    reduce_scatter x2, waiting for transfers between devices, local(): lax.psum_scatter(array, ROWS, scatter_dimension=0, tiled=True)  115 us
    ppermute x33, starting transfers between devices, exchange(): lax.ppermute(sent[s], 'ch', [(a, a ^ s) for a in range(groups)])  54.6 us
    all_gather x1, waiting for transfers between devices, local(): right = lax.all_gather(right, ROWS, axis=0, tiled=True)  51.2 us
    pallas_call x4, Pallas kernels, with_right(): pl.pallas_call(functools.partial(kernel, groups), grid_spec=pltpu.Prefetc...  44.4 us
    pallas_call x3, Pallas kernels, project(): pl.pallas_call(functools.partial(project_kernel, step), grid=(count,), in...  31 us
    pallas_call x2, Pallas kernels, last(): pl.pallas_call(functools.partial(last_kernel, step, groups), grid=(blocks...  29.8 us
    pallas_call x2, Pallas kernels, middle(): pl.pallas_call(functools.partial(middle_kernel, step, groups), grid=(bloc...  21.9 us
  transfers between devices with their start and end apart: 36, of which 20 were waited for; matrix products, arithmetic and copies ran while one was open for 1% of the time, Pallas kernels for 15%

profile of v5, /device:TPU:15, one launch (start us, length us, event | category | flops | bytes accessed | tf_op | source)
XLA Modules:
  0.0 705.5 jit_solution(16698024833829634148)
XLA Ops:
  10.5 14.7 %shard_map.82 = (bf16[128,32,128]{2,1,0:T(8,128)(2,1)}, bf16[128,32,128]{2,1,0:T(8,128)(2,1)}, bf16[128,32,128]{2,1,0:T(8,128)(2,1)}, bf16[128,32,128]{2,1,0:T(8,128)(2,1)}) custom-call(bf16[128,128,128]{2,1,0:T(8,128)(2,1)} %pair_ref.13, f32[16,1,1024]{2,1,0:T(1,128)} %broadcast_multiply_fusion.mask_ref, f32[1,128]{1,0:T(1,128)} %bitcast.32, ...), custom_call_target="tpu_custom_call" | custom-call | flops 1073741824 | bytes 8388608 | tf_op jit(solution)/shard_map/pallas_call | solution.py:240
  27.9 41.4 %collective-permute-done.refs_1_ = bf16[128,32,128]{2,1,0:T(8,128)(2,1)S(1)} collective-permute-done((bf16[128,32,128]{2,1,0:T(8,128)(2,1)}, bf16[128,32,128]{2,1,0:T(8,128)(2,1)S(1)}, u32[]{:S(2)}, u32[]{:S(2)}) %collective-permute-start) | collective-permute-done | bytes 1048608 | tf_op jit(solution)/shard_map/ppermute | solution.py:277
  73.0 44.8 %collective-permute-done.2.refs_3_ = bf16[128,32,128]{2,1,0:T(8,128)(2,1)S(1)} collective-permute-done((bf16[128,32,128]{2,1,0:T(8,128)(2,1)}, bf16[128,32,128]{2,1,0:T(8,128)(2,1)S(1)}, u32[]{:S(2)}, u32[]{:S(2)}) %collective-permute-start.2) | collective-permute-done | bytes 1048608 | tf_op jit(solution)/shard_map/ppermute | solution.py:277
  157.1 22.5 %collective-permute-done.11.refs_3_.refs_11_ = bf16[64,32,128]{2,1,0:T(8,128)(2,1)S(1)} collective-permute-done((bf16[64,32,128]{2,1,0:T(8,128)(2,1)}, bf16[64,32,128]{2,1,0:T(8,128)(2,1)S(1)}, u32[]{:S(2)}, u32[]{:S(2)}) %collective-permute-start.11) | collective-permute-done | bytes 524320 | tf_op jit(solution)/shard_map/ppermute | solution.py:277
  179.7 51.2 %all-gather.2.cloned.1.call-done.right_ref = bf16[4,32,128,512]{3,2,1,0:T(8,128)(2,1)} async-done(((bf16[1,32,128,512]{3,2,1,0:T(8,128)(2,1)}), bf16[4,32,128,512]{3,2,1,0:T(8,128)(2,1)}) %all-gather.2.cloned.1.call-update) | async-done | bytes 16777232 | tf_op jit(solution)/shard_map/all_gather | solution.py:349
  230.9 11.7 %shard_map.88 = (bf16[64,32,128]{2,1,0:T(8,128)(2,1)}, bf16[64,32,128]{2,1,0:T(8,128)(2,1)}, bf16[64,32,128]{2,1,0:T(8,128)(2,1)}, bf16[64,32,128]{2,1,0:T(8,128)(2,1)}) custom-call(s32[4]{0:T(128)} %pad_add_fusion.partner_ref, bf16[4,32,128,512]{3,2,1,0:T(8,128)(2,1)} %all-gather.2.cloned.1.call-done.right_ref, ...), custom_call_target="tpu_custom_call" | custom-call | flops 1073741824 | bytes 20971520 | tf_op jit(solution)/shard_map/pallas_call | solution.py:312
  248.4 11.6 %shard_map.85 = (bf16[64,32,128]{2,1,0:T(8,128)(2,1)}, bf16[64,32,128]{2,1,0:T(8,128)(2,1)}, bf16[64,32,128]{2,1,0:T(8,128)(2,1)}, bf16[64,32,128]{2,1,0:T(8,128)(2,1)}) custom-call(s32[4]{0:T(128)} %pad_add_fusion.partner_ref, bf16[4,32,128,512]{3,2,1,0:T(8,128)(2,1)} %all-gather.2.cloned.1.call-done.right_ref, ...), custom_call_target="tpu_custom_call" | custom-call | flops 1073741824 | bytes 20971520 | tf_op jit(solution)/shard_map/pallas_call | solution.py:312
  268.3 22.5 %collective-permute-done.14.refs_3_ = bf16[64,32,128]{2,1,0:T(8,128)(2,1)S(1)} collective-permute-done((bf16[64,32,128]{2,1,0:T(8,128)(2,1)}, bf16[64,32,128]{2,1,0:T(8,128)(2,1)S(1)}, u32[]{:S(2)}, u32[]{:S(2)}) %collective-permute-start.14) | collective-permute-done | bytes 524320 | tf_op jit(solution)/shard_map/ppermute | solution.py:277
  291.6 10.9 %shard_map.89 = (bf16[64,32,128]{2,1,0:T(8,128)(2,1)}, bf16[64,32,128]{2,1,0:T(8,128)(2,1)}, bf16[64,32,128]{2,1,0:T(8,128)(2,1)}, bf16[64,32,128]{2,1,0:T(8,128)(2,1)}, bf16[64,128,128]{2,1,0:T(8,128)(2,1)}) custom-call(bf16[128,128,128]{2,1,0:T(8,128)(2,1)} %pair_ref.13, bf16[128,128,128]{2,1,0:T(8,128)(2,1)} %gout_ref.3, f32[1,128]{1,0:T(1,128)} %bitcast.35, ...), custom_call_target="tpu_custom_call" | custom-call | flops 1073741824 | bytes 10485760 | tf_op jit(solution)/shard_map/pallas_call | solution.py:251
  302.6 24.4 %collective-permute-start.16 = (bf16[64,32,128]{2,1,0:T(8,128)(2,1)}, bf16[64,32,128]{2,1,0:T(8,128)(2,1)S(1)}, u32[]{:S(2)}, u32[]{:S(2)}) collective-permute-start(bf16[64,32,128]{2,1,0:T(8,128)(2,1)} %get-tuple-element.77), channel_id=1, source_target_pairs={{0,8},{4,12},{8,0},{12,4},{1,9},{5,13},{9,1},{13,5},{2,10},{6,14},... | collective-permute-start | bytes 1572872 | tf_op jit(solution)/shard_map/ppermute | solution.py:277
  327.0 30.3 %collective-permute-done.8.refs_3_ = bf16[64,32,128]{2,1,0:T(8,128)(2,1)S(1)} collective-permute-done((bf16[64,32,128]{2,1,0:T(8,128)(2,1)}, bf16[64,32,128]{2,1,0:T(8,128)(2,1)S(1)}, u32[]{:S(2)}, u32[]{:S(2)}) %collective-permute-start.8) | collective-permute-done | bytes 524320 | tf_op jit(solution)/shard_map/ppermute | solution.py:277
  358.1 11.0 %shard_map.86 = (bf16[64,32,128]{2,1,0:T(8,128)(2,1)}, bf16[64,32,128]{2,1,0:T(8,128)(2,1)}, bf16[64,32,128]{2,1,0:T(8,128)(2,1)}, bf16[64,32,128]{2,1,0:T(8,128)(2,1)}, bf16[64,128,128]{2,1,0:T(8,128)(2,1)}) custom-call(bf16[128,128,128]{2,1,0:T(8,128)(2,1)} %pair_ref.13, bf16[128,128,128]{2,1,0:T(8,128)(2,1)} %gout_ref.3, f32[1,128]{1,0:T(1,128)} %bitcast.36, ...), custom_call_target="tpu_custom_call" | custom-call | flops 1073741824 | bytes 10485760 | tf_op jit(solution)/shard_map/pallas_call | solution.py:251
  380.7 32.8 %collective-permute-done.22.refs_6_.refs_2_ = bf16[64,32,128]{2,1,0:T(8,128)(2,1)S(1)} collective-permute-done((bf16[64,32,128]{2,1,0:T(8,128)(2,1)}, bf16[64,32,128]{2,1,0:T(8,128)(2,1)S(1)}, u32[]{:S(2)}, u32[]{:S(2)}) %collective-permute-start.22) | collective-permute-done | bytes 524320 | tf_op jit(solution)/shard_map/ppermute | solution.py:277
  413.5 12.2 %collective-permute-done.23.refs_7_.refs_3_ = bf16[64,32,128]{2,1,0:T(8,128)(2,1)S(1)} collective-permute-done((bf16[64,32,128]{2,1,0:T(8,128)(2,1)}, bf16[64,32,128]{2,1,0:T(8,128)(2,1)S(1)}, u32[]{:S(2)}, u32[]{:S(2)}) %collective-permute-start.23) | collective-permute-done | bytes 524320 | tf_op jit(solution)/shard_map/ppermute | solution.py:277
  426.4 14.6 %shard_map.91 = (bf16[4,32,64,512]{3,2,1,0:T(8,128)(2,1)}, bf16[4,32,64,512]{3,2,1,0:T(8,128)(2,1)}) custom-call(s32[4]{0:T(128)} %pad_add_fusion.partner_ref, bf16[64,32,128]{2,1,0:T(8,128)(2,1)} %get-tuple-element.75.refs_0_, bf16[64,32,128]{2,1,0:T(8,128)(2,1)} %copy-done.6, bf16[64,32,128]{2,1,0:T(8,128)(2,1)} %copy-done.7, ...), custom_call_target="tpu_custom_call" | custom-call | flops 2147483648 | bytes 25165824 | tf_op jit(solution)/shard_map/pallas_call | solution.py:334
  455.0 10.6 %shard_map.94 = (bf16[64,32,128]{2,1,0:T(8,128)(2,1)}, bf16[64,32,128]{2,1,0:T(8,128)(2,1)}, bf16[64,32,128]{2,1,0:T(8,128)(2,1)}, bf16[64,32,128]{2,1,0:T(8,128)(2,1)}) custom-call(s32[4]{0:T(128)} %pad_add_fusion.partner_ref, bf16[4,32,128,512]{3,2,1,0:T(8,128)(2,1)} %all-gather.2.cloned.1.call-done.right_ref, ...), custom_call_target="tpu_custom_call" | custom-call | flops 1073741824 | bytes 20971520 | tf_op jit(solution)/shard_map/pallas_call | solution.py:312
  466.2 46.4 %reduce-scatter.3.cloned.1.call-done.in_ref = bf16[1,32,64,512]{3,2,1,0:T(8,128)(2,1)} async-done(((bf16[4,32,64,512]{3,2,1,0:T(8,128)(2,1)}), bf16[1,32,64,512]{3,2,1,0:T(8,128)(2,1)}) %reduce-scatter.3.cloned.1.call-update) | async-done | bytes 2097168 | tf_op jit(solution)/shard_map/reduce_scatter | solution.py:358
  518.5 68.7 %reduce-scatter.5.cloned.1.call-done.in_ref = bf16[1,32,64,512]{3,2,1,0:T(8,128)(2,1)} async-done(((bf16[4,32,64,512]{3,2,1,0:T(8,128)(2,1)}), bf16[1,32,64,512]{3,2,1,0:T(8,128)(2,1)}) %reduce-scatter.5.cloned.1.call-update) | async-done | bytes 2097168 | tf_op jit(solution)/shard_map/reduce_scatter | solution.py:358
  599.2 14.9 %shard_map.93.held_ref = bf16[128,128,128]{2,1,0:T(8,128)(2,1)} custom-call(bf16[128,128,128]{2,1,0:T(8,128)(2,1)} %pair_ref.13, bf16[64,128,128]{2,1,0:T(8,128)(2,1)} %get-tuple-element.74.sigm_ref, f32[16,1,1024]{2,1,0:T(1,128)} %broadcast_multiply_fusion.mask_ref, f32[1,128]{1,0:T(1,128)} %bitcast.37, ...), custom_call_target="tpu_custom_call", output_to_operand_aliasing={{}: (5, {})} | custom-call | flops 2415919104 | bytes 10485760 | tf_op jit(solution)/shard_map/pallas_call | solution.py:263
  614.1 13.6 %collective-permute-done.28.refs_2_ = bf16[64,32,128]{2,1,0:T(8,128)(2,1)S(1)} collective-permute-done((bf16[64,32,128]{2,1,0:T(8,128)(2,1)}, bf16[64,32,128]{2,1,0:T(8,128)(2,1)S(1)}, u32[]{:S(2)}, u32[]{:S(2)}) %collective-permute-start.28) | collective-permute-done | bytes 524320 | tf_op jit(solution)/shard_map/ppermute | solution.py:277
  627.6 33.2 %collective-permute-done.29.refs_3_ = bf16[64,32,128]{2,1,0:T(8,128)(2,1)S(1)} collective-permute-done((bf16[64,32,128]{2,1,0:T(8,128)(2,1)}, bf16[64,32,128]{2,1,0:T(8,128)(2,1)S(1)}, u32[]{:S(2)}, u32[]{:S(2)}) %collective-permute-start.29) | collective-permute-done | bytes 524320 | tf_op jit(solution)/shard_map/ppermute | solution.py:277
  660.8 11.2 %collective-permute-done.31.refs_6_ = bf16[64,32,128]{2,1,0:T(8,128)(2,1)S(1)} collective-permute-done((bf16[64,32,128]{2,1,0:T(8,128)(2,1)}, bf16[64,32,128]{2,1,0:T(8,128)(2,1)S(1)}, u32[]{:S(2)}, u32[]{:S(2)}) %collective-permute-start.31) | collective-permute-done | bytes 524320 | tf_op jit(solution)/shard_map/ppermute | solution.py:277
  672.1 11.2 %collective-permute-done.32.refs_7_ = bf16[64,32,128]{2,1,0:T(8,128)(2,1)S(1)} collective-permute-done((bf16[64,32,128]{2,1,0:T(8,128)(2,1)}, bf16[64,32,128]{2,1,0:T(8,128)(2,1)S(1)}, u32[]{:S(2)}, u32[]{:S(2)}) %collective-permute-start.32) | collective-permute-done | bytes 524320 | tf_op jit(solution)/shard_map/ppermute | solution.py:277
  684.1 14.9 %shard_map.96 = bf16[128,128,128]{2,1,0:T(8,128)(2,1)} custom-call(bf16[128,128,128]{2,1,0:T(8,128)(2,1)} %pair_ref.13, bf16[64,128,128]{2,1,0:T(8,128)(2,1)} %get-tuple-element.65.sigm_ref, f32[16,1,1024]{2,1,0:T(1,128)} %broadcast_multiply_fusion.mask_ref, f32[1,128]{1,0:T(1,128)} %bitcast.38, ...), custom_call_target="tpu_custom_call", output_to_operand_aliasing={{}: (5, {})} | custom-call | flops 2415919104 | bytes 10485760 | tf_op jit(solution)/shard_map/pallas_call | solution.py:263
  (169 shorter events, 110.9 us)
Async XLA Ops:
  6.5 224.3 %all-gather.2.cloned.1.call-start = ((), (), s32[]{:S(2)}) async-start(), calls=%async_computation.2 | async-start | bytes 20971520 | tf_op jit(solution)/shard_map/all_gather | solution.py:349
  27.8 90.1 %collective-permute-start.2 = (bf16[128,32,128]{2,1,0:T(8,128)(2,1)}, bf16[128,32,128]{2,1,0:T(8,128)(2,1)S(1)}, u32[]{:S(2)}, u32[]{:S(2)}) collective-permute-start(bf16[128,32,128]{2,1,0:T(8,128)(2,1)} %get-tuple-element.56), channel_id=1, source_target_pairs={{0,12},{4,8},{8,4},{12,0},{1,13},{5,9},{9,5},{13,1},{2,14},{6,10},... | collective-permute-start | bytes 3145736 | tf_op jit(solution)/shard_map/ppermute | solution.py:277
  124.0 388.7 %reduce-scatter.3.cloned.1.call-start = ((), (), s32[]{:S(2)}) async-start(), calls=%async_computation.3 | async-start | bytes 10485760 | tf_op jit(solution)/shard_map/reduce_scatter | solution.py:358
  144.0 101.0 %collective-permute-start.3 = (bf16[64,32,128]{2,1,0:T(8,128)(2,1)}, bf16[64,32,128]{2,1,0:T(8,128)(2,1)S(1)}, u32[]{:S(2)}, u32[]{:S(2)}) collective-permute-start(bf16[64,32,128]{2,1,0:T(8,128)(2,1)} %get-tuple-element.58), channel_id=1, source_target_pairs={{0,4},{4,0},{8,12},{12,8},{1,5},{5,1},{9,13},{13,9},{2,6},{6,2},{1... | collective-permute-start | bytes 1572872 | tf_op jit(solution)/shard_map/ppermute | solution.py:277
  145.0 102.5 %collective-permute-start.4 = (bf16[64,32,128]{2,1,0:T(8,128)(2,1)}, bf16[64,32,128]{2,1,0:T(8,128)(2,1)S(1)}, u32[]{:S(2)}, u32[]{:S(2)}) collective-permute-start(bf16[64,32,128]{2,1,0:T(8,128)(2,1)} %get-tuple-element.59), channel_id=1, source_target_pairs={{0,8},{4,12},{8,0},{12,4},{1,9},{5,13},{9,1},{13,5},{2,10},{6,14},... | collective-permute-start | bytes 1572872 | tf_op jit(solution)/shard_map/ppermute | solution.py:277
  152.9 94.6 %collective-permute-start.5 = (bf16[64,32,128]{2,1,0:T(8,128)(2,1)}, bf16[64,32,128]{2,1,0:T(8,128)(2,1)S(1)}, u32[]{:S(2)}, u32[]{:S(2)}) collective-permute-start(bf16[64,32,128]{2,1,0:T(8,128)(2,1)} %get-tuple-element.60), channel_id=1, source_target_pairs={{0,12},{4,8},{8,4},{12,0},{1,13},{5,9},{9,5},{13,1},{2,14},{6,10},... | collective-permute-start | bytes 1572872 | tf_op jit(solution)/shard_map/ppermute | solution.py:277
  260.0 66.9 %collective-permute-start.6 = (bf16[64,32,128]{2,1,0:T(8,128)(2,1)}, bf16[64,32,128]{2,1,0:T(8,128)(2,1)S(1)}, u32[]{:S(2)}, u32[]{:S(2)}) collective-permute-start(bf16[64,32,128]{2,1,0:T(8,128)(2,1)} %get-tuple-element.62), channel_id=1, source_target_pairs={{0,4},{4,0},{8,12},{12,8},{1,5},{5,1},{9,13},{13,9},{2,6},{6,2},{1... | collective-permute-start | bytes 1572872 | tf_op jit(solution)/shard_map/ppermute | solution.py:277
  261.2 65.8 %collective-permute-start.7 = (bf16[64,32,128]{2,1,0:T(8,128)(2,1)}, bf16[64,32,128]{2,1,0:T(8,128)(2,1)S(1)}, u32[]{:S(2)}, u32[]{:S(2)}) collective-permute-start(bf16[64,32,128]{2,1,0:T(8,128)(2,1)} %get-tuple-element.63), channel_id=1, source_target_pairs={{0,8},{4,12},{8,0},{12,4},{1,9},{5,13},{9,1},{13,5},{2,10},{6,14},... | collective-permute-start | bytes 1572872 | tf_op jit(solution)/shard_map/ppermute | solution.py:277
  264.9 92.4 %collective-permute-start.8 = (bf16[64,32,128]{2,1,0:T(8,128)(2,1)}, bf16[64,32,128]{2,1,0:T(8,128)(2,1)S(1)}, u32[]{:S(2)}, u32[]{:S(2)}) collective-permute-start(bf16[64,32,128]{2,1,0:T(8,128)(2,1)} %get-tuple-element.64), channel_id=1, source_target_pairs={{0,12},{4,8},{8,4},{12,0},{1,13},{5,9},{9,5},{13,1},{2,14},{6,10},... | collective-permute-start | bytes 1572872 | tf_op jit(solution)/shard_map/ppermute | solution.py:277
  302.5 69.9 %collective-permute-start.15 = (bf16[64,32,128]{2,1,0:T(8,128)(2,1)}, bf16[64,32,128]{2,1,0:T(8,128)(2,1)S(1)}, u32[]{:S(2)}, u32[]{:S(2)}) collective-permute-start(bf16[64,32,128]{2,1,0:T(8,128)(2,1)} %get-tuple-element.76), channel_id=1, source_target_pairs={{0,4},{4,0},{8,12},{12,8},{1,5},{5,1},{9,13},{13,9},{2,6},{6,2},{1... | collective-permute-start | bytes 1572872 | tf_op jit(solution)/shard_map/ppermute | solution.py:277
  302.6 69.8 %collective-permute-start.16 = (bf16[64,32,128]{2,1,0:T(8,128)(2,1)}, bf16[64,32,128]{2,1,0:T(8,128)(2,1)S(1)}, u32[]{:S(2)}, u32[]{:S(2)}) collective-permute-start(bf16[64,32,128]{2,1,0:T(8,128)(2,1)} %get-tuple-element.77), channel_id=1, source_target_pairs={{0,8},{4,12},{8,0},{12,4},{1,9},{5,13},{9,1},{13,5},{2,10},{6,14},... | collective-permute-start | bytes 1572872 | tf_op jit(solution)/shard_map/ppermute | solution.py:277
  326.9 53.8 %collective-permute-start.17 = (bf16[64,32,128]{2,1,0:T(8,128)(2,1)}, bf16[64,32,128]{2,1,0:T(8,128)(2,1)S(1)}, u32[]{:S(2)}, u32[]{:S(2)}) collective-permute-start(bf16[64,32,128]{2,1,0:T(8,128)(2,1)} %get-tuple-element.78), channel_id=1, source_target_pairs={{0,12},{4,8},{8,4},{12,0},{1,13},{5,9},{9,5},{13,1},{2,14},{6,10},... | collective-permute-start | bytes 1572872 | tf_op jit(solution)/shard_map/ppermute | solution.py:277
  441.1 146.1 %reduce-scatter.5.cloned.1.call-start = ((), (), s32[]{:S(2)}) async-start(), calls=%async_computation.4 | async-start | bytes 10485760 | tf_op jit(solution)/shard_map/reduce_scatter | solution.py:358
  452.3 63.8 %collective-permute-start.18 = (bf16[64,32,128]{2,1,0:T(8,128)(2,1)}, bf16[64,32,128]{2,1,0:T(8,128)(2,1)S(1)}, u32[]{:S(2)}, u32[]{:S(2)}) collective-permute-start(bf16[64,32,128]{2,1,0:T(8,128)(2,1)} %get-tuple-element.80), channel_id=1, source_target_pairs={{0,4},{4,0},{8,12},{12,8},{1,5},{5,1},{9,13},{13,9},{2,6},{6,2},{1... | collective-permute-start | bytes 1572872 | tf_op jit(solution)/shard_map/ppermute | solution.py:277
  452.3 66.0 %collective-permute-start.19 = (bf16[64,32,128]{2,1,0:T(8,128)(2,1)}, bf16[64,32,128]{2,1,0:T(8,128)(2,1)S(1)}, u32[]{:S(2)}, u32[]{:S(2)}) collective-permute-start(bf16[64,32,128]{2,1,0:T(8,128)(2,1)} %get-tuple-element.81), channel_id=1, source_target_pairs={{0,8},{4,12},{8,0},{12,4},{1,9},{5,13},{9,1},{13,5},{2,10},{6,14},... | collective-permute-start | bytes 1572872 | tf_op jit(solution)/shard_map/ppermute | solution.py:277
  454.6 135.9 %collective-permute-start.20 = (bf16[64,32,128]{2,1,0:T(8,128)(2,1)}, bf16[64,32,128]{2,1,0:T(8,128)(2,1)S(1)}, u32[]{:S(2)}, u32[]{:S(2)}) collective-permute-start(bf16[64,32,128]{2,1,0:T(8,128)(2,1)} %get-tuple-element.82), channel_id=1, source_target_pairs={{0,12},{4,8},{8,4},{12,0},{1,13},{5,9},{9,5},{13,1},{2,14},{6,10},... | collective-permute-start | bytes 1572872 | tf_op jit(solution)/shard_map/ppermute | solution.py:277
  465.5 127.1 %collective-permute-start.27 = (bf16[64,32,128]{2,1,0:T(8,128)(2,1)}, bf16[64,32,128]{2,1,0:T(8,128)(2,1)S(1)}, u32[]{:S(2)}, u32[]{:S(2)}) collective-permute-start(bf16[64,32,128]{2,1,0:T(8,128)(2,1)} %get-tuple-element.93), channel_id=1, source_target_pairs={{0,4},{4,0},{8,12},{12,8},{1,5},{5,1},{9,13},{13,9},{2,6},{6,2},{1... | collective-permute-start | bytes 1572872 | tf_op jit(solution)/shard_map/ppermute | solution.py:277
  515.9 76.8 %collective-permute-start.24 = (bf16[64,32,128]{2,1,0:T(8,128)(2,1)}, bf16[64,32,128]{2,1,0:T(8,128)(2,1)S(1)}, u32[]{:S(2)}, u32[]{:S(2)}) collective-permute-start(bf16[64,32,128]{2,1,0:T(8,128)(2,1)} %get-tuple-element.89), channel_id=1, source_target_pairs={{0,4},{4,0},{8,12},{12,8},{1,5},{5,1},{9,13},{13,9},{2,6},{6,2},{1... | collective-permute-start | bytes 1572872 | tf_op jit(solution)/shard_map/ppermute | solution.py:277
  516.2 78.0 %collective-permute-start.25 = (bf16[64,32,128]{2,1,0:T(8,128)(2,1)}, bf16[64,32,128]{2,1,0:T(8,128)(2,1)S(1)}, u32[]{:S(2)}, u32[]{:S(2)}) collective-permute-start(bf16[64,32,128]{2,1,0:T(8,128)(2,1)} %get-tuple-element.90), channel_id=1, source_target_pairs={{0,8},{4,12},{8,0},{12,4},{1,9},{5,13},{9,1},{13,5},{2,10},{6,14},... | collective-permute-start | bytes 1572872 | tf_op jit(solution)/shard_map/ppermute | solution.py:277
  518.3 77.1 %collective-permute-start.26 = (bf16[64,32,128]{2,1,0:T(8,128)(2,1)}, bf16[64,32,128]{2,1,0:T(8,128)(2,1)}, u32[]{:S(2)}, u32[]{:S(2)}) collective-permute-start(bf16[64,32,128]{2,1,0:T(8,128)(2,1)} %get-tuple-element.91), channel_id=1, source_target_pairs={{0,12},{4,8},{8,4},{12,0},{1,13},{5,9},{9,5},{13,1},{2,14},{6,10},... | collective-permute-start | bytes 1572872 | tf_op jit(solution)/shard_map/ppermute | solution.py:277
  592.7 68.1 %collective-permute-start.29 = (bf16[64,32,128]{2,1,0:T(8,128)(2,1)}, bf16[64,32,128]{2,1,0:T(8,128)(2,1)S(1)}, u32[]{:S(2)}, u32[]{:S(2)}) collective-permute-start(bf16[64,32,128]{2,1,0:T(8,128)(2,1)} %get-tuple-element.95), channel_id=1, source_target_pairs={{0,12},{4,8},{8,4},{12,0},{1,13},{5,9},{9,5},{13,1},{2,14},{6,10},... | collective-permute-start | bytes 1572872 | tf_op jit(solution)/shard_map/ppermute | solution.py:277
  592.7 68.1 %collective-permute-start.30 = (bf16[64,32,128]{2,1,0:T(8,128)(2,1)}, bf16[64,32,128]{2,1,0:T(8,128)(2,1)S(1)}, u32[]{:S(2)}, u32[]{:S(2)}) collective-permute-start(bf16[64,32,128]{2,1,0:T(8,128)(2,1)} %get-tuple-element.98), channel_id=1, source_target_pairs={{0,4},{4,0},{8,12},{12,8},{1,5},{5,1},{9,13},{13,9},{2,6},{6,2},{1... | collective-permute-start | bytes 1572872 | tf_op jit(solution)/shard_map/ppermute | solution.py:277
  594.1 77.9 %collective-permute-start.31 = (bf16[64,32,128]{2,1,0:T(8,128)(2,1)}, bf16[64,32,128]{2,1,0:T(8,128)(2,1)S(1)}, u32[]{:S(2)}, u32[]{:S(2)}) collective-permute-start(bf16[64,32,128]{2,1,0:T(8,128)(2,1)} %get-tuple-element.99), channel_id=1, source_target_pairs={{0,8},{4,12},{8,0},{12,4},{1,9},{5,13},{9,1},{13,5},{2,10},{6,14},... | collective-permute-start | bytes 1572872 | tf_op jit(solution)/shard_map/ppermute | solution.py:277
  595.3 88.0 %collective-permute-start.32 = (bf16[64,32,128]{2,1,0:T(8,128)(2,1)}, bf16[64,32,128]{2,1,0:T(8,128)(2,1)S(1)}, u32[]{:S(2)}, u32[]{:S(2)}) collective-permute-start(bf16[64,32,128]{2,1,0:T(8,128)(2,1)} %get-tuple-element.100), channel_id=1, source_target_pairs={{0,12},{4,8},{8,4},{12,0},{1,13},{5,9},{9,5},{13,1},{2,14},{6,10},... | collective-permute-start | bytes 1572872 | tf_op jit(solution)/shard_map/ppermute | solution.py:277
  (50 other events, 1807.1 us)
Sparse Core Ops, SparseCore 0:
  124.1 106.6 all-gather.1
  441.2 71.4 reduce-scatter.2
  515.4 71.7 reduce-scatter.4

commit v6 on v5

--- a/solution.py
+++ b/solution.py
@@ -111,78 +111,91 @@
 
 def gather_kernel(*refs):
     out_ref = refs[-1]
-    blocks, _, cols, _ = out_ref.shape
+    cols = refs[0].shape[2]
     for s, ref in enumerate(refs[:-1]):
-        turned = turn(ref[...]).astype(BF16)
-        for b in range(blocks):
-            out_ref[b, :, :, s * cols:(s + 1) * cols] = turned[:, b * cols:(b + 1) * cols]
-
-
-def split_kernel(in_ref, *out_refs):
+        out_ref[:, :, s * cols:(s + 1) * cols] = turn(ref[...]).astype(BF16)
+
+
+def split_kernel(terms, *refs):
+    in_refs, out_refs = refs[:terms], refs[terms:]
     cols = out_refs[0].shape[2]
     for s, ref in enumerate(out_refs):
-        ref[...] = turn(in_ref[0, :, :, s * cols:(s + 1) * cols]).astype(BF16)
-
-
-def combine_kernel(groups, partner_ref, right_ref, *refs):
-    left_refs, out_refs, left_buf, sums = refs[:groups], refs[groups:2 * groups], refs[2 * groups], refs[-1]
+        part = slice(s * cols, (s + 1) * cols)
+        total = in_refs[0][:, :, part].astype(F32)
+        for other in in_refs[1:]:
+            total += other[:, :, part].astype(F32)
+        ref[...] = turn(total.astype(BF16)).astype(BF16)
+
+
+def block_of(right_refs, chunks, u, b, c, cols):
+    parts = [ref[c] for ref in right_refs[u * chunks:(u + 1) * chunks]]
+    rows = parts[0] if chunks == 1 else jnp.concatenate(parts, axis=0)
+    return rows[b * cols:(b + 1) * cols]
+
+
+def combine_kernel(groups, peers, chunks, place_ref, *refs):
+    count = peers * chunks
+    right_refs, left_refs, out_refs = refs[:count], refs[count:count + groups], refs[count + groups:-2]
+    left_buf, sums = refs[-2:]
     rows, own, cols = left_refs[0].shape
+    span = groups // peers
     for s, ref in enumerate(left_refs):
         left_buf[:, :, s * cols:(s + 1) * cols] = turn(ref[...]).astype(BF16)
+    for n in range(groups):
+        place = place_ref[n]
+        for c in range(own):
+            sums[place, c] = dot(left_buf[c], block_of(right_refs, chunks, n // span, n % span, c, cols), 1, 1)
     for s, ref in enumerate(out_refs):
-        other = partner_ref[s]
-        for c in range(own):
-            sums[c] = dot(left_buf[c], right_ref[other, c], 1, 1)
-        ref[...] = turn(sums[...]).astype(BF16)
-
-
-def left_kernel(groups, partner_ref, right_ref, *refs):
-    grad_refs, out_refs, sums = refs[:groups], refs[groups:2 * groups], refs[-1]
+        ref[...] = turn(sums[s]).astype(BF16)
+
+
+def left_kernel(groups, peers, chunks, place_ref, *refs):
+    count = peers * chunks
+    right_refs, grad_refs, out_refs = refs[:count], refs[count:count + groups], refs[count + groups:-2]
+    grads, sums = refs[-2:]
     rows, own, cols = grad_refs[0].shape
-    grads = [turn(ref[...]).astype(BF16) for ref in grad_refs]
+    span = groups // peers
+    for s, ref in enumerate(grad_refs):
+        grads[s] = turn(ref[...]).astype(BF16)
     for c in range(own):
-        total = dot(grads[0][c], right_ref[partner_ref[0], c], 1, 0)
-        for s in range(1, groups):
-            total += dot(grads[s][c], right_ref[partner_ref[s], c], 1, 0)
+        total = 0.0
+        for n in range(groups):
+            block = block_of(right_refs, chunks, n // span, n % span, c, cols)
+            total += dot(grads[place_ref[n], c], block, 1, 0)
         sums[c] = total
     for s, ref in enumerate(out_refs):
         ref[...] = turn(sums[:, :, s * cols:(s + 1) * cols]).astype(BF16)
 
 
-def right_kernel(groups, chunks, partner_ref, *refs):
+def right_kernel(groups, peers, chunks, place_ref, *refs):
     count = groups * chunks
-    grad_refs, left_refs, out_refs, left_buf = refs[:count], refs[count:2 * count], refs[2 * count:-1], refs[-1]
+    grad_refs, left_refs, out_refs = refs[:count], refs[count:2 * count], refs[2 * count:-2]
+    grads, left_buf = refs[-2:]
     rows, own, cols = grad_refs[0].shape
-    part = out_refs[0].shape[2]
-    row_blocks = out_refs[0].shape[0]
-    span = groups // row_blocks
-    for n, ref in enumerate(left_refs):
+    span = groups // peers
+    for n, (grad_ref, left_ref) in enumerate(zip(grad_refs, left_refs)):
         piece, s = divmod(n, groups)
-        left_buf[:, piece * rows:(piece + 1) * rows, s * cols:(s + 1) * cols] = turn(ref[...]).astype(BF16)
-    for s in range(groups):
-        grads = [turn(grad_refs[piece * groups + s][...]).astype(BF16) for piece in range(chunks)]
-        grad = grads[0] if chunks == 1 else jnp.concatenate(grads, axis=1)
-        other = partner_ref[s]
-        owner = other // span
+        part = slice(piece * rows, (piece + 1) * rows)
+        grads[s, :, part] = turn(grad_ref[...]).astype(BF16)
+        left_buf[:, part, s * cols:(s + 1) * cols] = turn(left_ref[...]).astype(BF16)
+    for n in range(groups):
+        place = place_ref[n]
+        u, b = divmod(n, span)
         for c in range(own):
-            total = dot(grad[c], left_buf[c], 0, 0).astype(BF16)
-            for m in range(cols // part):
-                block = total[m * part:(m + 1) * part]
-                if span == 1:
-                    out_refs[m][owner, c] = block
-                else:
-                    chunk = (other % span) * (cols // part) + m
-                    for h, ref in enumerate(out_refs):
-
-                        @pl.when(chunk == h)
-                        def _(ref=ref, block=block, c=c):
-                            ref[owner, c] = block
+            total = dot(grads[place, c], left_buf[c], 0, 0).astype(BF16)
+            for h in range(chunks):
+                low, high = max(b * cols, h * rows), min((b + 1) * cols, (h + 1) * rows)
+                if low < high:
+                    out_refs[u * chunks + h][c, low - h * rows:high - h * rows] = total[
+                        low - b * cols:high - b * cols
+                    ]
 
 
 def local(chunks, pair, grad_out, token_mask, ln_gain, proj_weights, gate_weight, out_weight, out_gain):
     rows, cols, chans = pair.shape
     groups = lax.axis_size("ch")
-    row_blocks = lax.axis_size(ROWS)
+    sides, cores = lax.axis_size("row"), lax.axis_size("sub")
+    row_blocks = sides * cores
     own = chans // groups
     tokens = rows * row_blocks
     part_rows = rows // chunks
@@ -191,7 +204,9 @@
     step = 4 if cols % 128 == 0 and block % 4 == 0 else 1
     some = 16 if own % 16 == 0 else own
     z = lax.axis_index("ch")
-    partner = jnp.stack([z ^ s for s in range(groups)]).astype(jnp.int32)
+    span = groups // row_blocks
+    me = lax.axis_index(ROWS)
+    place = jnp.stack([z ^ ((me ^ (n // span)) * span + n % span) for n in range(groups)]).astype(jnp.int32)
 
     def mine(array, axis):
         parts = [lax.dynamic_slice_in_dim(array, (z ^ s) * own, own, axis) for s in range(groups)]
@@ -280,84 +295,121 @@
     def chan_spec(count):
         return pl.BlockSpec((count, some, cols), lambda g, *_: (0, g, 0))
 
-    def all_spec(*shape):
-        lead, tail = shape[0], shape[1:]
-        return pl.BlockSpec((lead, some) + tail, lambda g, *_: (0, g, 0, 0))
+    flat_spec = pl.BlockSpec((some, part_rows, tokens), lambda g, *_: (g, 0, 0))
+    flat_shape = jax.ShapeDtypeStruct((own, part_rows, tokens), BF16)
 
     def gather(got):
         return pl.pallas_call(
             gather_kernel,
             grid=(own // some,),
-            in_specs=[chan_spec(rows)] * groups,
-            out_specs=all_spec(rows // cols, cols, tokens),
-            out_shape=jax.ShapeDtypeStruct((rows // cols, own, cols, tokens), BF16),
-            compiler_params=params,
-            cost_estimate=cost(0, 4),
+            in_specs=[chan_spec(part_rows)] * groups,
+            out_specs=flat_spec,
+            out_shape=flat_shape,
+            compiler_params=params,
+            cost_estimate=cost(0, 2),
         )(*got)
 
-    def split(array):
-        return pl.pallas_call(
-            split_kernel,
+    def split(terms):
+        return pl.pallas_call(
+            functools.partial(split_kernel, len(terms)),
             grid=(own // some,),
-            in_specs=[all_spec(1, part_rows, tokens)],
+            in_specs=[flat_spec] * len(terms),
             out_specs=[chan_spec(part_rows)] * groups,
             out_shape=pieces(part_rows),
             compiler_params=params,
-            cost_estimate=cost(0, 2),
-        )(array)
+            cost_estimate=cost(0, 1 + len(terms)),
+        )(*terms)
+
+    def swap(array, axis, by):
+        return lax.ppermute(array, axis, [(a, a ^ by) for a in range(lax.axis_size(axis))])
+
+    def all_rows(array):
+        blocks = []
+        for x in range(sides):
+            came = swap(array, "row", x) if x else array
+            blocks += [swap(came, "sub", c) if c else came for c in range(cores)]
+        return blocks
+
+    def own_rows(partials):
+        terms = []
+        for x in range(sides):
+            of_cores = [swap(partials[x * cores + c], "sub", c) if c else partials[x * cores] for c in range(cores)]
+            if x:
+                total = sum(term.astype(F32) for term in of_cores).astype(BF16)
+                terms.append(swap(total, "row", x))
+            else:
+                terms += of_cores
+        return terms
 
     product = 2 * part_rows * tokens * tokens * own
 
     def with_right(kernel, got, scratch):
         return pl.pallas_call(
-            functools.partial(kernel, groups),
+            functools.partial(kernel, groups, row_blocks, chunks),
             grid_spec=pltpu.PrefetchScalarGridSpec(
                 num_scalar_prefetch=1, grid=(own // some,),
-                in_specs=[all_spec(groups, cols, tokens)] + [chan_spec(part_rows)] * groups,
+                in_specs=[flat_spec] * (row_blocks * chunks) + [chan_spec(part_rows)] * groups,
                 out_specs=[chan_spec(part_rows)] * groups,
                 scratch_shapes=scratch,
             ),
             out_shape=pieces(part_rows),
             compiler_params=params,
             cost_estimate=cost(product, 2 + row_blocks * chunks),
-        )(partner, right, *got)
+        )(place, *right, *got)
 
     def combine(left):
         return with_right(combine_kernel, left, [
-            pltpu.VMEM((some, part_rows, tokens), BF16), pltpu.VMEM((some, part_rows, cols), F32)
+            pltpu.VMEM((some, part_rows, tokens), BF16), pltpu.VMEM((groups, some, part_rows, cols), F32)
         ])
 
     def left_back(grad):
-        return with_right(left_kernel, grad, [pltpu.VMEM((some, part_rows, tokens), F32)])
+        return with_right(left_kernel, grad, [
+            pltpu.VMEM((groups, some, part_rows, cols), BF16), pltpu.VMEM((some, part_rows, tokens), F32)
+        ])
 
     def right_back(grads, lefts):
-        return pl.pallas_call(
-            functools.partial(right_kernel, groups, chunks),
+        count = row_blocks * chunks
+        out = pl.pallas_call(
+            functools.partial(right_kernel, groups, row_blocks, chunks),
             grid_spec=pltpu.PrefetchScalarGridSpec(
                 num_scalar_prefetch=1, grid=(own // some,),
                 in_specs=[chan_spec(part_rows)] * (2 * groups * chunks),
-                out_specs=[all_spec(row_blocks, part_rows, tokens)] * chunks,
-                scratch_shapes=[pltpu.VMEM((some, rows, tokens), BF16)],
+                out_specs=[flat_spec] * count,
+                scratch_shapes=[
+                    pltpu.VMEM((groups, some, rows, cols), BF16), pltpu.VMEM((some, rows, tokens), BF16)
+                ],
             ),
-            out_shape=[jax.ShapeDtypeStruct((row_blocks, own, part_rows, tokens), BF16)] * chunks,
+            out_shape=[flat_shape] * count,
             compiler_params=params,
             cost_estimate=cost(product * chunks, (2 + row_blocks) * chunks),
-        )(partner, *sum(grads, []), *sum(lefts, []))
+        )(place, *sum(grads, []), *sum(lefts, []))
+        return [out[h::chunks] for h in range(chunks)]
+
+    def tie(*lists):
+        values = iter(lax.optimization_barrier(tuple(sum(lists, []))))
+        return [[next(values) for _ in part] for part in lists]
 
     firsts = [p * blocks for p in range(chunks)]
-    right = gather(exchange(project(right_w, 0, rows // block)))
-    right = lax.all_gather(right, ROWS, axis=0, tiled=True)
-    lefts = [exchange(project(left_w, first, blocks)) for first in firsts]
-    sigms, left_grads, grads = [], [], []
+    sent = [list(project(weight, first, blocks)) for weight in (right_w, left_w) for first in firsts]
+    halves, gathered = [], []
+    for part in range(chunks):
+        got = exchange(sent[part])
+        got = tie(got, gathered, *sent[part + 1:part + 1 + chunks])[0]
+        gathered = [gather(got)]
+        halves.append(all_rows(gathered[0]))
+    right = [half[u] for u in range(row_blocks) for half in halves]
+    lefts = [exchange(pieces_of) for pieces_of in sent[chunks:]]
+    sigms, grads, backs = [], [], []
     for first, left in zip(firsts, lefts):
         *grad_comb, sigm = middle(exchange(combine(left)), first)
         sigms.append(sigm)
         grads.append(exchange(grad_comb))
-        left_grads.append(exchange(left_back(grads[-1])))
-    right_grads = [
-        exchange(split(lax.psum_scatter(array, ROWS, scatter_dimension=0, tiled=True)))
-        for array in right_back(grads, lefts)
-    ]
+    for part in range(chunks):
+        backs.append(list(left_back(grads[part])))
+        if part == 0 and chunks > 1:
+            grads[-1] = tie(grads[-1], backs[0])[0]
+    left_grads = [exchange(back) for back in backs]
+    right_grads = [exchange(split(own_rows(partials))) for partials in right_back(grads, lefts)]
     out = jnp.zeros((rows, cols, chans), BF16)
     for first, left_grad, right_grad, sigm in zip(firsts, left_grads, right_grads, sigms):
         out = last(left_grad, right_grad, sigm, first, out)

time: 709 us -> 736 us (1.038)
  waiting for transfers between devices: 466 us -> 497 us
  between operations: 13.4 us -> 0.38 us
    ppermute x0 -> x12, waiting for transfers between devices: none -> 155 us  [swap(): lax.ppermute(array, axis, [(a, a ^ by) for a in range(lax.axis_size(axis))])]
    reduce_scatter x2 -> x0, waiting for transfers between devices: 115 us -> none  [local(): lax.psum_scatter(array, ROWS, scatter_dimension=0, tiled=True)]
    all_gather x1 -> x0, waiting for transfers between devices: 51.2 us -> none  [local(): right = lax.all_gather(right, ROWS, axis=0, tiled=True)]
    ppermute x33 -> x36, waiting for transfers between devices: 299 us -> 342 us  [exchange(): lax.ppermute(sent[s], 'ch', [(a, a ^ s) for a in range(groups)])]
    ppermute x33 -> x36, starting transfers between devices: 54.6 us -> 36.8 us  [exchange(): lax.ppermute(sent[s], 'ch', [(a, a ^ s) for a in range(groups)])]
    ppermute x0 -> x12, starting transfers between devices: none -> 16.7 us  [swap(): lax.ppermute(array, axis, [(a, a ^ by) for a in range(lax.axis_size(axis))])]
    pallas_call x8 -> x9, Pallas kernels: 70.6 us -> 75.8 us  [the longest x4 45.2 us: with_right(): pl.pallas_call(functools.partial(kernel, groups, row_blocks, chunks), gri...]
    pallas_call x3 -> x4, Pallas kernels: 31 us -> 31.9 us  [project(): pl.pallas_call(functools.partial(project_kernel, step), grid=(count,), in...]
  transfers between devices with their start and end apart: 36 -> 48, of which waited for: 20 -> 26; matrix products, arithmetic and copies ran while one was open for 1% -> 2% of each run, Pallas kernels for 15% -> 16%
where the time goes in v6:
time: 736 us; the launch traced here: 735 us
  waiting for transfers between devices  497 us (68%)
  Pallas kernels  159 us (22%)
  starting transfers between devices  53.5 us (7%)
  local copies, waits for them, and re-layouts  15.5 us (2%)
  other arithmetic  8.86 us (1%)
    ppermute x36, waiting for transfers between devices, exchange(): lax.ppermute(sent[s], 'ch', [(a, a ^ s) for a in range(groups)])  342 us
    ppermute x12, waiting for transfers between devices, swap(): lax.ppermute(array, axis, [(a, a ^ by) for a in range(lax.axis_size(axis))])  155 us
    pallas_call x4, Pallas kernels, with_right(): pl.pallas_call(functools.partial(kernel, groups, row_blocks, chunks), gri...  45.2 us
    ppermute x36, starting transfers between devices, exchange(): lax.ppermute(sent[s], 'ch', [(a, a ^ s) for a in range(groups)])  36.8 us
    pallas_call x4, Pallas kernels, project(): pl.pallas_call(functools.partial(project_kernel, step), grid=(count,), in...  31.9 us
    pallas_call x2, Pallas kernels, last(): pl.pallas_call(functools.partial(last_kernel, step, groups), grid=(blocks...  29.8 us
    pallas_call x2, Pallas kernels, middle(): pl.pallas_call(functools.partial(middle_kernel, step, groups), grid=(bloc...  21.8 us
    ppermute x12, starting transfers between devices, swap(): lax.ppermute(array, axis, [(a, a ^ by) for a in range(lax.axis_size(axis))])  16.7 us
  transfers between devices with their start and end apart: 48, of which 26 were waited for; matrix products, arithmetic and copies ran while one was open for 2% of the time, Pallas kernels for 16%

profile of v6, /device:TPU:15, one launch (start us, length us, event | category | flops | bytes accessed | tf_op | source)
XLA Modules:
  0.0 734.8 jit_solution(10432004952368996462)
XLA Ops:
  63.7 28.8 %collective-permute-done.4.refs_2_ = bf16[64,32,128]{2,1,0:T(8,128)(2,1)S(1)} collective-permute-done((bf16[64,32,128]{2,1,0:T(8,128)(2,1)}, bf16[64,32,128]{2,1,0:T(8,128)(2,1)S(1)}, u32[]{:S(2)}, u32[]{:S(2)}) %collective-permute-start.4) | collective-permute-done | bytes 524320 | tf_op jit(solution)/shard_map/ppermute | solution.py:292
  92.5 12.0 %collective-permute-done.5.refs_3_ = bf16[64,32,128]{2,1,0:T(8,128)(2,1)S(1)} collective-permute-done((bf16[64,32,128]{2,1,0:T(8,128)(2,1)}, bf16[64,32,128]{2,1,0:T(8,128)(2,1)S(1)}, u32[]{:S(2)}, u32[]{:S(2)}) %collective-permute-start.5) | collective-permute-done | bytes 524320 | tf_op jit(solution)/shard_map/ppermute | solution.py:292
  112.8 41.8 %collective-permute-done.9.refs_5_ = bf16[32,64,512]{2,1,0:T(8,128)(2,1)} collective-permute-done((bf16[32,64,512]{2,1,0:T(8,128)(2,1)}, bf16[32,64,512]{2,1,0:T(8,128)(2,1)}, u32[]{:S(2)}, u32[]{:S(2)}) %collective-permute-start.9) | collective-permute-done | bytes 2097184 | tf_op jit(solution)/shard_map/ppermute | solution.py:324
  159.6 39.9 %collective-permute-done.8.refs_4_ = bf16[32,64,512]{2,1,0:T(8,128)(2,1)} collective-permute-done((bf16[32,64,512]{2,1,0:T(8,128)(2,1)S(1)}, bf16[32,64,512]{2,1,0:T(8,128)(2,1)}, u32[]{:S(2)}, u32[]{:S(2)}) %collective-permute-start.8) | collective-permute-done | bytes 2097184 | tf_op jit(solution)/shard_map/ppermute | solution.py:324
  202.2 13.6 %collective-permute-done.18.refs_9_ = bf16[64,32,128]{2,1,0:T(8,128)(2,1)S(1)} collective-permute-done((bf16[64,32,128]{2,1,0:T(8,128)(2,1)S(1)}, bf16[64,32,128]{2,1,0:T(8,128)(2,1)S(1)}, u32[]{:S(2)}, u32[]{:S(2)}) %collective-permute-start.18) | collective-permute-done | bytes 524320 | tf_op jit(solution)/shard_map/ppermute | solution.py:292
  217.0 21.9 %collective-permute-done.19.refs_10_ = bf16[64,32,128]{2,1,0:T(8,128)(2,1)S(1)} collective-permute-done((bf16[64,32,128]{2,1,0:T(8,128)(2,1)S(1)}, bf16[64,32,128]{2,1,0:T(8,128)(2,1)S(1)}, u32[]{:S(2)}, u32[]{:S(2)}) %collective-permute-start.19) | collective-permute-done | bytes 524320 | tf_op jit(solution)/shard_map/ppermute | solution.py:292
  239.1 22.9 %collective-permute-done.20.refs_11_ = bf16[64,32,128]{2,1,0:T(8,128)(2,1)} collective-permute-done((bf16[64,32,128]{2,1,0:T(8,128)(2,1)S(1)}, bf16[64,32,128]{2,1,0:T(8,128)(2,1)}, u32[]{:S(2)}, u32[]{:S(2)}) %collective-permute-start.20) | collective-permute-done | bytes 524320 | tf_op jit(solution)/shard_map/ppermute | solution.py:292
  267.3 12.4 %shard_map.90 = (bf16[64,32,128]{2,1,0:T(8,128)(2,1)}, bf16[64,32,128]{2,1,0:T(8,128)(2,1)}, bf16[64,32,128]{2,1,0:T(8,128)(2,1)}, bf16[64,32,128]{2,1,0:T(8,128)(2,1)}) custom-call(s32[4]{0:T(128)} %pad_add_fusion.place_ref, bf16[32,64,512]{2,1,0:T(8,128)(2,1)} %shard_map.85.refs_0_, bf16[32,64,512]{2,1,0:T(8,128)(2,1)} %shard_map.87.refs_1_, ...), custom_call_target="tpu_custom_call" | custom-call | flops 1073741824 | bytes 20971520 | tf_op jit(solution)/shard_map/pallas_call | solution.py:347
  284.6 11.6 %collective-permute-done.13.refs_10_.refs_14_ = bf16[64,32,128]{2,1,0:T(8,128)(2,1)} collective-permute-done((bf16[64,32,128]{2,1,0:T(8,128)(2,1)}, bf16[64,32,128]{2,1,0:T(8,128)(2,1)}, u32[]{:S(2)}, u32[]{:S(2)}) %collective-permute-start.13) | collective-permute-done | bytes 524320 | tf_op jit(solution)/shard_map/ppermute | solution.py:292
  296.3 36.3 %collective-permute-done.14.refs_11_.refs_15_ = bf16[64,32,128]{2,1,0:T(8,128)(2,1)S(1)} collective-permute-done((bf16[64,32,128]{2,1,0:T(8,128)(2,1)}, bf16[64,32,128]{2,1,0:T(8,128)(2,1)S(1)}, u32[]{:S(2)}, u32[]{:S(2)}) %collective-permute-start.14) | collective-permute-done | bytes 524320 | tf_op jit(solution)/shard_map/ppermute | solution.py:292
  333.4 12.3 %shard_map.88 = (bf16[64,32,128]{2,1,0:T(8,128)(2,1)}, bf16[64,32,128]{2,1,0:T(8,128)(2,1)}, bf16[64,32,128]{2,1,0:T(8,128)(2,1)}, bf16[64,32,128]{2,1,0:T(8,128)(2,1)}) custom-call(s32[4]{0:T(128)} %pad_add_fusion.place_ref, bf16[32,64,512]{2,1,0:T(8,128)(2,1)} %shard_map.85.refs_0_, bf16[32,64,512]{2,1,0:T(8,128)(2,1)} %shard_map.87.refs_1_, ...), custom_call_target="tpu_custom_call" | custom-call | flops 1073741824 | bytes 20971520 | tf_op jit(solution)/shard_map/pallas_call | solution.py:347
  374.0 22.0 %collective-permute-done.16.refs_2_ = bf16[64,32,128]{2,1,0:T(8,128)(2,1)S(1)} collective-permute-done((bf16[64,32,128]{2,1,0:T(8,128)(2,1)}, bf16[64,32,128]{2,1,0:T(8,128)(2,1)S(1)}, u32[]{:S(2)}, u32[]{:S(2)}) %collective-permute-start.16) | collective-permute-done | bytes 524320 | tf_op jit(solution)/shard_map/ppermute | solution.py:292
  396.1 26.7 %collective-permute-done.17.refs_3_ = bf16[64,32,128]{2,1,0:T(8,128)(2,1)S(1)} collective-permute-done((bf16[64,32,128]{2,1,0:T(8,128)(2,1)}, bf16[64,32,128]{2,1,0:T(8,128)(2,1)S(1)}, u32[]{:S(2)}, u32[]{:S(2)}) %collective-permute-start.17) | collective-permute-done | bytes 524320 | tf_op jit(solution)/shard_map/ppermute | solution.py:292
  437.7 11.6 %collective-permute-done.26.refs_11_.refs_3_ = bf16[64,32,128]{2,1,0:T(8,128)(2,1)S(1)} collective-permute-done((bf16[64,32,128]{2,1,0:T(8,128)(2,1)}, bf16[64,32,128]{2,1,0:T(8,128)(2,1)S(1)}, u32[]{:S(2)}, u32[]{:S(2)}) %collective-permute-start.26) | collective-permute-done | bytes 524320 | tf_op jit(solution)/shard_map/ppermute | solution.py:292
  460.3 18.4 %collective-permute-done.31.refs_6_.refs_10_ = bf16[64,32,128]{2,1,0:T(8,128)(2,1)S(1)} collective-permute-done((bf16[64,32,128]{2,1,0:T(8,128)(2,1)}, bf16[64,32,128]{2,1,0:T(8,128)(2,1)S(1)}, u32[]{:S(2)}, u32[]{:S(2)}) %collective-permute-start.31) | collective-permute-done | bytes 524320 | tf_op jit(solution)/shard_map/ppermute | solution.py:292
  491.0 14.4 %shard_map.93 = (bf16[32,64,512]{2,1,0:T(8,128)(2,1)}, bf16[32,64,512]{2,1,0:T(8,128)(2,1)}, bf16[32,64,512]{2,1,0:T(8,128)(2,1)}, bf16[32,64,512]{2,1,0:T(8,128...) custom-call(s32[4]{0:T(128)} %pad_add_fusion.place_ref, ...), custom_call_target="tpu_custom_call" | custom-call | flops 2147483648 | bytes 25165824 | tf_op jit(solution)/shard_map/pallas_call | solution.py:372
  533.0 31.1 %collective-permute-done.35.refs_2_ = bf16[32,64,512]{2,1,0:T(8,128)(2,1)} collective-permute-done((bf16[32,64,512]{2,1,0:T(8,128)(2,1)}, bf16[32,64,512]{2,1,0:T(8,128)(2,1)}, u32[]{:S(2)}, u32[]{:S(2)}) %collective-permute-start.35) | collective-permute-done | bytes 2097184 | tf_op jit(solution)/shard_map/ppermute | solution.py:324
  571.7 37.3 %collective-permute-done.44.refs_2_ = bf16[32,64,512]{2,1,0:T(8,128)(2,1)S(1)} collective-permute-done((bf16[32,64,512]{2,1,0:T(8,128)(2,1)S(1)}, bf16[32,64,512]{2,1,0:T(8,128)(2,1)S(1)}, u32[]{:S(2)}, u32[]{:S(2)}) %collective-permute-start.44) | collective-permute-done | bytes 2097184 | tf_op jit(solution)/shard_map/ppermute | solution.py:324
  619.7 32.6 %collective-permute-done.38.refs_7_ = bf16[64,32,128]{2,1,0:T(8,128)(2,1)S(1)} collective-permute-done((bf16[64,32,128]{2,1,0:T(8,128)(2,1)}, bf16[64,32,128]{2,1,0:T(8,128)(2,1)S(1)}, u32[]{:S(2)}, u32[]{:S(2)}) %collective-permute-start.38) | collective-permute-done | bytes 524320 | tf_op jit(solution)/shard_map/ppermute | solution.py:292
  657.1 14.9 %shard_map.95.held_ref = bf16[128,128,128]{2,1,0:T(8,128)(2,1)} custom-call(bf16[128,128,128]{2,1,0:T(8,128)(2,1)} %pair_ref.15, bf16[64,128,128]{2,1,0:T(8,128)(2,1)} %get-tuple-element.108.sigm_ref, f32[16,1,1024]{2,1,0:T(1,128)} %broadcast_multiply_fusion.mask_ref, f32[1,128]{1,0:T(1,128)} %bitcast.39, ...), custom_call_target="tpu_custom_call", output_to_operand_aliasing={{}: (5, {})} | custom-call | flops 2415919104 | bytes 10485760 | tf_op jit(solution)/shard_map/pallas_call | solution.py:278
  672.0 12.5 %collective-permute-done.40.refs_2_ = bf16[64,32,128]{2,1,0:T(8,128)(2,1)S(1)} collective-permute-done((bf16[64,32,128]{2,1,0:T(8,128)(2,1)}, bf16[64,32,128]{2,1,0:T(8,128)(2,1)S(1)}, u32[]{:S(2)}, u32[]{:S(2)}) %collective-permute-start.40) | collective-permute-done | bytes 524320 | tf_op jit(solution)/shard_map/ppermute | solution.py:292
  684.4 12.1 %collective-permute-done.41.refs_3_ = bf16[64,32,128]{2,1,0:T(8,128)(2,1)S(1)} collective-permute-done((bf16[64,32,128]{2,1,0:T(8,128)(2,1)}, bf16[64,32,128]{2,1,0:T(8,128)(2,1)S(1)}, u32[]{:S(2)}, u32[]{:S(2)}) %collective-permute-start.41) | collective-permute-done | bytes 524320 | tf_op jit(solution)/shard_map/ppermute | solution.py:292
  706.9 12.1 %collective-permute-done.47.refs_7_ = bf16[64,32,128]{2,1,0:T(8,128)(2,1)S(1)} collective-permute-done((bf16[64,32,128]{2,1,0:T(8,128)(2,1)}, bf16[64,32,128]{2,1,0:T(8,128)(2,1)S(1)}, u32[]{:S(2)}, u32[]{:S(2)}) %collective-permute-start.47) | collective-permute-done | bytes 524320 | tf_op jit(solution)/shard_map/ppermute | solution.py:292
  719.8 14.9 %shard_map.98 = bf16[128,128,128]{2,1,0:T(8,128)(2,1)} custom-call(bf16[128,128,128]{2,1,0:T(8,128)(2,1)} %pair_ref.15, bf16[64,128,128]{2,1,0:T(8,128)(2,1)} %get-tuple-element.103.sigm_ref, f32[16,1,1024]{2,1,0:T(1,128)} %broadcast_multiply_fusion.mask_ref, f32[1,128]{1,0:T(1,128)} %bitcast.40, ...), custom_call_target="tpu_custom_call", output_to_operand_aliasing={{}: (5, {})} | custom-call | flops 2415919104 | bytes 10485760 | tf_op jit(solution)/shard_map/pallas_call | solution.py:278
  (206 shorter events, 220.2 us)
Async XLA Ops:
  23.7 68.8 %collective-permute-start.4 = (bf16[64,32,128]{2,1,0:T(8,128)(2,1)}, bf16[64,32,128]{2,1,0:T(8,128)(2,1)S(1)}, u32[]{:S(2)}, u32[]{:S(2)}) collective-permute-start(bf16[64,32,128]{2,1,0:T(8,128)(2,1)} %get-tuple-element.81), channel_id=1, source_target_pairs={{0,8},{4,12},{8,0},{12,4},{1,9},{5,13},{9,1},{13,5},{2,10},{6,14},... | collective-permute-start | bytes 1572872 | tf_op jit(solution)/shard_map/ppermute | solution.py:292
  33.5 71.1 %collective-permute-start.5 = (bf16[64,32,128]{2,1,0:T(8,128)(2,1)}, bf16[64,32,128]{2,1,0:T(8,128)(2,1)S(1)}, u32[]{:S(2)}, u32[]{:S(2)}) collective-permute-start(bf16[64,32,128]{2,1,0:T(8,128)(2,1)} %get-tuple-element.82), channel_id=1, source_target_pairs={{0,12},{4,8},{8,4},{12,0},{1,13},{5,9},{9,5},{13,1},{2,14},{6,10},... | collective-permute-start | bytes 1572872 | tf_op jit(solution)/shard_map/ppermute | solution.py:292
  109.2 90.3 %collective-permute-start.8 = (bf16[32,64,512]{2,1,0:T(8,128)(2,1)S(1)}, bf16[32,64,512]{2,1,0:T(8,128)(2,1)}, u32[]{:S(2)}, u32[]{:S(2)}) collective-permute-start(bf16[32,64,512]{2,1,0:T(8,128)(2,1)S(1)} %copy-done), channel_id=1, source_target_pairs={{0,2},{2,0},{1,3},{3,1},{4,6},{6,4},{5,7},{7,5},{8,10},{10,8},{9,1... | collective-permute-start | bytes 6291464 | tf_op jit(solution)/shard_map/ppermute | solution.py:324
  110.4 154.3 %collective-permute-start.7 = (bf16[32,64,512]{2,1,0:T(8,128)(2,1)}, bf16[32,64,512]{2,1,0:T(8,128)(2,1)}, u32[]{:S(2)}, u32[]{:S(2)}) collective-permute-start(bf16[32,64,512]{2,1,0:T(8,128)(2,1)} %shard_map.87.refs_1_), channel_id=1, source_target_pairs={{0,1},{1,0},{2,3},{3,2},{4,5},{5,4},{6,7},{7,6},{8,9},{9,8},{10,11... | collective-permute-start | bytes 6291464 | tf_op jit(solution)/shard_map/ppermute | solution.py:324
  112.8 154.2 %collective-permute-start.6 = (bf16[32,64,512]{2,1,0:T(8,128)(2,1)S(1)}, bf16[32,64,512]{2,1,0:T(8,128)(2,1)}, u32[]{:S(2)}, u32[]{:S(2)}) collective-permute-start(bf16[32,64,512]{2,1,0:T(8,128)(2,1)S(1)} %copy-done), channel_id=1, source_target_pairs={{0,1},{1,0},{2,3},{3,2},{4,5},{5,4},{6,7},{7,6},{8,9},{9,8},{10,11... | collective-permute-start | bytes 6291464 | tf_op jit(solution)/shard_map/ppermute | solution.py:324
  154.5 112.8 %collective-permute-start.11 = (bf16[32,64,512]{2,1,0:T(8,128)(2,1)}, bf16[32,64,512]{2,1,0:T(8,128)(2,1)}, u32[]{:S(2)}, u32[]{:S(2)}) collective-permute-start(bf16[32,64,512]{2,1,0:T(8,128)(2,1)} %collective-permute-done.9.refs_5_), channel_id=1, source_target_pairs={{0,1},{1,0},{2,3},{3,2},{4,5},{5,4},{6,7},{7,6},{8,9},{9,8},{10,11... | collective-permute-start | bytes 6291464 | tf_op jit(solution)/shard_map/ppermute | solution.py:324
  199.5 67.8 %collective-permute-start.10 = (bf16[32,64,512]{2,1,0:T(8,128)(2,1)}, bf16[32,64,512]{2,1,0:T(8,128)(2,1)}, u32[]{:S(2)}, u32[]{:S(2)}) collective-permute-start(bf16[32,64,512]{2,1,0:T(8,128)(2,1)} %collective-permute-done.8.refs_4_), channel_id=1, source_target_pairs={{0,1},{1,0},{2,3},{3,2},{4,5},{5,4},{6,7},{7,6},{8,9},{9,8},{10,11... | collective-permute-start | bytes 6291464 | tf_op jit(solution)/shard_map/ppermute | solution.py:324
  267.0 65.6 %collective-permute-start.14 = (bf16[64,32,128]{2,1,0:T(8,128)(2,1)}, bf16[64,32,128]{2,1,0:T(8,128)(2,1)S(1)}, u32[]{:S(2)}, u32[]{:S(2)}) collective-permute-start(bf16[64,32,128]{2,1,0:T(8,128)(2,1)} %get-tuple-element.94), channel_id=1, source_target_pairs={{0,12},{4,8},{8,4},{12,0},{1,13},{5,9},{9,5},{13,1},{2,14},{6,10},... | collective-permute-start | bytes 1572872 | tf_op jit(solution)/shard_map/ppermute | solution.py:292
  279.7 69.4 %collective-permute-start.21 = (bf16[64,32,128]{2,1,0:T(8,128)(2,1)}, bf16[64,32,128]{2,1,0:T(8,128)(2,1)S(1)}, u32[]{:S(2)}, u32[]{:S(2)}) collective-permute-start(bf16[64,32,128]{2,1,0:T(8,128)(2,1)} %get-tuple-element.105), channel_id=1, source_target_pairs={{0,4},{4,0},{8,12},{12,8},{1,5},{5,1},{9,13},{13,9},{2,6},{6,2},{1... | collective-permute-start | bytes 1572872 | tf_op jit(solution)/shard_map/ppermute | solution.py:292
  280.7 68.4 %collective-permute-start.22 = (bf16[64,32,128]{2,1,0:T(8,128)(2,1)}, bf16[64,32,128]{2,1,0:T(8,128)(2,1)S(1)}, u32[]{:S(2)}, u32[]{:S(2)}) collective-permute-start(bf16[64,32,128]{2,1,0:T(8,128)(2,1)} %get-tuple-element.106), channel_id=1, source_target_pairs={{0,8},{4,12},{8,0},{12,4},{1,9},{5,13},{9,1},{13,5},{2,10},{6,14},... | collective-permute-start | bytes 1572872 | tf_op jit(solution)/shard_map/ppermute | solution.py:292
  282.1 76.4 %collective-permute-start.23 = (bf16[64,32,128]{2,1,0:T(8,128)(2,1)}, bf16[64,32,128]{2,1,0:T(8,128)(2,1)S(1)}, u32[]{:S(2)}, u32[]{:S(2)}) collective-permute-start(bf16[64,32,128]{2,1,0:T(8,128)(2,1)} %get-tuple-element.107), channel_id=1, source_target_pairs={{0,12},{4,8},{8,4},{12,0},{1,13},{5,9},{9,5},{13,1},{2,14},{6,10},... | collective-permute-start | bytes 1572872 | tf_op jit(solution)/shard_map/ppermute | solution.py:292
  349.1 73.7 %collective-permute-start.17 = (bf16[64,32,128]{2,1,0:T(8,128)(2,1)}, bf16[64,32,128]{2,1,0:T(8,128)(2,1)S(1)}, u32[]{:S(2)}, u32[]{:S(2)}) collective-permute-start(bf16[64,32,128]{2,1,0:T(8,128)(2,1)} %get-tuple-element.102), channel_id=1, source_target_pairs={{0,12},{4,8},{8,4},{12,0},{1,13},{5,9},{9,5},{13,1},{2,14},{6,10},... | collective-permute-start | bytes 1572872 | tf_op jit(solution)/shard_map/ppermute | solution.py:292
  370.2 67.5 %collective-permute-start.24 = (bf16[64,32,128]{2,1,0:T(8,128)(2,1)}, bf16[64,32,128]{2,1,0:T(8,128)(2,1)S(1)}, u32[]{:S(2)}, u32[]{:S(2)}) collective-permute-start(bf16[64,32,128]{2,1,0:T(8,128)(2,1)} %get-tuple-element.110), channel_id=1, source_target_pairs={{0,4},{4,0},{8,12},{12,8},{1,5},{5,1},{9,13},{13,9},{2,6},{6,2},{1... | collective-permute-start | bytes 1572872 | tf_op jit(solution)/shard_map/ppermute | solution.py:292
  370.3 67.4 %collective-permute-start.25 = (bf16[64,32,128]{2,1,0:T(8,128)(2,1)}, bf16[64,32,128]{2,1,0:T(8,128)(2,1)S(1)}, u32[]{:S(2)}, u32[]{:S(2)}) collective-permute-start(bf16[64,32,128]{2,1,0:T(8,128)(2,1)} %get-tuple-element.111), channel_id=1, source_target_pairs={{0,8},{4,12},{8,0},{12,4},{1,9},{5,13},{9,1},{13,5},{2,10},{6,14},... | collective-permute-start | bytes 1572872 | tf_op jit(solution)/shard_map/ppermute | solution.py:292
  374.0 75.3 %collective-permute-start.26 = (bf16[64,32,128]{2,1,0:T(8,128)(2,1)}, bf16[64,32,128]{2,1,0:T(8,128)(2,1)S(1)}, u32[]{:S(2)}, u32[]{:S(2)}) collective-permute-start(bf16[64,32,128]{2,1,0:T(8,128)(2,1)} %get-tuple-element.112), channel_id=1, source_target_pairs={{0,12},{4,8},{8,4},{12,0},{1,13},{5,9},{9,5},{13,1},{2,14},{6,10},... | collective-permute-start | bytes 1572872 | tf_op jit(solution)/shard_map/ppermute | solution.py:292
  437.6 52.5 %collective-permute-start.32 = (bf16[64,32,128]{2,1,0:T(8,128)(2,1)}, bf16[64,32,128]{2,1,0:T(8,128)(2,1)S(1)}, u32[]{:S(2)}, u32[]{:S(2)}) collective-permute-start(bf16[64,32,128]{2,1,0:T(8,128)(2,1)} %get-tuple-element.120), channel_id=1, source_target_pairs={{0,12},{4,8},{8,4},{12,0},{1,13},{5,9},{9,5},{13,1},{2,14},{6,10},... | collective-permute-start | bytes 1572872 | tf_op jit(solution)/shard_map/ppermute | solution.py:292
  509.7 61.9 %collective-permute-start.42 = (bf16[32,64,512]{2,1,0:T(8,128)(2,1)}, bf16[32,64,512]{2,1,0:T(8,128)(2,1)S(1)}, u32[]{:S(2)}, u32[]{:S(2)}) collective-permute-start(bf16[32,64,512]{2,1,0:T(8,128)(2,1)} %get-tuple-element.138), channel_id=1, source_target_pairs={{0,1},{1,0},{2,3},{3,2},{4,5},{5,4},{6,7},{7,6},{8,9},{9,8},{10,11... | collective-permute-start | bytes 6291464 | tf_op jit(solution)/shard_map/ppermute | solution.py:324
  520.0 89.0 %collective-permute-start.44 = (bf16[32,64,512]{2,1,0:T(8,128)(2,1)S(1)}, bf16[32,64,512]{2,1,0:T(8,128)(2,1)S(1)}, u32[]{:S(2)}, u32[]{:S(2)}) collective-permute-start(bf16[32,64,512]{2,1,0:T(8,128)(2,1)S(1)} %add_convert_fusion), channel_id=1, source_target_pairs={{0,2},{2,0},{1,3},{3,1},{4,6},{6,4},{5,7},{7,5},{8,10},{10,8},{9,1... | collective-permute-start | bytes 6291464 | tf_op jit(solution)/shard_map/ppermute | solution.py:324
  564.2 51.0 %collective-permute-start.29 = (bf16[64,32,128]{2,1,0:T(8,128)(2,1)}, bf16[64,32,128]{2,1,0:T(8,128)(2,1)}, u32[]{:S(2)}, u32[]{:S(2)}) collective-permute-start(bf16[64,32,128]{2,1,0:T(8,128)(2,1)} %get-tuple-element.116), channel_id=1, source_target_pairs={{0,12},{4,8},{8,4},{12,0},{1,13},{5,9},{9,5},{13,1},{2,14},{6,10},... | collective-permute-start | bytes 1572872 | tf_op jit(solution)/shard_map/ppermute | solution.py:292
  615.1 69.3 %collective-permute-start.40 = (bf16[64,32,128]{2,1,0:T(8,128)(2,1)}, bf16[64,32,128]{2,1,0:T(8,128)(2,1)S(1)}, u32[]{:S(2)}, u32[]{:S(2)}) collective-permute-start(bf16[64,32,128]{2,1,0:T(8,128)(2,1)} %get-tuple-element.135), channel_id=1, source_target_pairs={{0,8},{4,12},{8,0},{12,4},{1,9},{5,13},{9,1},{13,5},{2,10},{6,14},... | collective-permute-start | bytes 1572872 | tf_op jit(solution)/shard_map/ppermute | solution.py:292
  615.2 81.3 %collective-permute-start.41 = (bf16[64,32,128]{2,1,0:T(8,128)(2,1)}, bf16[64,32,128]{2,1,0:T(8,128)(2,1)S(1)}, u32[]{:S(2)}, u32[]{:S(2)}) collective-permute-start(bf16[64,32,128]{2,1,0:T(8,128)(2,1)} %get-tuple-element.136), channel_id=1, source_target_pairs={{0,12},{4,8},{8,4},{12,0},{1,13},{5,9},{9,5},{13,1},{2,14},{6,10},... | collective-permute-start | bytes 1572872 | tf_op jit(solution)/shard_map/ppermute | solution.py:292
  616.5 80.1 %collective-permute-start.45 = (bf16[64,32,128]{2,1,0:T(8,128)(2,1)}, bf16[64,32,128]{2,1,0:T(8,128)(2,1)S(1)}, u32[]{:S(2)}, u32[]{:S(2)}) collective-permute-start(bf16[64,32,128]{2,1,0:T(8,128)(2,1)} %get-tuple-element.142), channel_id=1, source_target_pairs={{0,4},{4,0},{8,12},{12,8},{1,5},{5,1},{9,13},{13,9},{2,6},{6,2},{1... | collective-permute-start | bytes 1572872 | tf_op jit(solution)/shard_map/ppermute | solution.py:292
  618.7 88.2 %collective-permute-start.46 = (bf16[64,32,128]{2,1,0:T(8,128)(2,1)}, bf16[64,32,128]{2,1,0:T(8,128)(2,1)S(1)}, u32[]{:S(2)}, u32[]{:S(2)}) collective-permute-start(bf16[64,32,128]{2,1,0:T(8,128)(2,1)} %get-tuple-element.143), channel_id=1, source_target_pairs={{0,8},{4,12},{8,0},{12,4},{1,9},{5,13},{9,1},{13,5},{2,10},{6,14},... | collective-permute-start | bytes 1572872 | tf_op jit(solution)/shard_map/ppermute | solution.py:292
  652.3 66.7 %collective-permute-start.47 = (bf16[64,32,128]{2,1,0:T(8,128)(2,1)}, bf16[64,32,128]{2,1,0:T(8,128)(2,1)S(1)}, u32[]{:S(2)}, u32[]{:S(2)}) collective-permute-start(bf16[64,32,128]{2,1,0:T(8,128)(2,1)} %get-tuple-element.144), channel_id=1, source_target_pairs={{0,12},{4,8},{8,4},{12,0},{1,13},{5,9},{9,5},{13,1},{2,14},{6,10},... | collective-permute-start | bytes 1572872 | tf_op jit(solution)/shard_map/ppermute | solution.py:292
  (68 other events, 2293.2 us)

commit v7 on v6

--- a/solution.py
+++ b/solution.py
@@ -320,23 +320,28 @@
             cost_estimate=cost(0, 1 + len(terms)),
         )(*terms)
 
+    def tie(*lists):
+        values = iter(lax.optimization_barrier(tuple(sum(lists, []))))
+        return [[next(values) for _ in part] for part in lists]
+
     def swap(array, axis, by):
         return lax.ppermute(array, axis, [(a, a ^ by) for a in range(lax.axis_size(axis))])
 
-    def all_rows(array):
-        blocks = []
+    def all_rows(array, sent):
+        blocks, moved = [], []
         for x in range(sides):
-            came = swap(array, "row", x) if x else array
+            came = swap(sent, "row", x) if x else array
+            moved += [came] if x else []
             blocks += [swap(came, "sub", c) if c else came for c in range(cores)]
-        return blocks
-
-    def own_rows(partials):
+        return blocks, moved
+
+    def own_rows(partials, before):
         terms = []
         for x in range(sides):
             of_cores = [swap(partials[x * cores + c], "sub", c) if c else partials[x * cores] for c in range(cores)]
             if x:
                 total = sum(term.astype(F32) for term in of_cores).astype(BF16)
-                terms.append(swap(total, "row", x))
+                terms.append(swap(tie([total], before)[0][0], "row", x))
             else:
                 terms += of_cores
         return terms
@@ -385,20 +390,17 @@
         )(place, *sum(grads, []), *sum(lefts, []))
         return [out[h::chunks] for h in range(chunks)]
 
-    def tie(*lists):
-        values = iter(lax.optimization_barrier(tuple(sum(lists, []))))
-        return [[next(values) for _ in part] for part in lists]
-
     firsts = [p * blocks for p in range(chunks)]
     sent = [list(project(weight, first, blocks)) for weight in (right_w, left_w) for first in firsts]
-    halves, gathered = [], []
+    lefts = [exchange(pieces_of) for pieces_of in sent[chunks:]]
+    halves, moved = [], []
     for part in range(chunks):
-        got = exchange(sent[part])
-        got = tie(got, gathered, *sent[part + 1:part + 1 + chunks])[0]
-        gathered = [gather(got)]
-        halves.append(all_rows(gathered[0]))
+        got = tie(exchange(sent[part]), moved, *sent[part + 1:part + 1 + chunks])[0]
+        block_here = gather(got)
+        over = tie([block_here], lefts[part - 1][1:3])[0][0] if part else block_here
+        row_parts, moved = all_rows(block_here, over)
+        halves.append(row_parts)
     right = [half[u] for u in range(row_blocks) for half in halves]
-    lefts = [exchange(pieces_of) for pieces_of in sent[chunks:]]
     sigms, grads, backs = [], [], []
     for first, left in zip(firsts, lefts):
         *grad_comb, sigm = middle(exchange(combine(left)), first)
@@ -409,7 +411,9 @@
         if part == 0 and chunks > 1:
             grads[-1] = tie(grads[-1], backs[0])[0]
     left_grads = [exchange(back) for back in backs]
-    right_grads = [exchange(split(own_rows(partials))) for partials in right_back(grads, lefts)]
+    right_grads = [
+        exchange(split(own_rows(partials, back[1:3]))) for partials, back in zip(right_back(grads, lefts), left_grads)
+    ]
     out = jnp.zeros((rows, cols, chans), BF16)
     for first, left_grad, right_grad, sigm in zip(firsts, left_grads, right_grads, sigms):
         out = last(left_grad, right_grad, sigm, first, out)

time: 736 us -> 662 us (0.90)
  waiting for transfers between devices: 497 us -> 419 us
    ppermute x12, waiting for transfers between devices: 155 us -> 95.2 us  [swap(): lax.ppermute(array, axis, [(a, a ^ by) for a in range(lax.axis_size(axis))])]
    ppermute x36, waiting for transfers between devices: 342 us -> 324 us  [exchange(): lax.ppermute(sent[s], 'ch', [(a, a ^ s) for a in range(groups)])]
  transfers between devices with their start and end apart: 48 -> 48, of which waited for: 26 -> 26; matrix products, arithmetic and copies ran while one was open for 2% -> 2% of each run, Pallas kernels for 16% -> 18%
where the time goes in v7:
time: 662 us; the launch traced here: 655 us
  waiting for transfers between devices  419 us (63%)
  Pallas kernels  159 us (24%)
  starting transfers between devices  53.5 us (8%)
  local copies, waits for them, and re-layouts  16.7 us (3%)
    ppermute x36, waiting for transfers between devices, exchange(): lax.ppermute(sent[s], 'ch', [(a, a ^ s) for a in range(groups)])  324 us
    ppermute x12, waiting for transfers between devices, swap(): lax.ppermute(array, axis, [(a, a ^ by) for a in range(lax.axis_size(axis))])  95.2 us
    pallas_call x4, Pallas kernels, with_right(): pl.pallas_call(functools.partial(kernel, groups, row_blocks, chunks), gri...  45 us
    ppermute x36, starting transfers between devices, exchange(): lax.ppermute(sent[s], 'ch', [(a, a ^ s) for a in range(groups)])  35.4 us
    pallas_call x4, Pallas kernels, project(): pl.pallas_call(functools.partial(project_kernel, step), grid=(count,), in...  31.9 us
    pallas_call x2, Pallas kernels, last(): pl.pallas_call(functools.partial(last_kernel, step, groups), grid=(blocks...  29.8 us
    pallas_call x2, Pallas kernels, middle(): pl.pallas_call(functools.partial(middle_kernel, step, groups), grid=(bloc...  21.9 us
    ppermute x12, starting transfers between devices, swap(): lax.ppermute(array, axis, [(a, a ^ by) for a in range(lax.axis_size(axis))])  18.1 us
  transfers between devices with their start and end apart: 48, of which 26 were waited for; matrix products, arithmetic and copies ran while one was open for 2% of the time, Pallas kernels for 18%

profile of v7, /device:TPU:15, one launch (start us, length us, event | category | flops | bytes accessed | tf_op | source)
XLA Modules:
  0.0 654.6 jit_solution(9390824340298310138)
XLA Ops:
  37.2 22.4 %collective-permute-done.2.refs_3_ = bf16[64,32,128]{2,1,0:T(8,128)(2,1)S(1)} collective-permute-done((bf16[64,32,128]{2,1,0:T(8,128)(2,1)}, bf16[64,32,128]{2,1,0:T(8,128)(2,1)S(1)}, u32[]{:S(2)}, u32[]{:S(2)}) %collective-permute-start.2) | collective-permute-done | bytes 524320 | tf_op jit(solution)/shard_map/ppermute | solution.py:292
  67.8 15.4 %collective-permute-done.3.refs_1_ = bf16[64,32,128]{2,1,0:T(8,128)(2,1)S(1)} collective-permute-done((bf16[64,32,128]{2,1,0:T(8,128)(2,1)S(1)}, bf16[64,32,128]{2,1,0:T(8,128)(2,1)S(1)}, u32[]{:S(2)}, u32[]{:S(2)}) %collective-permute-start.3) | collective-permute-done | bytes 524320 | tf_op jit(solution)/shard_map/ppermute | solution.py:292
  94.0 16.3 %collective-permute-done.5.refs_3_ = bf16[64,32,128]{2,1,0:T(8,128)(2,1)S(1)} collective-permute-done((bf16[64,32,128]{2,1,0:T(8,128)(2,1)S(1)}, bf16[64,32,128]{2,1,0:T(8,128)(2,1)S(1)}, u32[]{:S(2)}, u32[]{:S(2)}) %collective-permute-start.5) | collective-permute-done | bytes 524320 | tf_op jit(solution)/shard_map/ppermute | solution.py:292
  114.6 17.2 %collective-permute-done.10.refs_10_ = bf16[64,32,128]{2,1,0:T(8,128)(2,1)S(1)} collective-permute-done((bf16[64,32,128]{2,1,0:T(8,128)(2,1)S(1)}, bf16[64,32,128]{2,1,0:T(8,128)(2,1)S(1)}, u32[]{:S(2)}, u32[]{:S(2)}) %collective-permute-start.10) | collective-permute-done | bytes 524320 | tf_op jit(solution)/shard_map/ppermute | solution.py:292
  137.0 38.9 %collective-permute-done.11.refs_5_ = bf16[32,64,512]{2,1,0:T(8,128)(2,1)} collective-permute-done((bf16[32,64,512]{2,1,0:T(8,128)(2,1)}, bf16[32,64,512]{2,1,0:T(8,128)(2,1)}, u32[]{:S(2)}, u32[]{:S(2)}) %collective-permute-start.11) | collective-permute-done | bytes 2097184 | tf_op jit(solution)/shard_map/ppermute | solution.py:328
  180.3 24.7 %collective-permute-done.20.refs_11_ = bf16[64,32,128]{2,1,0:T(8,128)(2,1)} collective-permute-done((bf16[64,32,128]{2,1,0:T(8,128)(2,1)S(1)}, bf16[64,32,128]{2,1,0:T(8,128)(2,1)}, u32[]{:S(2)}, u32[]{:S(2)}) %collective-permute-start.20) | collective-permute-done | bytes 524320 | tf_op jit(solution)/shard_map/ppermute | solution.py:292
  210.3 12.4 %shard_map.90 = (bf16[64,32,128]{2,1,0:T(8,128)(2,1)}, bf16[64,32,128]{2,1,0:T(8,128)(2,1)}, bf16[64,32,128]{2,1,0:T(8,128)(2,1)}, bf16[64,32,128]{2,1,0:T(8,128)(2,1)}) custom-call(s32[4]{0:T(128)} %pad_add_fusion.place_ref, bf16[32,64,512]{2,1,0:T(8,128)(2,1)} %shard_map.85.refs_0_, bf16[32,64,512]{2,1,0:T(8,128)(2,1)} %shard_map.87.refs_1_, ...), custom_call_target="tpu_custom_call" | custom-call | flops 1073741824 | bytes 20971520 | tf_op jit(solution)/shard_map/pallas_call | solution.py:352
  227.6 14.0 %collective-permute-done.15.refs_10_.refs_14_ = bf16[64,32,128]{2,1,0:T(8,128)(2,1)S(1)} collective-permute-done((bf16[64,32,128]{2,1,0:T(8,128)(2,1)}, bf16[64,32,128]{2,1,0:T(8,128)(2,1)S(1)}, u32[]{:S(2)}, u32[]{:S(2)}) %collective-permute-start.15) | collective-permute-done | bytes 524320 | tf_op jit(solution)/shard_map/ppermute | solution.py:292
  241.6 36.1 %collective-permute-done.16.refs_11_.refs_15_ = bf16[64,32,128]{2,1,0:T(8,128)(2,1)S(1)} collective-permute-done((bf16[64,32,128]{2,1,0:T(8,128)(2,1)}, bf16[64,32,128]{2,1,0:T(8,128)(2,1)S(1)}, u32[]{:S(2)}, u32[]{:S(2)}) %collective-permute-start.16) | collective-permute-done | bytes 524320 | tf_op jit(solution)/shard_map/ppermute | solution.py:292
  278.5 12.4 %shard_map.88 = (bf16[64,32,128]{2,1,0:T(8,128)(2,1)}, bf16[64,32,128]{2,1,0:T(8,128)(2,1)}, bf16[64,32,128]{2,1,0:T(8,128)(2,1)}, bf16[64,32,128]{2,1,0:T(8,128)(2,1)}) custom-call(s32[4]{0:T(128)} %pad_add_fusion.place_ref, bf16[32,64,512]{2,1,0:T(8,128)(2,1)} %shard_map.85.refs_0_, bf16[32,64,512]{2,1,0:T(8,128)(2,1)} %shard_map.87.refs_1_, ...), custom_call_target="tpu_custom_call" | custom-call | flops 1073741824 | bytes 20971520 | tf_op jit(solution)/shard_map/pallas_call | solution.py:352
  314.7 17.4 %collective-permute-done.18.refs_2_ = bf16[64,32,128]{2,1,0:T(8,128)(2,1)S(1)} collective-permute-done((bf16[64,32,128]{2,1,0:T(8,128)(2,1)}, bf16[64,32,128]{2,1,0:T(8,128)(2,1)S(1)}, u32[]{:S(2)}, u32[]{:S(2)}) %collective-permute-start.18) | collective-permute-done | bytes 524320 | tf_op jit(solution)/shard_map/ppermute | solution.py:292
  332.0 35.6 %collective-permute-done.19.refs_3_ = bf16[64,32,128]{2,1,0:T(8,128)(2,1)S(1)} collective-permute-done((bf16[64,32,128]{2,1,0:T(8,128)(2,1)}, bf16[64,32,128]{2,1,0:T(8,128)(2,1)S(1)}, u32[]{:S(2)}, u32[]{:S(2)}) %collective-permute-start.19) | collective-permute-done | bytes 524320 | tf_op jit(solution)/shard_map/ppermute | solution.py:292
  368.4 10.9 %shard_map.89 = (bf16[64,32,128]{2,1,0:T(8,128)(2,1)}, bf16[64,32,128]{2,1,0:T(8,128)(2,1)}, bf16[64,32,128]{2,1,0:T(8,128)(2,1)}, bf16[64,32,128]{2,1,0:T(8,128)(2,1)}, bf16[64,128,128]{2,1,0:T(8,128)(2,1)}) custom-call(bf16[128,128,128]{2,1,0:T(8,128)(2,1)} %pair_ref.15, bf16[128,128,128]{2,1,0:T(8,128)(2,1)} %gout_ref.3, f32[1,128]{1,0:T(1,128)} %bitcast.38, ...), custom_call_target="tpu_custom_call" | custom-call | flops 1073741824 | bytes 10485760 | tf_op jit(solution)/shard_map/pallas_call | solution.py:266
  401.7 20.2 %collective-permute-done.31.refs_6_.refs_10_ = bf16[64,32,128]{2,1,0:T(8,128)(2,1)S(1)} collective-permute-done((bf16[64,32,128]{2,1,0:T(8,128)(2,1)}, bf16[64,32,128]{2,1,0:T(8,128)(2,1)S(1)}, u32[]{:S(2)}, u32[]{:S(2)}) %collective-permute-start.31) | collective-permute-done | bytes 524320 | tf_op jit(solution)/shard_map/ppermute | solution.py:292
  421.9 13.1 %collective-permute-done.32.refs_7_.refs_11_ = bf16[64,32,128]{2,1,0:T(8,128)(2,1)S(1)} collective-permute-done((bf16[64,32,128]{2,1,0:T(8,128)(2,1)}, bf16[64,32,128]{2,1,0:T(8,128)(2,1)S(1)}, u32[]{:S(2)}, u32[]{:S(2)}) %collective-permute-start.32) | collective-permute-done | bytes 524320 | tf_op jit(solution)/shard_map/ppermute | solution.py:292
  435.8 14.3 %shard_map.93 = (bf16[32,64,512]{2,1,0:T(8,128)(2,1)}, bf16[32,64,512]{2,1,0:T(8,128)(2,1)}, bf16[32,64,512]{2,1,0:T(8,128)(2,1)}, bf16[32,64,512]{2,1,0:T(8,128...) custom-call(s32[4]{0:T(128)} %pad_add_fusion.place_ref, ...), custom_call_target="tpu_custom_call" | custom-call | flops 2147483648 | bytes 25165824 | tf_op jit(solution)/shard_map/pallas_call | solution.py:377
  481.2 15.0 %collective-permute-done.39.refs_1_ = bf16[64,32,128]{2,1,0:T(8,128)(2,1)S(1)} collective-permute-done((bf16[64,32,128]{2,1,0:T(8,128)(2,1)}, bf16[64,32,128]{2,1,0:T(8,128)(2,1)S(1)}, u32[]{:S(2)}, u32[]{:S(2)}) %collective-permute-start.39) | collective-permute-done | bytes 524320 | tf_op jit(solution)/shard_map/ppermute | solution.py:292
  501.7 20.1 %collective-permute-done.35.refs_2_ = bf16[32,64,512]{2,1,0:T(8,128)(2,1)S(1)} collective-permute-done((bf16[32,64,512]{2,1,0:T(8,128)(2,1)S(1)}, bf16[32,64,512]{2,1,0:T(8,128)(2,1)S(1)}, u32[]{:S(2)}, u32[]{:S(2)}) %collective-permute-start.35) | collective-permute-done | bytes 2097184 | tf_op jit(solution)/shard_map/ppermute | solution.py:328
  530.5 36.2 %collective-permute-done.44.refs_2_ = bf16[32,64,512]{2,1,0:T(8,128)(2,1)S(1)} collective-permute-done((bf16[32,64,512]{2,1,0:T(8,128)(2,1)S(1)}, bf16[32,64,512]{2,1,0:T(8,128)(2,1)S(1)}, u32[]{:S(2)}, u32[]{:S(2)}) %collective-permute-start.44) | collective-permute-done | bytes 2097184 | tf_op jit(solution)/shard_map/ppermute | solution.py:328
  583.1 14.9 %shard_map.95.held_ref = bf16[128,128,128]{2,1,0:T(8,128)(2,1)} custom-call(bf16[128,128,128]{2,1,0:T(8,128)(2,1)} %pair_ref.15, bf16[64,128,128]{2,1,0:T(8,128)(2,1)} %get-tuple-element.112.sigm_ref, f32[16,1,1024]{2,1,0:T(1,128)} %broadcast_multiply_fusion.mask_ref, f32[1,128]{1,0:T(1,128)} %bitcast.39, ...), custom_call_target="tpu_custom_call", output_to_operand_aliasing={{}: (5, {})} | custom-call | flops 2415919104 | bytes 10485760 | tf_op jit(solution)/shard_map/pallas_call | solution.py:278
  598.0 18.3 %collective-permute-done.41.refs_3_ = bf16[64,32,128]{2,1,0:T(8,128)(2,1)S(1)} collective-permute-done((bf16[64,32,128]{2,1,0:T(8,128)(2,1)}, bf16[64,32,128]{2,1,0:T(8,128)(2,1)S(1)}, u32[]{:S(2)}, u32[]{:S(2)}) %collective-permute-start.41) | collective-permute-done | bytes 524320 | tf_op jit(solution)/shard_map/ppermute | solution.py:292
  616.3 11.4 %collective-permute-done.46.refs_6_ = bf16[64,32,128]{2,1,0:T(8,128)(2,1)S(1)} collective-permute-done((bf16[64,32,128]{2,1,0:T(8,128)(2,1)}, bf16[64,32,128]{2,1,0:T(8,128)(2,1)S(1)}, u32[]{:S(2)}, u32[]{:S(2)}) %collective-permute-start.46) | collective-permute-done | bytes 524320 | tf_op jit(solution)/shard_map/ppermute | solution.py:292
  627.6 11.2 %collective-permute-done.47.refs_7_ = bf16[64,32,128]{2,1,0:T(8,128)(2,1)S(1)} collective-permute-done((bf16[64,32,128]{2,1,0:T(8,128)(2,1)}, bf16[64,32,128]{2,1,0:T(8,128)(2,1)S(1)}, u32[]{:S(2)}, u32[]{:S(2)}) %collective-permute-start.47) | collective-permute-done | bytes 524320 | tf_op jit(solution)/shard_map/ppermute | solution.py:292
  639.7 14.9 %shard_map.98 = bf16[128,128,128]{2,1,0:T(8,128)(2,1)} custom-call(bf16[128,128,128]{2,1,0:T(8,128)(2,1)} %pair_ref.15, bf16[64,128,128]{2,1,0:T(8,128)(2,1)} %get-tuple-element.107.sigm_ref, f32[16,1,1024]{2,1,0:T(1,128)} %broadcast_multiply_fusion.mask_ref, f32[1,128]{1,0:T(1,128)} %bitcast.40, ...), custom_call_target="tpu_custom_call", output_to_operand_aliasing={{}: (5, {})} | custom-call | flops 2415919104 | bytes 10485760 | tf_op jit(solution)/shard_map/pallas_call | solution.py:278
  (218 shorter events, 191.0 us)
Async XLA Ops:
  63.9 46.4 %collective-permute-start.6 = (bf16[32,64,512]{2,1,0:T(8,128)(2,1)}, bf16[32,64,512]{2,1,0:T(8,128)(2,1)}, u32[]{:S(2)}, u32[]{:S(2)}) collective-permute-start(bf16[32,64,512]{2,1,0:T(8,128)(2,1)} %shard_map.85.refs_0_), channel_id=1, source_target_pairs={{0,2},{2,0},{1,3},{3,1},{4,6},{6,4},{5,7},{7,5},{8,10},{10,8},{9,1... | collective-permute-start | bytes 6291464 | tf_op jit(solution)/shard_map/ppermute | solution.py:328
  66.8 47.8 %collective-permute-start.9 = (bf16[64,32,128]{2,1,0:T(8,128)(2,1)S(1)}, bf16[64,32,128]{2,1,0:T(8,128)(2,1)S(1)}, u32[]{:S(2)}, u32[]{:S(2)}) collective-permute-start(bf16[64,32,128]{2,1,0:T(8,128)(2,1)S(1)} %copy-done.46), channel_id=1, source_target_pairs={{0,4},{4,0},{8,12},{12,8},{1,5},{5,1},{9,13},{13,9},{2,6},{6,2},{1... | collective-permute-start | bytes 1572872 | tf_op jit(solution)/shard_map/ppermute | solution.py:292
  83.3 48.5 %collective-permute-start.10 = (bf16[64,32,128]{2,1,0:T(8,128)(2,1)S(1)}, bf16[64,32,128]{2,1,0:T(8,128)(2,1)S(1)}, u32[]{:S(2)}, u32[]{:S(2)}) collective-permute-start(bf16[64,32,128]{2,1,0:T(8,128)(2,1)S(1)} %copy-done.45), channel_id=1, source_target_pairs={{0,8},{4,12},{8,0},{12,4},{1,9},{5,13},{9,1},{13,5},{2,10},{6,14},... | collective-permute-start | bytes 1572872 | tf_op jit(solution)/shard_map/ppermute | solution.py:292
  133.0 74.7 %collective-permute-start.7 = (bf16[32,64,512]{2,1,0:T(8,128)(2,1)S(1)}, bf16[32,64,512]{2,1,0:T(8,128)(2,1)}, u32[]{:S(2)}, u32[]{:S(2)}) collective-permute-start(bf16[32,64,512]{2,1,0:T(8,128)(2,1)S(1)} %copy-done), channel_id=1, source_target_pairs={{0,1},{1,0},{2,3},{3,2},{4,5},{5,4},{6,7},{7,6},{8,9},{9,8},{10,11... | collective-permute-start | bytes 6291464 | tf_op jit(solution)/shard_map/ppermute | solution.py:328
  136.5 72.5 %collective-permute-start.8 = (bf16[32,64,512]{2,1,0:T(8,128)(2,1)}, bf16[32,64,512]{2,1,0:T(8,128)(2,1)}, u32[]{:S(2)}, u32[]{:S(2)}) collective-permute-start(bf16[32,64,512]{2,1,0:T(8,128)(2,1)} %shard_map.87.refs_1_), channel_id=1, source_target_pairs={{0,1},{1,0},{2,3},{3,2},{4,5},{5,4},{6,7},{7,6},{8,9},{9,8},{10,11... | collective-permute-start | bytes 6291464 | tf_op jit(solution)/shard_map/ppermute | solution.py:328
  136.5 73.8 %collective-permute-start.12 = (bf16[32,64,512]{2,1,0:T(8,128)(2,1)}, bf16[32,64,512]{2,1,0:T(8,128)(2,1)}, u32[]{:S(2)}, u32[]{:S(2)}) collective-permute-start(bf16[32,64,512]{2,1,0:T(8,128)(2,1)} %collective-permute-done.6.refs_4_), channel_id=1, source_target_pairs={{0,1},{1,0},{2,3},{3,2},{4,5},{5,4},{6,7},{7,6},{8,9},{9,8},{10,11... | collective-permute-start | bytes 6291464 | tf_op jit(solution)/shard_map/ppermute | solution.py:328
  209.0 68.7 %collective-permute-start.16 = (bf16[64,32,128]{2,1,0:T(8,128)(2,1)}, bf16[64,32,128]{2,1,0:T(8,128)(2,1)S(1)}, u32[]{:S(2)}, u32[]{:S(2)}) collective-permute-start(bf16[64,32,128]{2,1,0:T(8,128)(2,1)} %get-tuple-element.97), channel_id=1, source_target_pairs={{0,12},{4,8},{8,4},{12,0},{1,13},{5,9},{9,5},{13,1},{2,14},{6,10},... | collective-permute-start | bytes 1572872 | tf_op jit(solution)/shard_map/ppermute | solution.py:292
  222.7 69.6 %collective-permute-start.21 = (bf16[64,32,128]{2,1,0:T(8,128)(2,1)}, bf16[64,32,128]{2,1,0:T(8,128)(2,1)S(1)}, u32[]{:S(2)}, u32[]{:S(2)}) collective-permute-start(bf16[64,32,128]{2,1,0:T(8,128)(2,1)} %get-tuple-element.109), channel_id=1, source_target_pairs={{0,4},{4,0},{8,12},{12,8},{1,5},{5,1},{9,13},{13,9},{2,6},{6,2},{1... | collective-permute-start | bytes 1572872 | tf_op jit(solution)/shard_map/ppermute | solution.py:292
  223.6 70.0 %collective-permute-start.22 = (bf16[64,32,128]{2,1,0:T(8,128)(2,1)}, bf16[64,32,128]{2,1,0:T(8,128)(2,1)S(1)}, u32[]{:S(2)}, u32[]{:S(2)}) collective-permute-start(bf16[64,32,128]{2,1,0:T(8,128)(2,1)} %get-tuple-element.110), channel_id=1, source_target_pairs={{0,8},{4,12},{8,0},{12,4},{1,9},{5,13},{9,1},{13,5},{2,10},{6,14},... | collective-permute-start | bytes 1572872 | tf_op jit(solution)/shard_map/ppermute | solution.py:292
  224.1 76.1 %collective-permute-start.23 = (bf16[64,32,128]{2,1,0:T(8,128)(2,1)}, bf16[64,32,128]{2,1,0:T(8,128)(2,1)S(1)}, u32[]{:S(2)}, u32[]{:S(2)}) collective-permute-start(bf16[64,32,128]{2,1,0:T(8,128)(2,1)} %get-tuple-element.111), channel_id=1, source_target_pairs={{0,12},{4,8},{8,4},{12,0},{1,13},{5,9},{9,5},{13,1},{2,14},{6,10},... | collective-permute-start | bytes 1572872 | tf_op jit(solution)/shard_map/ppermute | solution.py:292
  292.3 75.3 %collective-permute-start.19 = (bf16[64,32,128]{2,1,0:T(8,128)(2,1)}, bf16[64,32,128]{2,1,0:T(8,128)(2,1)S(1)}, u32[]{:S(2)}, u32[]{:S(2)}) collective-permute-start(bf16[64,32,128]{2,1,0:T(8,128)(2,1)} %get-tuple-element.106), channel_id=1, source_target_pairs={{0,12},{4,8},{8,4},{12,0},{1,13},{5,9},{9,5},{13,1},{2,14},{6,10},... | collective-permute-start | bytes 1572872 | tf_op jit(solution)/shard_map/ppermute | solution.py:292
  311.9 68.9 %collective-permute-start.24 = (bf16[64,32,128]{2,1,0:T(8,128)(2,1)}, bf16[64,32,128]{2,1,0:T(8,128)(2,1)S(1)}, u32[]{:S(2)}, u32[]{:S(2)}) collective-permute-start(bf16[64,32,128]{2,1,0:T(8,128)(2,1)} %get-tuple-element.114), channel_id=1, source_target_pairs={{0,4},{4,0},{8,12},{12,8},{1,5},{5,1},{9,13},{13,9},{2,6},{6,2},{1... | collective-permute-start | bytes 1572872 | tf_op jit(solution)/shard_map/ppermute | solution.py:292
  312.0 70.1 %collective-permute-start.25 = (bf16[64,32,128]{2,1,0:T(8,128)(2,1)}, bf16[64,32,128]{2,1,0:T(8,128)(2,1)S(1)}, u32[]{:S(2)}, u32[]{:S(2)}) collective-permute-start(bf16[64,32,128]{2,1,0:T(8,128)(2,1)} %get-tuple-element.115), channel_id=1, source_target_pairs={{0,8},{4,12},{8,0},{12,4},{1,9},{5,13},{9,1},{13,5},{2,10},{6,14},... | collective-permute-start | bytes 1572872 | tf_op jit(solution)/shard_map/ppermute | solution.py:292
  313.4 77.3 %collective-permute-start.26 = (bf16[64,32,128]{2,1,0:T(8,128)(2,1)}, bf16[64,32,128]{2,1,0:T(8,128)(2,1)S(1)}, u32[]{:S(2)}, u32[]{:S(2)}) collective-permute-start(bf16[64,32,128]{2,1,0:T(8,128)(2,1)} %get-tuple-element.116), channel_id=1, source_target_pairs={{0,12},{4,8},{8,4},{12,0},{1,13},{5,9},{9,5},{13,1},{2,14},{6,10},... | collective-permute-start | bytes 1572872 | tf_op jit(solution)/shard_map/ppermute | solution.py:292
  380.8 54.2 %collective-permute-start.32 = (bf16[64,32,128]{2,1,0:T(8,128)(2,1)}, bf16[64,32,128]{2,1,0:T(8,128)(2,1)S(1)}, u32[]{:S(2)}, u32[]{:S(2)}) collective-permute-start(bf16[64,32,128]{2,1,0:T(8,128)(2,1)} %get-tuple-element.124), channel_id=1, source_target_pairs={{0,12},{4,8},{8,4},{12,0},{1,13},{5,9},{9,5},{13,1},{2,14},{6,10},... | collective-permute-start | bytes 1572872 | tf_op jit(solution)/shard_map/ppermute | solution.py:292
  478.0 52.3 %collective-permute-start.42 = (bf16[32,64,512]{2,1,0:T(8,128)(2,1)}, bf16[32,64,512]{2,1,0:T(8,128)(2,1)S(1)}, u32[]{:S(2)}, u32[]{:S(2)}) collective-permute-start(bf16[32,64,512]{2,1,0:T(8,128)(2,1)} %get-tuple-element.143), channel_id=1, source_target_pairs={{0,1},{1,0},{2,3},{3,2},{4,5},{5,4},{6,7},{7,6},{8,9},{9,8},{10,11... | collective-permute-start | bytes 6291464 | tf_op jit(solution)/shard_map/ppermute | solution.py:328
  499.2 67.5 %collective-permute-start.44 = (bf16[32,64,512]{2,1,0:T(8,128)(2,1)S(1)}, bf16[32,64,512]{2,1,0:T(8,128)(2,1)S(1)}, u32[]{:S(2)}, u32[]{:S(2)}) collective-permute-start(bf16[32,64,512]{2,1,0:T(8,128)(2,1)S(1)} %add_convert_fusion), channel_id=1, source_target_pairs={{0,2},{2,0},{1,3},{3,1},{4,6},{6,4},{5,7},{7,5},{8,10},{10,8},{9,1... | collective-permute-start | bytes 6291464 | tf_op jit(solution)/shard_map/ppermute | solution.py:328
  500.4 72.4 %collective-permute-start.29 = (bf16[64,32,128]{2,1,0:T(8,128)(2,1)}, bf16[64,32,128]{2,1,0:T(8,128)(2,1)S(1)}, u32[]{:S(2)}, u32[]{:S(2)}) collective-permute-start(bf16[64,32,128]{2,1,0:T(8,128)(2,1)} %get-tuple-element.120), channel_id=1, source_target_pairs={{0,12},{4,8},{8,4},{12,0},{1,13},{5,9},{9,5},{13,1},{2,14},{6,10},... | collective-permute-start | bytes 1572872 | tf_op jit(solution)/shard_map/ppermute | solution.py:292
  527.8 47.2 %collective-permute-start.36 = (bf16[64,32,128]{2,1,0:T(8,128)(2,1)}, bf16[64,32,128]{2,1,0:T(8,128)(2,1)}, u32[]{:S(2)}, u32[]{:S(2)}) collective-permute-start(bf16[64,32,128]{2,1,0:T(8,128)(2,1)} %get-tuple-element.135), channel_id=1, source_target_pairs={{0,4},{4,0},{8,12},{12,8},{1,5},{5,1},{9,13},{13,9},{2,6},{6,2},{1... | collective-permute-start | bytes 1572872 | tf_op jit(solution)/shard_map/ppermute | solution.py:292
  527.9 47.5 %collective-permute-start.37 = (bf16[64,32,128]{2,1,0:T(8,128)(2,1)}, bf16[64,32,128]{2,1,0:T(8,128)(2,1)}, u32[]{:S(2)}, u32[]{:S(2)}) collective-permute-start(bf16[64,32,128]{2,1,0:T(8,128)(2,1)} %get-tuple-element.136), channel_id=1, source_target_pairs={{0,8},{4,12},{8,0},{12,4},{1,9},{5,13},{9,1},{13,5},{2,10},{6,14},... | collective-permute-start | bytes 1572872 | tf_op jit(solution)/shard_map/ppermute | solution.py:292
  530.3 49.7 %collective-permute-start.38 = (bf16[64,32,128]{2,1,0:T(8,128)(2,1)}, bf16[64,32,128]{2,1,0:T(8,128)(2,1)}, u32[]{:S(2)}, u32[]{:S(2)}) collective-permute-start(bf16[64,32,128]{2,1,0:T(8,128)(2,1)} %get-tuple-element.137), channel_id=1, source_target_pairs={{0,12},{4,8},{8,4},{12,0},{1,13},{5,9},{9,5},{13,1},{2,14},{6,10},... | collective-permute-start | bytes 1572872 | tf_op jit(solution)/shard_map/ppermute | solution.py:292
  566.7 49.5 %collective-permute-start.41 = (bf16[64,32,128]{2,1,0:T(8,128)(2,1)}, bf16[64,32,128]{2,1,0:T(8,128)(2,1)S(1)}, u32[]{:S(2)}, u32[]{:S(2)}) collective-permute-start(bf16[64,32,128]{2,1,0:T(8,128)(2,1)} %get-tuple-element.141), channel_id=1, source_target_pairs={{0,12},{4,8},{8,4},{12,0},{1,13},{5,9},{9,5},{13,1},{2,14},{6,10},... | collective-permute-start | bytes 1572872 | tf_op jit(solution)/shard_map/ppermute | solution.py:292
  575.0 52.6 %collective-permute-start.46 = (bf16[64,32,128]{2,1,0:T(8,128)(2,1)}, bf16[64,32,128]{2,1,0:T(8,128)(2,1)S(1)}, u32[]{:S(2)}, u32[]{:S(2)}) collective-permute-start(bf16[64,32,128]{2,1,0:T(8,128)(2,1)} %get-tuple-element.149), channel_id=1, source_target_pairs={{0,8},{4,12},{8,0},{12,4},{1,9},{5,13},{9,1},{13,5},{2,10},{6,14},... | collective-permute-start | bytes 1572872 | tf_op jit(solution)/shard_map/ppermute | solution.py:292
  575.4 63.5 %collective-permute-start.47 = (bf16[64,32,128]{2,1,0:T(8,128)(2,1)}, bf16[64,32,128]{2,1,0:T(8,128)(2,1)S(1)}, u32[]{:S(2)}, u32[]{:S(2)}) collective-permute-start(bf16[64,32,128]{2,1,0:T(8,128)(2,1)} %get-tuple-element.150), channel_id=1, source_target_pairs={{0,12},{4,8},{8,4},{12,0},{1,13},{5,9},{9,5},{13,1},{2,14},{6,10},... | collective-permute-start | bytes 1572872 | tf_op jit(solution)/shard_map/ppermute | solution.py:292
  (74 other events, 1886.5 us)

commit v8 on v7

--- a/solution.py
+++ b/solution.py
@@ -327,13 +327,13 @@
     def swap(array, axis, by):
         return lax.ppermute(array, axis, [(a, a ^ by) for a in range(lax.axis_size(axis))])
 
-    def all_rows(array, sent):
-        blocks, moved = [], []
-        for x in range(sides):
-            came = swap(sent, "row", x) if x else array
-            moved += [came] if x else []
+    def all_rows(array, before, beside):
+        blocks = [swap(array, "sub", c) if c else array for c in range(cores)]
+        sent = tie([array], blocks[1:], before)[0][0]
+        for x in range(1, sides):
+            came = tie([swap(sent, "row", x)], beside)[0][0]
             blocks += [swap(came, "sub", c) if c else came for c in range(cores)]
-        return blocks, moved
+        return blocks
 
     def own_rows(partials, before):
         terms = []
@@ -396,21 +396,21 @@
     halves, moved = [], []
     for part in range(chunks):
         got = tie(exchange(sent[part]), moved, *sent[part + 1:part + 1 + chunks])[0]
-        block_here = gather(got)
-        over = tie([block_here], lefts[part - 1][1:3])[0][0] if part else block_here
-        row_parts, moved = all_rows(block_here, over)
-        halves.append(row_parts)
+        before, beside = (moved + lefts[0][1:2], lefts[0][2:] + lefts[-1][2:3]) if part else ([], [])
+        halves.append(all_rows(gather(got), before, beside))
+        moved = halves[-1][cores:]
     right = [half[u] for u in range(row_blocks) for half in halves]
     sigms, grads, backs = [], [], []
     for first, left in zip(firsts, lefts):
         *grad_comb, sigm = middle(exchange(combine(left)), first)
         sigms.append(sigm)
         grads.append(exchange(grad_comb))
+    left_grads = []
     for part in range(chunks):
         backs.append(list(left_back(grads[part])))
+        left_grads.append(exchange(backs[part]))
         if part == 0 and chunks > 1:
-            grads[-1] = tie(grads[-1], backs[0])[0]
-    left_grads = [exchange(back) for back in backs]
+            grads[-1] = tie(grads[-1], backs[0], left_grads[0][1:2])[0]
     right_grads = [
         exchange(split(own_rows(partials, back[1:3]))) for partials, back in zip(right_back(grads, lefts), left_grads)
     ]

time: 662 us -> 686 us (1.036)
  waiting for transfers between devices: 419 us -> 443 us
    ppermute x12, waiting for transfers between devices: 95.2 us -> 109 us  [swap(): lax.ppermute(array, axis, [(a, a ^ by) for a in range(lax.axis_size(axis))])]
    ppermute x36, waiting for transfers between devices: 324 us -> 334 us  [exchange(): lax.ppermute(sent[s], 'ch', [(a, a ^ s) for a in range(groups)])]
  transfers between devices with their start and end apart: 48 -> 48, of which waited for: 26 -> 29; matrix products, arithmetic and copies ran while one was open for 2% -> 2% of each run, Pallas kernels for 18% -> 17%
where the time goes in v8:
time: 686 us; the launch traced here: 679 us
  waiting for transfers between devices  443 us (65%)
  Pallas kernels  160 us (23%)
  starting transfers between devices  50.4 us (7%)
  local copies, waits for them, and re-layouts  16.6 us (2%)
  other arithmetic  8.95 us (1%)
    ppermute x36, waiting for transfers between devices, exchange(): lax.ppermute(sent[s], 'ch', [(a, a ^ s) for a in range(groups)])  334 us
    ppermute x12, waiting for transfers between devices, swap(): lax.ppermute(array, axis, [(a, a ^ by) for a in range(lax.axis_size(axis))])  109 us
    pallas_call x4, Pallas kernels, with_right(): pl.pallas_call(functools.partial(kernel, groups, row_blocks, chunks), gri...  45.5 us
    ppermute x36, starting transfers between devices, exchange(): lax.ppermute(sent[s], 'ch', [(a, a ^ s) for a in range(groups)])  38.2 us
    pallas_call x4, Pallas kernels, project(): pl.pallas_call(functools.partial(project_kernel, step), grid=(count,), in...  31.9 us
    pallas_call x2, Pallas kernels, last(): pl.pallas_call(functools.partial(last_kernel, step, groups), grid=(blocks...  29.8 us
    pallas_call x2, Pallas kernels, middle(): pl.pallas_call(functools.partial(middle_kernel, step, groups), grid=(bloc...  21.8 us
    pallas_call x1, Pallas kernels, right_back(): pl.pallas_call(functools.partial(right_kernel, groups, row_blocks, chunks...  14.4 us
  transfers between devices with their start and end apart: 48, of which 29 were waited for; matrix products, arithmetic and copies ran while one was open for 2% of the time, Pallas kernels for 17%

profile of v8, /device:TPU:15, one launch (start us, length us, event | category | flops | bytes accessed | tf_op | source)
XLA Modules:
  0.0 679.3 jit_solution(9312296220439593751)
XLA Ops:
  37.2 22.4 %collective-permute-done.2.refs_3_ = bf16[64,32,128]{2,1,0:T(8,128)(2,1)S(1)} collective-permute-done((bf16[64,32,128]{2,1,0:T(8,128)(2,1)}, bf16[64,32,128]{2,1,0:T(8,128)(2,1)S(1)}, u32[]{:S(2)}, u32[]{:S(2)}) %collective-permute-start.2) | collective-permute-done | bytes 524320 | tf_op jit(solution)/shard_map/ppermute | solution.py:292
  69.8 46.8 %collective-permute-done.7.refs_4_ = bf16[32,64,512]{2,1,0:T(8,128)(2,1)S(1)} collective-permute-done((bf16[32,64,512]{2,1,0:T(8,128)(2,1)}, bf16[32,64,512]{2,1,0:T(8,128)(2,1)S(1)}, u32[]{:S(2)}, u32[]{:S(2)}) %collective-permute-start.7) | collective-permute-done | bytes 2097184 | tf_op jit(solution)/shard_map/ppermute | solution.py:328
  128.4 12.1 %collective-permute-done.3.refs_1_ = bf16[64,32,128]{2,1,0:T(8,128)(2,1)S(1)} collective-permute-done((bf16[64,32,128]{2,1,0:T(8,128)(2,1)}, bf16[64,32,128]{2,1,0:T(8,128)(2,1)S(1)}, u32[]{:S(2)}, u32[]{:S(2)}) %collective-permute-start.3) | collective-permute-done | bytes 524320 | tf_op jit(solution)/shard_map/ppermute | solution.py:292
  140.5 13.5 %collective-permute-done.4.refs_2_ = bf16[64,32,128]{2,1,0:T(8,128)(2,1)S(1)} collective-permute-done((bf16[64,32,128]{2,1,0:T(8,128)(2,1)}, bf16[64,32,128]{2,1,0:T(8,128)(2,1)S(1)}, u32[]{:S(2)}, u32[]{:S(2)}) %collective-permute-start.4) | collective-permute-done | bytes 524320 | tf_op jit(solution)/shard_map/ppermute | solution.py:292
  154.0 12.2 %collective-permute-done.5.refs_3_ = bf16[64,32,128]{2,1,0:T(8,128)(2,1)S(1)} collective-permute-done((bf16[64,32,128]{2,1,0:T(8,128)(2,1)}, bf16[64,32,128]{2,1,0:T(8,128)(2,1)S(1)}, u32[]{:S(2)}, u32[]{:S(2)}) %collective-permute-start.5) | collective-permute-done | bytes 524320 | tf_op jit(solution)/shard_map/ppermute | solution.py:292
  171.6 13.5 %collective-permute-done.10.refs_9_ = bf16[64,32,128]{2,1,0:T(8,128)(2,1)S(1)} collective-permute-done((bf16[64,32,128]{2,1,0:T(8,128)(2,1)S(1)}, bf16[64,32,128]{2,1,0:T(8,128)(2,1)S(1)}, u32[]{:S(2)}, u32[]{:S(2)}) %collective-permute-start.10) | collective-permute-done | bytes 524320 | tf_op jit(solution)/shard_map/ppermute | solution.py:292
  189.1 41.8 %collective-permute-done.14.refs_10_.refs_14_ = bf16[64,32,128]{2,1,0:T(8,128)(2,1)S(1)} collective-permute-done((bf16[64,32,128]{2,1,0:T(8,128)(2,1)S(1)}, bf16[64,32,128]{2,1,0:T(8,128)(2,1)S(1)}, u32[]{:S(2)}, u32[]{:S(2)}) %collective-permute-start.14) | collective-permute-done | bytes 524320 | tf_op jit(solution)/shard_map/ppermute | solution.py:292
  230.9 11.2 %collective-permute-done.12.refs_10_ = bf16[64,32,128]{2,1,0:T(8,128)(2,1)} collective-permute-done((bf16[64,32,128]{2,1,0:T(8,128)(2,1)S(1)}, bf16[64,32,128]{2,1,0:T(8,128)(2,1)}, u32[]{:S(2)}, u32[]{:S(2)}) %collective-permute-start.12) | collective-permute-done | bytes 524320 | tf_op jit(solution)/shard_map/ppermute | solution.py:292
  242.1 12.3 %collective-permute-done.13.refs_11_ = bf16[64,32,128]{2,1,0:T(8,128)(2,1)} collective-permute-done((bf16[64,32,128]{2,1,0:T(8,128)(2,1)S(1)}, bf16[64,32,128]{2,1,0:T(8,128)(2,1)}, u32[]{:S(2)}, u32[]{:S(2)}) %collective-permute-start.13) | collective-permute-done | bytes 524320 | tf_op jit(solution)/shard_map/ppermute | solution.py:292
  260.1 12.4 %shard_map.90 = (bf16[64,32,128]{2,1,0:T(8,128)(2,1)}, bf16[64,32,128]{2,1,0:T(8,128)(2,1)}, bf16[64,32,128]{2,1,0:T(8,128)(2,1)}, bf16[64,32,128]{2,1,0:T(8,128)(2,1)}) custom-call(s32[4]{0:T(128)} %pad_add_fusion.place_ref, bf16[32,64,512]{2,1,0:T(8,128)(2,1)} %shard_map.85.refs_0_, bf16[32,64,512]{2,1,0:T(8,128)(2,1)} %shard_map.87.refs_1_, ...), custom_call_target="tpu_custom_call" | custom-call | flops 1073741824 | bytes 20971520 | tf_op jit(solution)/shard_map/pallas_call | solution.py:352
  275.9 12.3 %shard_map.88 = (bf16[64,32,128]{2,1,0:T(8,128)(2,1)}, bf16[64,32,128]{2,1,0:T(8,128)(2,1)}, bf16[64,32,128]{2,1,0:T(8,128)(2,1)}, bf16[64,32,128]{2,1,0:T(8,128)(2,1)}) custom-call(s32[4]{0:T(128)} %pad_add_fusion.place_ref, bf16[32,64,512]{2,1,0:T(8,128)(2,1)} %shard_map.85.refs_0_, bf16[32,64,512]{2,1,0:T(8,128)(2,1)} %shard_map.87.refs_1_, ...), custom_call_target="tpu_custom_call" | custom-call | flops 1073741824 | bytes 20971520 | tf_op jit(solution)/shard_map/pallas_call | solution.py:352
  304.5 22.8 %collective-permute-done.23.refs_3_ = bf16[64,32,128]{2,1,0:T(8,128)(2,1)S(1)} collective-permute-done((bf16[64,32,128]{2,1,0:T(8,128)(2,1)}, bf16[64,32,128]{2,1,0:T(8,128)(2,1)S(1)}, u32[]{:S(2)}, u32[]{:S(2)}) %collective-permute-start.23) | collective-permute-done | bytes 524320 | tf_op jit(solution)/shard_map/ppermute | solution.py:292
  341.8 17.3 %collective-permute-done.19.refs_2_ = bf16[64,32,128]{2,1,0:T(8,128)(2,1)S(1)} collective-permute-done((bf16[64,32,128]{2,1,0:T(8,128)(2,1)}, bf16[64,32,128]{2,1,0:T(8,128)(2,1)S(1)}, u32[]{:S(2)}, u32[]{:S(2)}) %collective-permute-start.19) | collective-permute-done | bytes 524320 | tf_op jit(solution)/shard_map/ppermute | solution.py:292
  359.1 35.5 %collective-permute-done.20.refs_3_ = bf16[64,32,128]{2,1,0:T(8,128)(2,1)S(1)} collective-permute-done((bf16[64,32,128]{2,1,0:T(8,128)(2,1)}, bf16[64,32,128]{2,1,0:T(8,128)(2,1)S(1)}, u32[]{:S(2)}, u32[]{:S(2)}) %collective-permute-start.20) | collective-permute-done | bytes 524320 | tf_op jit(solution)/shard_map/ppermute | solution.py:292
  428.4 20.8 %collective-permute-done.31.refs_6_.refs_10_ = bf16[64,32,128]{2,1,0:T(8,128)(2,1)S(1)} collective-permute-done((bf16[64,32,128]{2,1,0:T(8,128)(2,1)}, bf16[64,32,128]{2,1,0:T(8,128)(2,1)S(1)}, u32[]{:S(2)}, u32[]{:S(2)}) %collective-permute-start.31) | collective-permute-done | bytes 524320 | tf_op jit(solution)/shard_map/ppermute | solution.py:292
  449.2 13.0 %collective-permute-done.32.refs_7_.refs_11_ = bf16[64,32,128]{2,1,0:T(8,128)(2,1)S(1)} collective-permute-done((bf16[64,32,128]{2,1,0:T(8,128)(2,1)}, bf16[64,32,128]{2,1,0:T(8,128)(2,1)S(1)}, u32[]{:S(2)}, u32[]{:S(2)}) %collective-permute-start.32) | collective-permute-done | bytes 524320 | tf_op jit(solution)/shard_map/ppermute | solution.py:292
  463.0 14.4 %shard_map.93 = (bf16[32,64,512]{2,1,0:T(8,128)(2,1)}, bf16[32,64,512]{2,1,0:T(8,128)(2,1)}, bf16[32,64,512]{2,1,0:T(8,128)(2,1)}, bf16[32,64,512]{2,1,0:T(8,128...) custom-call(s32[4]{0:T(128)} %pad_add_fusion.place_ref, ...), custom_call_target="tpu_custom_call" | custom-call | flops 2147483648 | bytes 25165824 | tf_op jit(solution)/shard_map/pallas_call | solution.py:377
  512.2 11.1 %collective-permute-done.40.refs_2_ = bf16[64,32,128]{2,1,0:T(8,128)(2,1)S(1)} collective-permute-done((bf16[64,32,128]{2,1,0:T(8,128)(2,1)}, bf16[64,32,128]{2,1,0:T(8,128)(2,1)S(1)}, u32[]{:S(2)}, u32[]{:S(2)}) %collective-permute-start.40) | collective-permute-done | bytes 524320 | tf_op jit(solution)/shard_map/ppermute | solution.py:292
  524.8 21.6 %collective-permute-done.35.refs_2_ = bf16[32,64,512]{2,1,0:T(8,128)(2,1)} collective-permute-done((bf16[32,64,512]{2,1,0:T(8,128)(2,1)S(1)}, bf16[32,64,512]{2,1,0:T(8,128)(2,1)}, u32[]{:S(2)}, u32[]{:S(2)}) %collective-permute-start.35) | collective-permute-done | bytes 2097184 | tf_op jit(solution)/shard_map/ppermute | solution.py:328
  554.6 36.5 %collective-permute-done.44.refs_2_ = bf16[32,64,512]{2,1,0:T(8,128)(2,1)S(1)} collective-permute-done((bf16[32,64,512]{2,1,0:T(8,128)(2,1)}, bf16[32,64,512]{2,1,0:T(8,128)(2,1)S(1)}, u32[]{:S(2)}, u32[]{:S(2)}) %collective-permute-start.44) | collective-permute-done | bytes 2097184 | tf_op jit(solution)/shard_map/ppermute | solution.py:328
  605.4 14.9 %shard_map.95.held_ref = bf16[128,128,128]{2,1,0:T(8,128)(2,1)} custom-call(bf16[128,128,128]{2,1,0:T(8,128)(2,1)} %pair_ref.15, bf16[64,128,128]{2,1,0:T(8,128)(2,1)} %get-tuple-element.116.sigm_ref, f32[16,1,1024]{2,1,0:T(1,128)} %broadcast_multiply_fusion.mask_ref, f32[1,128]{1,0:T(1,128)} %bitcast.39, ...), custom_call_target="tpu_custom_call", output_to_operand_aliasing={{}: (5, {})} | custom-call | flops 2415919104 | bytes 10485760 | tf_op jit(solution)/shard_map/pallas_call | solution.py:278
  620.6 30.6 %collective-permute-done.46.refs_6_ = bf16[64,32,128]{2,1,0:T(8,128)(2,1)S(1)} collective-permute-done((bf16[64,32,128]{2,1,0:T(8,128)(2,1)}, bf16[64,32,128]{2,1,0:T(8,128)(2,1)S(1)}, u32[]{:S(2)}, u32[]{:S(2)}) %collective-permute-start.46) | collective-permute-done | bytes 524320 | tf_op jit(solution)/shard_map/ppermute | solution.py:292
  651.2 12.4 %collective-permute-done.47.refs_7_ = bf16[64,32,128]{2,1,0:T(8,128)(2,1)S(1)} collective-permute-done((bf16[64,32,128]{2,1,0:T(8,128)(2,1)}, bf16[64,32,128]{2,1,0:T(8,128)(2,1)S(1)}, u32[]{:S(2)}, u32[]{:S(2)}) %collective-permute-start.47) | collective-permute-done | bytes 524320 | tf_op jit(solution)/shard_map/ppermute | solution.py:292
  664.4 14.9 %shard_map.98 = bf16[128,128,128]{2,1,0:T(8,128)(2,1)} custom-call(bf16[128,128,128]{2,1,0:T(8,128)(2,1)} %pair_ref.15, bf16[64,128,128]{2,1,0:T(8,128)(2,1)} %get-tuple-element.111.sigm_ref, f32[16,1,1024]{2,1,0:T(1,128)} %broadcast_multiply_fusion.mask_ref, f32[1,128]{1,0:T(1,128)} %bitcast.40, ...), custom_call_target="tpu_custom_call", output_to_operand_aliasing={{}: (5, {})} | custom-call | flops 2415919104 | bytes 10485760 | tf_op jit(solution)/shard_map/pallas_call | solution.py:278
  (218 shorter events, 202.8 us)
Async XLA Ops:
  69.5 47.1 %collective-permute-start.7 = (bf16[32,64,512]{2,1,0:T(8,128)(2,1)}, bf16[32,64,512]{2,1,0:T(8,128)(2,1)S(1)}, u32[]{:S(2)}, u32[]{:S(2)}) collective-permute-start(bf16[32,64,512]{2,1,0:T(8,128)(2,1)} %shard_map.85.refs_0_), channel_id=1, source_target_pairs={{0,2},{2,0},{1,3},{3,1},{4,6},{6,4},{5,7},{7,5},{8,10},{10,8},{9,1... | collective-permute-start | bytes 6291464 | tf_op jit(solution)/shard_map/ppermute | solution.py:328
  116.6 49.6 %collective-permute-start.8 = (bf16[32,64,512]{2,1,0:T(8,128)(2,1)S(1)}, bf16[32,64,512]{2,1,0:T(8,128)(2,1)S(1)}, u32[]{:S(2)}, u32[]{:S(2)}) collective-permute-start(bf16[32,64,512]{2,1,0:T(8,128)(2,1)S(1)} %collective-permute-done.7.refs_4_), channel_id=1, source_target_pairs={{0,1},{1,0},{2,3},{3,2},{4,5},{5,4},{6,7},{7,6},{8,9},{9,8},{10,11... | collective-permute-start | bytes 6291464 | tf_op jit(solution)/shard_map/ppermute | solution.py:328
  120.3 45.9 %collective-permute-start.5 = (bf16[64,32,128]{2,1,0:T(8,128)(2,1)}, bf16[64,32,128]{2,1,0:T(8,128)(2,1)S(1)}, u32[]{:S(2)}, u32[]{:S(2)}) collective-permute-start(bf16[64,32,128]{2,1,0:T(8,128)(2,1)} %get-tuple-element.87), channel_id=1, source_target_pairs={{0,12},{4,8},{8,4},{12,0},{1,13},{5,9},{9,5},{13,1},{2,14},{6,10},... | collective-permute-start | bytes 1572872 | tf_op jit(solution)/shard_map/ppermute | solution.py:292
  185.1 69.3 %collective-permute-start.11 = (bf16[32,64,512]{2,1,0:T(8,128)(2,1)}, bf16[32,64,512]{2,1,0:T(8,128)(2,1)}, u32[]{:S(2)}, u32[]{:S(2)}) collective-permute-start(bf16[32,64,512]{2,1,0:T(8,128)(2,1)} %shard_map.87.refs_1_), channel_id=1, source_target_pairs={{0,2},{2,0},{1,3},{3,1},{4,6},{6,4},{5,7},{7,5},{8,10},{10,8},{9,1... | collective-permute-start | bytes 6291464 | tf_op jit(solution)/shard_map/ppermute | solution.py:328
  185.4 45.5 %collective-permute-start.14 = (bf16[64,32,128]{2,1,0:T(8,128)(2,1)S(1)}, bf16[64,32,128]{2,1,0:T(8,128)(2,1)S(1)}, u32[]{:S(2)}, u32[]{:S(2)}) collective-permute-start(bf16[64,32,128]{2,1,0:T(8,128)(2,1)S(1)} %copy-done.49), channel_id=1, source_target_pairs={{0,8},{4,12},{8,0},{12,4},{1,9},{5,13},{9,1},{13,5},{2,10},{6,14},... | collective-permute-start | bytes 1572872 | tf_op jit(solution)/shard_map/ppermute | solution.py:292
  186.6 55.5 %collective-permute-start.12 = (bf16[64,32,128]{2,1,0:T(8,128)(2,1)S(1)}, bf16[64,32,128]{2,1,0:T(8,128)(2,1)}, u32[]{:S(2)}, u32[]{:S(2)}) collective-permute-start(bf16[64,32,128]{2,1,0:T(8,128)(2,1)S(1)} %copy-done.47), channel_id=1, source_target_pairs={{0,8},{4,12},{8,0},{12,4},{1,9},{5,13},{9,1},{13,5},{2,10},{6,14},... | collective-permute-start | bytes 1572872 | tf_op jit(solution)/shard_map/ppermute | solution.py:292
  187.8 66.6 %collective-permute-start.13 = (bf16[64,32,128]{2,1,0:T(8,128)(2,1)S(1)}, bf16[64,32,128]{2,1,0:T(8,128)(2,1)}, u32[]{:S(2)}, u32[]{:S(2)}) collective-permute-start(bf16[64,32,128]{2,1,0:T(8,128)(2,1)S(1)} %copy-done.46), channel_id=1, source_target_pairs={{0,12},{4,8},{8,4},{12,0},{1,13},{5,9},{9,5},{13,1},{2,14},{6,10},... | collective-permute-start | bytes 1572872 | tf_op jit(solution)/shard_map/ppermute | solution.py:292
  275.0 52.4 %collective-permute-start.23 = (bf16[64,32,128]{2,1,0:T(8,128)(2,1)}, bf16[64,32,128]{2,1,0:T(8,128)(2,1)S(1)}, u32[]{:S(2)}, u32[]{:S(2)}) collective-permute-start(bf16[64,32,128]{2,1,0:T(8,128)(2,1)} %get-tuple-element.115), channel_id=1, source_target_pairs={{0,12},{4,8},{8,4},{12,0},{1,13},{5,9},{9,5},{13,1},{2,14},{6,10},... | collective-permute-start | bytes 1572872 | tf_op jit(solution)/shard_map/ppermute | solution.py:292
  288.3 52.6 %collective-permute-start.18 = (bf16[64,32,128]{2,1,0:T(8,128)(2,1)}, bf16[64,32,128]{2,1,0:T(8,128)(2,1)S(1)}, u32[]{:S(2)}, u32[]{:S(2)}) collective-permute-start(bf16[64,32,128]{2,1,0:T(8,128)(2,1)} %get-tuple-element.108), channel_id=1, source_target_pairs={{0,4},{4,0},{8,12},{12,8},{1,5},{5,1},{9,13},{13,9},{2,6},{6,2},{1... | collective-permute-start | bytes 1572872 | tf_op jit(solution)/shard_map/ppermute | solution.py:292
  297.9 61.2 %collective-permute-start.19 = (bf16[64,32,128]{2,1,0:T(8,128)(2,1)}, bf16[64,32,128]{2,1,0:T(8,128)(2,1)S(1)}, u32[]{:S(2)}, u32[]{:S(2)}) collective-permute-start(bf16[64,32,128]{2,1,0:T(8,128)(2,1)} %get-tuple-element.109), channel_id=1, source_target_pairs={{0,8},{4,12},{8,0},{12,4},{1,9},{5,13},{9,1},{13,5},{2,10},{6,14},... | collective-permute-start | bytes 1572872 | tf_op jit(solution)/shard_map/ppermute | solution.py:292
  303.8 90.9 %collective-permute-start.20 = (bf16[64,32,128]{2,1,0:T(8,128)(2,1)}, bf16[64,32,128]{2,1,0:T(8,128)(2,1)S(1)}, u32[]{:S(2)}, u32[]{:S(2)}) collective-permute-start(bf16[64,32,128]{2,1,0:T(8,128)(2,1)} %get-tuple-element.110), channel_id=1, source_target_pairs={{0,12},{4,8},{8,4},{12,0},{1,13},{5,9},{9,5},{13,1},{2,14},{6,10},... | collective-permute-start | bytes 1572872 | tf_op jit(solution)/shard_map/ppermute | solution.py:292
  339.1 68.9 %collective-permute-start.24 = (bf16[64,32,128]{2,1,0:T(8,128)(2,1)}, bf16[64,32,128]{2,1,0:T(8,128)(2,1)S(1)}, u32[]{:S(2)}, u32[]{:S(2)}) collective-permute-start(bf16[64,32,128]{2,1,0:T(8,128)(2,1)} %get-tuple-element.118), channel_id=1, source_target_pairs={{0,4},{4,0},{8,12},{12,8},{1,5},{5,1},{9,13},{13,9},{2,6},{6,2},{1... | collective-permute-start | bytes 1572872 | tf_op jit(solution)/shard_map/ppermute | solution.py:292
  339.2 70.0 %collective-permute-start.25 = (bf16[64,32,128]{2,1,0:T(8,128)(2,1)}, bf16[64,32,128]{2,1,0:T(8,128)(2,1)S(1)}, u32[]{:S(2)}, u32[]{:S(2)}) collective-permute-start(bf16[64,32,128]{2,1,0:T(8,128)(2,1)} %get-tuple-element.119), channel_id=1, source_target_pairs={{0,8},{4,12},{8,0},{12,4},{1,9},{5,13},{9,1},{13,5},{2,10},{6,14},... | collective-permute-start | bytes 1572872 | tf_op jit(solution)/shard_map/ppermute | solution.py:292
  340.9 76.2 %collective-permute-start.26 = (bf16[64,32,128]{2,1,0:T(8,128)(2,1)}, bf16[64,32,128]{2,1,0:T(8,128)(2,1)S(1)}, u32[]{:S(2)}, u32[]{:S(2)}) collective-permute-start(bf16[64,32,128]{2,1,0:T(8,128)(2,1)} %get-tuple-element.120), channel_id=1, source_target_pairs={{0,12},{4,8},{8,4},{12,0},{1,13},{5,9},{9,5},{13,1},{2,14},{6,10},... | collective-permute-start | bytes 1572872 | tf_op jit(solution)/shard_map/ppermute | solution.py:292
  408.0 54.1 %collective-permute-start.32 = (bf16[64,32,128]{2,1,0:T(8,128)(2,1)}, bf16[64,32,128]{2,1,0:T(8,128)(2,1)S(1)}, u32[]{:S(2)}, u32[]{:S(2)}) collective-permute-start(bf16[64,32,128]{2,1,0:T(8,128)(2,1)} %get-tuple-element.128), channel_id=1, source_target_pairs={{0,12},{4,8},{8,4},{12,0},{1,13},{5,9},{9,5},{13,1},{2,14},{6,10},... | collective-permute-start | bytes 1572872 | tf_op jit(solution)/shard_map/ppermute | solution.py:292
  500.8 45.6 %collective-permute-start.35 = (bf16[32,64,512]{2,1,0:T(8,128)(2,1)S(1)}, bf16[32,64,512]{2,1,0:T(8,128)(2,1)}, u32[]{:S(2)}, u32[]{:S(2)}) collective-permute-start(bf16[32,64,512]{2,1,0:T(8,128)(2,1)S(1)} %add_convert_fusion.1), channel_id=1, source_target_pairs={{0,2},{2,0},{1,3},{3,1},{4,6},{6,4},{5,7},{7,5},{8,10},{10,8},{9,1... | collective-permute-start | bytes 6291464 | tf_op jit(solution)/shard_map/ppermute | solution.py:328
  502.0 52.2 %collective-permute-start.42 = (bf16[32,64,512]{2,1,0:T(8,128)(2,1)}, bf16[32,64,512]{2,1,0:T(8,128)(2,1)S(1)}, u32[]{:S(2)}, u32[]{:S(2)}) collective-permute-start(bf16[32,64,512]{2,1,0:T(8,128)(2,1)} %get-tuple-element.147), channel_id=1, source_target_pairs={{0,1},{1,0},{2,3},{3,2},{4,5},{5,4},{6,7},{7,6},{8,9},{9,8},{10,11... | collective-permute-start | bytes 6291464 | tf_op jit(solution)/shard_map/ppermute | solution.py:328
  523.2 67.9 %collective-permute-start.44 = (bf16[32,64,512]{2,1,0:T(8,128)(2,1)}, bf16[32,64,512]{2,1,0:T(8,128)(2,1)S(1)}, u32[]{:S(2)}, u32[]{:S(2)}) collective-permute-start(bf16[32,64,512]{2,1,0:T(8,128)(2,1)} %add_convert_fusion), channel_id=1, source_target_pairs={{0,2},{2,0},{1,3},{3,1},{4,6},{6,4},{5,7},{7,5},{8,10},{10,8},{9,1... | collective-permute-start | bytes 6291464 | tf_op jit(solution)/shard_map/ppermute | solution.py:328
  524.4 72.8 %collective-permute-start.29 = (bf16[64,32,128]{2,1,0:T(8,128)(2,1)}, bf16[64,32,128]{2,1,0:T(8,128)(2,1)S(1)}, u32[]{:S(2)}, u32[]{:S(2)}) collective-permute-start(bf16[64,32,128]{2,1,0:T(8,128)(2,1)} %get-tuple-element.124), channel_id=1, source_target_pairs={{0,12},{4,8},{8,4},{12,0},{1,13},{5,9},{9,5},{13,1},{2,14},{6,10},... | collective-permute-start | bytes 1572872 | tf_op jit(solution)/shard_map/ppermute | solution.py:292
  551.0 49.3 %collective-permute-start.36 = (bf16[64,32,128]{2,1,0:T(8,128)(2,1)}, bf16[64,32,128]{2,1,0:T(8,128)(2,1)S(1)}, u32[]{:S(2)}, u32[]{:S(2)}) collective-permute-start(bf16[64,32,128]{2,1,0:T(8,128)(2,1)} %get-tuple-element.139), channel_id=1, source_target_pairs={{0,4},{4,0},{8,12},{12,8},{1,5},{5,1},{9,13},{13,9},{2,6},{6,2},{1... | collective-permute-start | bytes 1572872 | tf_op jit(solution)/shard_map/ppermute | solution.py:292
  553.4 47.2 %collective-permute-start.37 = (bf16[64,32,128]{2,1,0:T(8,128)(2,1)}, bf16[64,32,128]{2,1,0:T(8,128)(2,1)S(1)}, u32[]{:S(2)}, u32[]{:S(2)}) collective-permute-start(bf16[64,32,128]{2,1,0:T(8,128)(2,1)} %get-tuple-element.140), channel_id=1, source_target_pairs={{0,8},{4,12},{8,0},{12,4},{1,9},{5,13},{9,1},{13,5},{2,10},{6,14},... | collective-permute-start | bytes 1572872 | tf_op jit(solution)/shard_map/ppermute | solution.py:292
  554.2 48.1 %collective-permute-start.38 = (bf16[64,32,128]{2,1,0:T(8,128)(2,1)}, bf16[64,32,128]{2,1,0:T(8,128)(2,1)}, u32[]{:S(2)}, u32[]{:S(2)}) collective-permute-start(bf16[64,32,128]{2,1,0:T(8,128)(2,1)} %get-tuple-element.141), channel_id=1, source_target_pairs={{0,12},{4,8},{8,4},{12,0},{1,13},{5,9},{9,5},{13,1},{2,14},{6,10},... | collective-permute-start | bytes 1572872 | tf_op jit(solution)/shard_map/ppermute | solution.py:292
  600.3 50.8 %collective-permute-start.46 = (bf16[64,32,128]{2,1,0:T(8,128)(2,1)}, bf16[64,32,128]{2,1,0:T(8,128)(2,1)S(1)}, u32[]{:S(2)}, u32[]{:S(2)}) collective-permute-start(bf16[64,32,128]{2,1,0:T(8,128)(2,1)} %get-tuple-element.153), channel_id=1, source_target_pairs={{0,8},{4,12},{8,0},{12,4},{1,9},{5,13},{9,1},{13,5},{2,10},{6,14},... | collective-permute-start | bytes 1572872 | tf_op jit(solution)/shard_map/ppermute | solution.py:292
  600.6 63.0 %collective-permute-start.47 = (bf16[64,32,128]{2,1,0:T(8,128)(2,1)}, bf16[64,32,128]{2,1,0:T(8,128)(2,1)S(1)}, u32[]{:S(2)}, u32[]{:S(2)}) collective-permute-start(bf16[64,32,128]{2,1,0:T(8,128)(2,1)} %get-tuple-element.154), channel_id=1, source_target_pairs={{0,12},{4,8},{8,4},{12,0},{1,13},{5,9},{9,5},{13,1},{2,14},{6,10},... | collective-permute-start | bytes 1572872 | tf_op jit(solution)/shard_map/ppermute | solution.py:292
  (74 other events, 1812.6 us)

commit v9 on v8

--- a/solution.py
+++ b/solution.py
@@ -394,11 +394,12 @@
     sent = [list(project(weight, first, blocks)) for weight in (right_w, left_w) for first in firsts]
     lefts = [exchange(pieces_of) for pieces_of in sent[chunks:]]
     halves, moved = [], []
+    rights = [exchange(pieces_of) for pieces_of in sent[:chunks]]
     for part in range(chunks):
-        got = tie(exchange(sent[part]), moved, *sent[part + 1:part + 1 + chunks])[0]
-        before, beside = (moved + lefts[0][1:2], lefts[0][2:] + lefts[-1][2:3]) if part else ([], [])
+        got = tie(rights[part], moved, *sent[part + 1:part + 1 + chunks])[0]
+        before, beside = (moved + lefts[0][1:2], lefts[0][2:] + lefts[-1][2:3]) if part else ([], rights[-1][1:])
         halves.append(all_rows(gather(got), before, beside))
-        moved = halves[-1][cores:]
+        moved = halves[-1][cores::cores]
     right = [half[u] for u in range(row_blocks) for half in halves]
     sigms, grads, backs = [], [], []
     for first, left in zip(firsts, lefts):

time: 686 us -> 638 us (0.930)
  waiting for transfers between devices: 443 us -> 396 us
    ppermute x12, waiting for transfers between devices: 109 us -> 63.5 us  [swap(): lax.ppermute(array, axis, [(a, a ^ by) for a in range(lax.axis_size(axis))])]
  transfers between devices with their start and end apart: 48 -> 48, of which waited for: 29 -> 28; matrix products, arithmetic and copies ran while one was open for 2% -> 2% of each run, Pallas kernels for 17% -> 18%
where the time goes in v9:
time: 638 us; the launch traced here: 632 us
  waiting for transfers between devices  396 us (62%)
  Pallas kernels  159 us (25%)
  starting transfers between devices  50.1 us (8%)
  local copies, waits for them, and re-layouts  16.8 us (3%)
  other arithmetic  9.03 us (1%)
    ppermute x36, waiting for transfers between devices, exchange(): lax.ppermute(sent[s], 'ch', [(a, a ^ s) for a in range(groups)])  333 us
    ppermute x12, waiting for transfers between devices, swap(): lax.ppermute(array, axis, [(a, a ^ by) for a in range(lax.axis_size(axis))])  63.5 us
    pallas_call x4, Pallas kernels, with_right(): pl.pallas_call(functools.partial(kernel, groups, row_blocks, chunks), gri...  45.2 us
    ppermute x36, starting transfers between devices, exchange(): lax.ppermute(sent[s], 'ch', [(a, a ^ s) for a in range(groups)])  37.7 us
    pallas_call x4, Pallas kernels, project(): pl.pallas_call(functools.partial(project_kernel, step), grid=(count,), in...  32 us
    pallas_call x2, Pallas kernels, last(): pl.pallas_call(functools.partial(last_kernel, step, groups), grid=(blocks...  29.8 us
    pallas_call x2, Pallas kernels, middle(): pl.pallas_call(functools.partial(middle_kernel, step, groups), grid=(bloc...  21.9 us
    pallas_call x1, Pallas kernels, right_back(): pl.pallas_call(functools.partial(right_kernel, groups, row_blocks, chunks...  14.3 us
  transfers between devices with their start and end apart: 48, of which 28 were waited for; matrix products, arithmetic and copies ran while one was open for 2% of the time, Pallas kernels for 18%

profile of v9, /device:TPU:15, one launch (start us, length us, event | category | flops | bytes accessed | tf_op | source)
XLA Modules:
  0.0 632.2 jit_solution(7430142186319108556)
XLA Ops:
  37.3 22.4 %collective-permute-done.2.refs_3_ = bf16[64,32,128]{2,1,0:T(8,128)(2,1)S(1)} collective-permute-done((bf16[64,32,128]{2,1,0:T(8,128)(2,1)}, bf16[64,32,128]{2,1,0:T(8,128)(2,1)S(1)}, u32[]{:S(2)}, u32[]{:S(2)}) %collective-permute-start.2) | collective-permute-done | bytes 524320 | tf_op jit(solution)/shard_map/ppermute | solution.py:292
  80.6 10.8 %collective-permute-done.3.refs_1_ = bf16[64,32,128]{2,1,0:T(8,128)(2,1)S(1)} collective-permute-done((bf16[64,32,128]{2,1,0:T(8,128)(2,1)S(1)}, bf16[64,32,128]{2,1,0:T(8,128)(2,1)S(1)}, u32[]{:S(2)}, u32[]{:S(2)}) %collective-permute-start.3) | collective-permute-done | bytes 524320 | tf_op jit(solution)/shard_map/ppermute | solution.py:292
  95.1 22.5 %collective-permute-done.5.refs_3_ = bf16[64,32,128]{2,1,0:T(8,128)(2,1)S(1)} collective-permute-done((bf16[64,32,128]{2,1,0:T(8,128)(2,1)S(1)}, bf16[64,32,128]{2,1,0:T(8,128)(2,1)S(1)}, u32[]{:S(2)}, u32[]{:S(2)}) %collective-permute-start.5) | collective-permute-done | bytes 524320 | tf_op jit(solution)/shard_map/ppermute | solution.py:292
  123.6 13.5 %collective-permute-done.9.refs_9_ = bf16[64,32,128]{2,1,0:T(8,128)(2,1)S(1)} collective-permute-done((bf16[64,32,128]{2,1,0:T(8,128)(2,1)S(1)}, bf16[64,32,128]{2,1,0:T(8,128)(2,1)S(1)}, u32[]{:S(2)}, u32[]{:S(2)}) %collective-permute-start.9) | collective-permute-done | bytes 524320 | tf_op jit(solution)/shard_map/ppermute | solution.py:292
  144.0 39.9 %collective-permute-done.13.refs_10_.refs_14_ = bf16[64,32,128]{2,1,0:T(8,128)(2,1)S(1)} collective-permute-done((bf16[64,32,128]{2,1,0:T(8,128)(2,1)S(1)}, bf16[64,32,128]{2,1,0:T(8,128)(2,1)S(1)}, u32[]{:S(2)}, u32[]{:S(2)}) %collective-permute-start.13) | collective-permute-done | bytes 524320 | tf_op jit(solution)/shard_map/ppermute | solution.py:292
  183.9 11.2 %collective-permute-done.11.refs_10_ = bf16[64,32,128]{2,1,0:T(8,128)(2,1)} collective-permute-done((bf16[64,32,128]{2,1,0:T(8,128)(2,1)S(1)}, bf16[64,32,128]{2,1,0:T(8,128)(2,1)}, u32[]{:S(2)}, u32[]{:S(2)}) %collective-permute-start.11) | collective-permute-done | bytes 524320 | tf_op jit(solution)/shard_map/ppermute | solution.py:292
  195.1 12.3 %collective-permute-done.12.refs_11_ = bf16[64,32,128]{2,1,0:T(8,128)(2,1)} collective-permute-done((bf16[64,32,128]{2,1,0:T(8,128)(2,1)S(1)}, bf16[64,32,128]{2,1,0:T(8,128)(2,1)}, u32[]{:S(2)}, u32[]{:S(2)}) %collective-permute-start.12) | collective-permute-done | bytes 524320 | tf_op jit(solution)/shard_map/ppermute | solution.py:292
  213.0 12.4 %shard_map.90 = (bf16[64,32,128]{2,1,0:T(8,128)(2,1)}, bf16[64,32,128]{2,1,0:T(8,128)(2,1)}, bf16[64,32,128]{2,1,0:T(8,128)(2,1)}, bf16[64,32,128]{2,1,0:T(8,128)(2,1)}) custom-call(s32[4]{0:T(128)} %pad_add_fusion.place_ref, bf16[32,64,512]{2,1,0:T(8,128)(2,1)} %shard_map.85.refs_0_, bf16[32,64,512]{2,1,0:T(8,128)(2,1)} %shard_map.87.refs_1_, ...), custom_call_target="tpu_custom_call" | custom-call | flops 1073741824 | bytes 20971520 | tf_op jit(solution)/shard_map/pallas_call | solution.py:352
  229.0 12.4 %shard_map.88 = (bf16[64,32,128]{2,1,0:T(8,128)(2,1)}, bf16[64,32,128]{2,1,0:T(8,128)(2,1)}, bf16[64,32,128]{2,1,0:T(8,128)(2,1)}, bf16[64,32,128]{2,1,0:T(8,128)(2,1)}) custom-call(s32[4]{0:T(128)} %pad_add_fusion.place_ref, bf16[32,64,512]{2,1,0:T(8,128)(2,1)} %shard_map.85.refs_0_, bf16[32,64,512]{2,1,0:T(8,128)(2,1)} %shard_map.87.refs_1_, ...), custom_call_target="tpu_custom_call" | custom-call | flops 1073741824 | bytes 20971520 | tf_op jit(solution)/shard_map/pallas_call | solution.py:352
  257.5 22.8 %collective-permute-done.23.refs_3_ = bf16[64,32,128]{2,1,0:T(8,128)(2,1)S(1)} collective-permute-done((bf16[64,32,128]{2,1,0:T(8,128)(2,1)}, bf16[64,32,128]{2,1,0:T(8,128)(2,1)S(1)}, u32[]{:S(2)}, u32[]{:S(2)}) %collective-permute-start.23) | collective-permute-done | bytes 524320 | tf_op jit(solution)/shard_map/ppermute | solution.py:292
  281.1 10.9 %shard_map.91 = (bf16[64,32,128]{2,1,0:T(8,128)(2,1)}, bf16[64,32,128]{2,1,0:T(8,128)(2,1)}, bf16[64,32,128]{2,1,0:T(8,128)(2,1)}, bf16[64,32,128]{2,1,0:T(8,128)(2,1)}, bf16[64,128,128]{2,1,0:T(8,128)(2,1)}) custom-call(bf16[128,128,128]{2,1,0:T(8,128)(2,1)} %pair_ref.15, bf16[128,128,128]{2,1,0:T(8,128)(2,1)} %gout_ref.3, f32[1,128]{1,0:T(1,128)} %bitcast.37, ...), custom_call_target="tpu_custom_call" | custom-call | flops 1073741824 | bytes 10485760 | tf_op jit(solution)/shard_map/pallas_call | solution.py:266
  294.7 17.3 %collective-permute-done.19.refs_2_ = bf16[64,32,128]{2,1,0:T(8,128)(2,1)S(1)} collective-permute-done((bf16[64,32,128]{2,1,0:T(8,128)(2,1)}, bf16[64,32,128]{2,1,0:T(8,128)(2,1)S(1)}, u32[]{:S(2)}, u32[]{:S(2)}) %collective-permute-start.19) | collective-permute-done | bytes 524320 | tf_op jit(solution)/shard_map/ppermute | solution.py:292
  312.1 35.5 %collective-permute-done.20.refs_3_ = bf16[64,32,128]{2,1,0:T(8,128)(2,1)S(1)} collective-permute-done((bf16[64,32,128]{2,1,0:T(8,128)(2,1)}, bf16[64,32,128]{2,1,0:T(8,128)(2,1)S(1)}, u32[]{:S(2)}, u32[]{:S(2)}) %collective-permute-start.20) | collective-permute-done | bytes 524320 | tf_op jit(solution)/shard_map/ppermute | solution.py:292
  348.4 11.0 %shard_map.89 = (bf16[64,32,128]{2,1,0:T(8,128)(2,1)}, bf16[64,32,128]{2,1,0:T(8,128)(2,1)}, bf16[64,32,128]{2,1,0:T(8,128)(2,1)}, bf16[64,32,128]{2,1,0:T(8,128)(2,1)}, bf16[64,128,128]{2,1,0:T(8,128)(2,1)}) custom-call(bf16[128,128,128]{2,1,0:T(8,128)(2,1)} %pair_ref.15, bf16[128,128,128]{2,1,0:T(8,128)(2,1)} %gout_ref.3, f32[1,128]{1,0:T(1,128)} %bitcast.38, ...), custom_call_target="tpu_custom_call" | custom-call | flops 1073741824 | bytes 10485760 | tf_op jit(solution)/shard_map/pallas_call | solution.py:266
  381.1 21.0 %collective-permute-done.31.refs_6_.refs_10_ = bf16[64,32,128]{2,1,0:T(8,128)(2,1)S(1)} collective-permute-done((bf16[64,32,128]{2,1,0:T(8,128)(2,1)}, bf16[64,32,128]{2,1,0:T(8,128)(2,1)S(1)}, u32[]{:S(2)}, u32[]{:S(2)}) %collective-permute-start.31) | collective-permute-done | bytes 524320 | tf_op jit(solution)/shard_map/ppermute | solution.py:292
  402.2 13.0 %collective-permute-done.32.refs_7_.refs_11_ = bf16[64,32,128]{2,1,0:T(8,128)(2,1)S(1)} collective-permute-done((bf16[64,32,128]{2,1,0:T(8,128)(2,1)}, bf16[64,32,128]{2,1,0:T(8,128)(2,1)S(1)}, u32[]{:S(2)}, u32[]{:S(2)}) %collective-permute-start.32) | collective-permute-done | bytes 524320 | tf_op jit(solution)/shard_map/ppermute | solution.py:292
  415.9 14.3 %shard_map.93 = (bf16[32,64,512]{2,1,0:T(8,128)(2,1)}, bf16[32,64,512]{2,1,0:T(8,128)(2,1)}, bf16[32,64,512]{2,1,0:T(8,128)(2,1)}, bf16[32,64,512]{2,1,0:T(8,128...) custom-call(s32[4]{0:T(128)} %pad_add_fusion.place_ref, ...), custom_call_target="tpu_custom_call" | custom-call | flops 2147483648 | bytes 25165824 | tf_op jit(solution)/shard_map/pallas_call | solution.py:377
  465.0 11.2 %collective-permute-done.40.refs_2_ = bf16[64,32,128]{2,1,0:T(8,128)(2,1)S(1)} collective-permute-done((bf16[64,32,128]{2,1,0:T(8,128)(2,1)}, bf16[64,32,128]{2,1,0:T(8,128)(2,1)S(1)}, u32[]{:S(2)}, u32[]{:S(2)}) %collective-permute-start.40) | collective-permute-done | bytes 524320 | tf_op jit(solution)/shard_map/ppermute | solution.py:292
  476.8 22.7 %collective-permute-done.35.refs_2_ = bf16[32,64,512]{2,1,0:T(8,128)(2,1)} collective-permute-done((bf16[32,64,512]{2,1,0:T(8,128)(2,1)S(1)}, bf16[32,64,512]{2,1,0:T(8,128)(2,1)}, u32[]{:S(2)}, u32[]{:S(2)}) %collective-permute-start.35) | collective-permute-done | bytes 2097184 | tf_op jit(solution)/shard_map/ppermute | solution.py:328
  507.6 36.7 %collective-permute-done.44.refs_2_ = bf16[32,64,512]{2,1,0:T(8,128)(2,1)S(1)} collective-permute-done((bf16[32,64,512]{2,1,0:T(8,128)(2,1)}, bf16[32,64,512]{2,1,0:T(8,128)(2,1)S(1)}, u32[]{:S(2)}, u32[]{:S(2)}) %collective-permute-start.44) | collective-permute-done | bytes 2097184 | tf_op jit(solution)/shard_map/ppermute | solution.py:328
  558.2 14.9 %shard_map.95.held_ref = bf16[128,128,128]{2,1,0:T(8,128)(2,1)} custom-call(bf16[128,128,128]{2,1,0:T(8,128)(2,1)} %pair_ref.15, bf16[64,128,128]{2,1,0:T(8,128)(2,1)} %get-tuple-element.118.sigm_ref, f32[16,1,1024]{2,1,0:T(1,128)} %broadcast_multiply_fusion.mask_ref, f32[1,128]{1,0:T(1,128)} %bitcast.39, ...), custom_call_target="tpu_custom_call", output_to_operand_aliasing={{}: (5, {})} | custom-call | flops 2415919104 | bytes 10485760 | tf_op jit(solution)/shard_map/pallas_call | solution.py:278
  573.4 30.4 %collective-permute-done.46.refs_6_ = bf16[64,32,128]{2,1,0:T(8,128)(2,1)S(1)} collective-permute-done((bf16[64,32,128]{2,1,0:T(8,128)(2,1)}, bf16[64,32,128]{2,1,0:T(8,128)(2,1)S(1)}, u32[]{:S(2)}, u32[]{:S(2)}) %collective-permute-start.46) | collective-permute-done | bytes 524320 | tf_op jit(solution)/shard_map/ppermute | solution.py:292
  603.8 12.6 %collective-permute-done.47.refs_7_ = bf16[64,32,128]{2,1,0:T(8,128)(2,1)S(1)} collective-permute-done((bf16[64,32,128]{2,1,0:T(8,128)(2,1)}, bf16[64,32,128]{2,1,0:T(8,128)(2,1)S(1)}, u32[]{:S(2)}, u32[]{:S(2)}) %collective-permute-start.47) | collective-permute-done | bytes 524320 | tf_op jit(solution)/shard_map/ppermute | solution.py:292
  617.3 14.9 %shard_map.98 = bf16[128,128,128]{2,1,0:T(8,128)(2,1)} custom-call(bf16[128,128,128]{2,1,0:T(8,128)(2,1)} %pair_ref.15, bf16[64,128,128]{2,1,0:T(8,128)(2,1)} %get-tuple-element.113.sigm_ref, f32[16,1,1024]{2,1,0:T(1,128)} %broadcast_multiply_fusion.mask_ref, f32[1,128]{1,0:T(1,128)} %bitcast.40, ...), custom_call_target="tpu_custom_call", output_to_operand_aliasing={{}: (5, {})} | custom-call | flops 2415919104 | bytes 10485760 | tf_op jit(solution)/shard_map/pallas_call | solution.py:278
  (220 shorter events, 185.3 us)
Async XLA Ops:
  14.4 45.2 %collective-permute-start.2 = (bf16[64,32,128]{2,1,0:T(8,128)(2,1)}, bf16[64,32,128]{2,1,0:T(8,128)(2,1)S(1)}, u32[]{:S(2)}, u32[]{:S(2)}) collective-permute-start(bf16[64,32,128]{2,1,0:T(8,128)(2,1)} %get-tuple-element.84), channel_id=1, source_target_pairs={{0,12},{4,8},{8,4},{12,0},{1,13},{5,9},{9,5},{13,1},{2,14},{6,10},... | collective-permute-start | bytes 1572872 | tf_op jit(solution)/shard_map/ppermute | solution.py:292
  69.7 47.8 %collective-permute-start.7 = (bf16[32,64,512]{2,1,0:T(8,128)(2,1)}, bf16[32,64,512]{2,1,0:T(8,128)(2,1)}, u32[]{:S(2)}, u32[]{:S(2)}) collective-permute-start(bf16[32,64,512]{2,1,0:T(8,128)(2,1)} %shard_map.85.refs_0_), channel_id=1, source_target_pairs={{0,2},{2,0},{1,3},{3,1},{4,6},{6,4},{5,7},{7,5},{8,10},{10,8},{9,1... | collective-permute-start | bytes 6291464 | tf_op jit(solution)/shard_map/ppermute | solution.py:328
  137.0 70.3 %collective-permute-start.10 = (bf16[32,64,512]{2,1,0:T(8,128)(2,1)}, bf16[32,64,512]{2,1,0:T(8,128)(2,1)}, u32[]{:S(2)}, u32[]{:S(2)}) collective-permute-start(bf16[32,64,512]{2,1,0:T(8,128)(2,1)} %shard_map.87.refs_1_), channel_id=1, source_target_pairs={{0,2},{2,0},{1,3},{3,1},{4,6},{6,4},{5,7},{7,5},{8,10},{10,8},{9,1... | collective-permute-start | bytes 6291464 | tf_op jit(solution)/shard_map/ppermute | solution.py:328
  138.3 45.5 %collective-permute-start.13 = (bf16[64,32,128]{2,1,0:T(8,128)(2,1)S(1)}, bf16[64,32,128]{2,1,0:T(8,128)(2,1)S(1)}, u32[]{:S(2)}, u32[]{:S(2)}) collective-permute-start(bf16[64,32,128]{2,1,0:T(8,128)(2,1)S(1)} %copy-done.49), channel_id=1, source_target_pairs={{0,8},{4,12},{8,0},{12,4},{1,9},{5,13},{9,1},{13,5},{2,10},{6,14},... | collective-permute-start | bytes 1572872 | tf_op jit(solution)/shard_map/ppermute | solution.py:292
  139.5 55.6 %collective-permute-start.11 = (bf16[64,32,128]{2,1,0:T(8,128)(2,1)S(1)}, bf16[64,32,128]{2,1,0:T(8,128)(2,1)}, u32[]{:S(2)}, u32[]{:S(2)}) collective-permute-start(bf16[64,32,128]{2,1,0:T(8,128)(2,1)S(1)} %copy-done.45), channel_id=1, source_target_pairs={{0,8},{4,12},{8,0},{12,4},{1,9},{5,13},{9,1},{13,5},{2,10},{6,14},... | collective-permute-start | bytes 1572872 | tf_op jit(solution)/shard_map/ppermute | solution.py:292
  140.7 66.7 %collective-permute-start.12 = (bf16[64,32,128]{2,1,0:T(8,128)(2,1)S(1)}, bf16[64,32,128]{2,1,0:T(8,128)(2,1)}, u32[]{:S(2)}, u32[]{:S(2)}) collective-permute-start(bf16[64,32,128]{2,1,0:T(8,128)(2,1)S(1)} %copy-done.44), channel_id=1, source_target_pairs={{0,12},{4,8},{8,4},{12,0},{1,13},{5,9},{9,5},{13,1},{2,14},{6,10},... | collective-permute-start | bytes 1572872 | tf_op jit(solution)/shard_map/ppermute | solution.py:292
  142.0 70.9 %collective-permute-start.14 = (bf16[32,64,512]{2,1,0:T(8,128)(2,1)}, bf16[32,64,512]{2,1,0:T(8,128)(2,1)}, u32[]{:S(2)}, u32[]{:S(2)}) collective-permute-start(bf16[32,64,512]{2,1,0:T(8,128)(2,1)} %collective-permute-done.7.refs_4_), channel_id=1, source_target_pairs={{0,1},{1,0},{2,3},{3,2},{4,5},{5,4},{6,7},{7,6},{8,9},{9,8},{10,11... | collective-permute-start | bytes 6291464 | tf_op jit(solution)/shard_map/ppermute | solution.py:328
  227.9 52.4 %collective-permute-start.23 = (bf16[64,32,128]{2,1,0:T(8,128)(2,1)}, bf16[64,32,128]{2,1,0:T(8,128)(2,1)S(1)}, u32[]{:S(2)}, u32[]{:S(2)}) collective-permute-start(bf16[64,32,128]{2,1,0:T(8,128)(2,1)} %get-tuple-element.117), channel_id=1, source_target_pairs={{0,12},{4,8},{8,4},{12,0},{1,13},{5,9},{9,5},{13,1},{2,14},{6,10},... | collective-permute-start | bytes 1572872 | tf_op jit(solution)/shard_map/ppermute | solution.py:292
  241.3 52.5 %collective-permute-start.18 = (bf16[64,32,128]{2,1,0:T(8,128)(2,1)}, bf16[64,32,128]{2,1,0:T(8,128)(2,1)S(1)}, u32[]{:S(2)}, u32[]{:S(2)}) collective-permute-start(bf16[64,32,128]{2,1,0:T(8,128)(2,1)} %get-tuple-element.110), channel_id=1, source_target_pairs={{0,4},{4,0},{8,12},{12,8},{1,5},{5,1},{9,13},{13,9},{2,6},{6,2},{1... | collective-permute-start | bytes 1572872 | tf_op jit(solution)/shard_map/ppermute | solution.py:292
  250.9 61.2 %collective-permute-start.19 = (bf16[64,32,128]{2,1,0:T(8,128)(2,1)}, bf16[64,32,128]{2,1,0:T(8,128)(2,1)S(1)}, u32[]{:S(2)}, u32[]{:S(2)}) collective-permute-start(bf16[64,32,128]{2,1,0:T(8,128)(2,1)} %get-tuple-element.111), channel_id=1, source_target_pairs={{0,8},{4,12},{8,0},{12,4},{1,9},{5,13},{9,1},{13,5},{2,10},{6,14},... | collective-permute-start | bytes 1572872 | tf_op jit(solution)/shard_map/ppermute | solution.py:292
  256.7 90.9 %collective-permute-start.20 = (bf16[64,32,128]{2,1,0:T(8,128)(2,1)}, bf16[64,32,128]{2,1,0:T(8,128)(2,1)S(1)}, u32[]{:S(2)}, u32[]{:S(2)}) collective-permute-start(bf16[64,32,128]{2,1,0:T(8,128)(2,1)} %get-tuple-element.112), channel_id=1, source_target_pairs={{0,12},{4,8},{8,4},{12,0},{1,13},{5,9},{9,5},{13,1},{2,14},{6,10},... | collective-permute-start | bytes 1572872 | tf_op jit(solution)/shard_map/ppermute | solution.py:292
  292.0 69.0 %collective-permute-start.24 = (bf16[64,32,128]{2,1,0:T(8,128)(2,1)}, bf16[64,32,128]{2,1,0:T(8,128)(2,1)S(1)}, u32[]{:S(2)}, u32[]{:S(2)}) collective-permute-start(bf16[64,32,128]{2,1,0:T(8,128)(2,1)} %get-tuple-element.120), channel_id=1, source_target_pairs={{0,4},{4,0},{8,12},{12,8},{1,5},{5,1},{9,13},{13,9},{2,6},{6,2},{1... | collective-permute-start | bytes 1572872 | tf_op jit(solution)/shard_map/ppermute | solution.py:292
  292.1 70.0 %collective-permute-start.25 = (bf16[64,32,128]{2,1,0:T(8,128)(2,1)}, bf16[64,32,128]{2,1,0:T(8,128)(2,1)S(1)}, u32[]{:S(2)}, u32[]{:S(2)}) collective-permute-start(bf16[64,32,128]{2,1,0:T(8,128)(2,1)} %get-tuple-element.121), channel_id=1, source_target_pairs={{0,8},{4,12},{8,0},{12,4},{1,9},{5,13},{9,1},{13,5},{2,10},{6,14},... | collective-permute-start | bytes 1572872 | tf_op jit(solution)/shard_map/ppermute | solution.py:292
  293.8 76.3 %collective-permute-start.26 = (bf16[64,32,128]{2,1,0:T(8,128)(2,1)}, bf16[64,32,128]{2,1,0:T(8,128)(2,1)S(1)}, u32[]{:S(2)}, u32[]{:S(2)}) collective-permute-start(bf16[64,32,128]{2,1,0:T(8,128)(2,1)} %get-tuple-element.122), channel_id=1, source_target_pairs={{0,12},{4,8},{8,4},{12,0},{1,13},{5,9},{9,5},{13,1},{2,14},{6,10},... | collective-permute-start | bytes 1572872 | tf_op jit(solution)/shard_map/ppermute | solution.py:292
  361.0 54.1 %collective-permute-start.32 = (bf16[64,32,128]{2,1,0:T(8,128)(2,1)}, bf16[64,32,128]{2,1,0:T(8,128)(2,1)S(1)}, u32[]{:S(2)}, u32[]{:S(2)}) collective-permute-start(bf16[64,32,128]{2,1,0:T(8,128)(2,1)} %get-tuple-element.130), channel_id=1, source_target_pairs={{0,12},{4,8},{8,4},{12,0},{1,13},{5,9},{9,5},{13,1},{2,14},{6,10},... | collective-permute-start | bytes 1572872 | tf_op jit(solution)/shard_map/ppermute | solution.py:292
  453.7 45.7 %collective-permute-start.35 = (bf16[32,64,512]{2,1,0:T(8,128)(2,1)S(1)}, bf16[32,64,512]{2,1,0:T(8,128)(2,1)}, u32[]{:S(2)}, u32[]{:S(2)}) collective-permute-start(bf16[32,64,512]{2,1,0:T(8,128)(2,1)S(1)} %add_convert_fusion.1), channel_id=1, source_target_pairs={{0,2},{2,0},{1,3},{3,1},{4,6},{6,4},{5,7},{7,5},{8,10},{10,8},{9,1... | collective-permute-start | bytes 6291464 | tf_op jit(solution)/shard_map/ppermute | solution.py:328
  454.0 53.1 %collective-permute-start.42 = (bf16[32,64,512]{2,1,0:T(8,128)(2,1)}, bf16[32,64,512]{2,1,0:T(8,128)(2,1)S(1)}, u32[]{:S(2)}, u32[]{:S(2)}) collective-permute-start(bf16[32,64,512]{2,1,0:T(8,128)(2,1)} %get-tuple-element.149), channel_id=1, source_target_pairs={{0,1},{1,0},{2,3},{3,2},{4,5},{5,4},{6,7},{7,6},{8,9},{9,8},{10,11... | collective-permute-start | bytes 6291464 | tf_op jit(solution)/shard_map/ppermute | solution.py:328
  476.2 68.1 %collective-permute-start.44 = (bf16[32,64,512]{2,1,0:T(8,128)(2,1)}, bf16[32,64,512]{2,1,0:T(8,128)(2,1)S(1)}, u32[]{:S(2)}, u32[]{:S(2)}) collective-permute-start(bf16[32,64,512]{2,1,0:T(8,128)(2,1)} %add_convert_fusion), channel_id=1, source_target_pairs={{0,2},{2,0},{1,3},{3,1},{4,6},{6,4},{5,7},{7,5},{8,10},{10,8},{9,1... | collective-permute-start | bytes 6291464 | tf_op jit(solution)/shard_map/ppermute | solution.py:328
  476.5 73.9 %collective-permute-start.29 = (bf16[64,32,128]{2,1,0:T(8,128)(2,1)}, bf16[64,32,128]{2,1,0:T(8,128)(2,1)S(1)}, u32[]{:S(2)}, u32[]{:S(2)}) collective-permute-start(bf16[64,32,128]{2,1,0:T(8,128)(2,1)} %get-tuple-element.126), channel_id=1, source_target_pairs={{0,12},{4,8},{8,4},{12,0},{1,13},{5,9},{9,5},{13,1},{2,14},{6,10},... | collective-permute-start | bytes 1572872 | tf_op jit(solution)/shard_map/ppermute | solution.py:292
  504.1 49.1 %collective-permute-start.36 = (bf16[64,32,128]{2,1,0:T(8,128)(2,1)}, bf16[64,32,128]{2,1,0:T(8,128)(2,1)S(1)}, u32[]{:S(2)}, u32[]{:S(2)}) collective-permute-start(bf16[64,32,128]{2,1,0:T(8,128)(2,1)} %get-tuple-element.141), channel_id=1, source_target_pairs={{0,4},{4,0},{8,12},{12,8},{1,5},{5,1},{9,13},{13,9},{2,6},{6,2},{1... | collective-permute-start | bytes 1572872 | tf_op jit(solution)/shard_map/ppermute | solution.py:292
  506.3 47.2 %collective-permute-start.37 = (bf16[64,32,128]{2,1,0:T(8,128)(2,1)}, bf16[64,32,128]{2,1,0:T(8,128)(2,1)S(1)}, u32[]{:S(2)}, u32[]{:S(2)}) collective-permute-start(bf16[64,32,128]{2,1,0:T(8,128)(2,1)} %get-tuple-element.142), channel_id=1, source_target_pairs={{0,8},{4,12},{8,0},{12,4},{1,9},{5,13},{9,1},{13,5},{2,10},{6,14},... | collective-permute-start | bytes 1572872 | tf_op jit(solution)/shard_map/ppermute | solution.py:292
  507.1 48.1 %collective-permute-start.38 = (bf16[64,32,128]{2,1,0:T(8,128)(2,1)}, bf16[64,32,128]{2,1,0:T(8,128)(2,1)}, u32[]{:S(2)}, u32[]{:S(2)}) collective-permute-start(bf16[64,32,128]{2,1,0:T(8,128)(2,1)} %get-tuple-element.143), channel_id=1, source_target_pairs={{0,12},{4,8},{8,4},{12,0},{1,13},{5,9},{9,5},{13,1},{2,14},{6,10},... | collective-permute-start | bytes 1572872 | tf_op jit(solution)/shard_map/ppermute | solution.py:292
  553.2 50.6 %collective-permute-start.46 = (bf16[64,32,128]{2,1,0:T(8,128)(2,1)}, bf16[64,32,128]{2,1,0:T(8,128)(2,1)S(1)}, u32[]{:S(2)}, u32[]{:S(2)}) collective-permute-start(bf16[64,32,128]{2,1,0:T(8,128)(2,1)} %get-tuple-element.155), channel_id=1, source_target_pairs={{0,8},{4,12},{8,0},{12,4},{1,9},{5,13},{9,1},{13,5},{2,10},{6,14},... | collective-permute-start | bytes 1572872 | tf_op jit(solution)/shard_map/ppermute | solution.py:292
  553.5 63.0 %collective-permute-start.47 = (bf16[64,32,128]{2,1,0:T(8,128)(2,1)}, bf16[64,32,128]{2,1,0:T(8,128)(2,1)S(1)}, u32[]{:S(2)}, u32[]{:S(2)}) collective-permute-start(bf16[64,32,128]{2,1,0:T(8,128)(2,1)} %get-tuple-element.156), channel_id=1, source_target_pairs={{0,12},{4,8},{8,4},{12,0},{1,13},{5,9},{9,5},{13,1},{2,14},{6,10},... | collective-permute-start | bytes 1572872 | tf_op jit(solution)/shard_map/ppermute | solution.py:292
  (75 other events, 1785.1 us)
